TPU v7x, 32 devices: a whole 2x2x4 slice. The times are simulated.
32 devices in a mesh: section: 4 (over x, core), tp: 8 (over z, y).
Axes of the slice: x: 2, y: 2, z: 4, core: 2. Of those that a mesh axis runs over, the one named last changes fastest.
Arguments:
- gate_codes: bfloat16 [4, 96, 1280], P('section', None, 'tp'), may hold values from -128 to 127, as said below
- gate_exponents: int32 [4, 96, 40], P('section', None, 'tp'), may hold values from -8 to -6
- up_codes: bfloat16 [4, 96, 1280], P('section', None, 'tp'), may hold values from -128 to 127, as said below
- up_exponents: int32 [4, 96, 40], P('section', None, 'tp'), may hold values from -8 to -6
- down_codes: bfloat16 [4, 1280, 4096], P('section', 'tp'), may hold values from -128 to 127, as said below
- down_exponents: int32 [4, 40, 4096], P('section', 'tp'), may hold values from -14 to -12
- grad_held: bfloat16 [4, 96, 4096], P('section', 'tp'), may hold values from -6 to 6
Outputs:
- down_grad: bfloat16 [4, 1280, 4096], P('section', 'tp')
- gate_grad: bfloat16 [4, 96, 1280], P('section', None, 'tp')
- up_grad: bfloat16 [4, 96, 1280], P('section', None, 'tp')
Inputs may be any that keep to these rules, and one draw needn't show every extreme that they name: `gate_codes`: every entry is a whole number, independent of the others. `up_codes`: every entry is a whole number, independent of the others. `down_codes`: every entry is a whole number, independent of the others.
All inputs are finite; a program needn't handle non-finite values.
Results may differ from a plain program's by a relative error of at most 0.005.
Values may be sent and summed in bfloat16 or wider, within the bound.
No kernel may reach another device: no remote copies, remote signals or barrier semaphores. Data moves between devices by JAX's collectives and lax.ppermute only.
A program may use at most 64 MiB of HBM per device.

v0:
```python
import functools

import jax
import jax.numpy as jnp
from jax import lax
from jax.experimental import pallas as pl
from jax.experimental.pallas import tpu as pltpu
from jax.sharding import PartitionSpec as P

TILE = 16
WHOLE = pl.BlockSpec(memory_space=pltpu.VMEM)
LEFT = pl.BlockSpec(memory_space=pltpu.HBM)
COST = pl.CostEstimate(flops=0, bytes_accessed=16 * 1024 * 1024, transcendentals=0)
PARAMS = pltpu.CompilerParams(vmem_limit_bytes=24 * 1024 * 1024)


def send(array, flip, hop):
    sections, count = lax.axis_size("section"), lax.axis_size("tp")
    if hop == 0:
        return lax.ppermute(array, "tp", [(t, t ^ flip) for t in range(count)])
    pairs = [
        (s * count + t, ((s - hop) % sections) * count + (t ^ flip))
        for s in range(sections)
        for t in range(count)
    ]
    return lax.ppermute(array, ("section", "tp"), pairs)


def fetched(refs, held_refs, sems):
    copies = [pltpu.make_async_copy(ref, held, sems.at[i]) for i, (ref, held) in enumerate(zip(refs, held_refs))]
    for copy in copies:
        copy.start()
    return copies


def pack_kernel(held_ref, packed_ref, rows_ref, sems):
    for copy in fetched([held_ref], [rows_ref], sems):
        copy.wait()
    count, width = rows_ref.shape
    free = TILE - count
    keep = width * count // TILE
    rows = rows_ref[...]
    parts = [rows[at : at + free, keep:] for at in range(0, count, free)]
    packed_ref[...] = jnp.concatenate([rows[:, :keep], jnp.concatenate(parts, axis=1)], axis=0)


def pack(rows):
    count, width = rows.shape
    return pl.pallas_call(
        pack_kernel,
        out_shape=pltpu.VMEM((TILE, width * count // TILE), jnp.bfloat16),
        in_specs=[LEFT],
        out_specs=WHOLE,
        scratch_shapes=[pltpu.VMEM(rows.shape, rows.dtype), pltpu.SemaphoreType.DMA((1,))],
        compiler_params=PARAMS,
    )(pltpu.with_memory_space_constraint(rows, pltpu.HBM))


def spread(tokens, slots, count):
    shape = (tokens, len(slots) * TILE)
    lane = lax.broadcasted_iota(jnp.int32, shape, 1)
    row = lane & (TILE - 1)
    place = lane >> (TILE.bit_length() - 1)
    slot = jnp.full(shape, slots[0], jnp.int32)
    for i in range(1, len(slots)):
        slot = jnp.where(place == i, slots[i], slot)
    token = (slot ^ lax.axis_index("tp")) * count + row
    hit = (lax.broadcasted_iota(jnp.int32, shape, 0) == token) & (row < count)
    return jnp.where(hit, 1.0, 0.0).astype(jnp.bfloat16)


def decoded(codes_ref, exponents_ref):
    blocks = exponents_ref.shape[0]
    per = codes_ref.shape[0] // blocks
    parts = []
    for b in range(blocks):
        scale = jnp.exp2(exponents_ref[b].astype(jnp.float32))
        codes = codes_ref[pl.ds(b * per, per), :].astype(jnp.float32)
        parts.append((codes * scale).astype(jnp.bfloat16))
    return jnp.concatenate(parts, axis=0)


def prepare_kernel(groups, count, *refs):
    gate_ref, gate_exp_ref, up_ref, up_exp_ref, down_ref, down_exp_ref = held = refs[-7:-1]
    copies = fetched(refs[:6], held, refs[-1])
    weight_ref, hidden_ref = refs[6:8]
    factor_refs = refs[8:-7]
    for copy in copies[:4]:
        copy.wait()
    where = spread(gate_ref.shape[1], sum(groups, []), count)
    gate = jnp.dot(decoded(gate_ref, gate_exp_ref), where, preferred_element_type=jnp.float32)
    up = jnp.dot(decoded(up_ref, up_exp_ref), where, preferred_element_type=jnp.float32)
    sigmoid = jax.nn.sigmoid(gate)
    silu = gate * sigmoid
    hidden_ref[...] = (silu * up).astype(jnp.bfloat16)
    gate_factor = up * sigmoid * (1.0 + gate * (1.0 - sigmoid))
    at = 0
    for i, group in enumerate(groups):
        lanes = slice(at, at + len(group) * TILE)
        at = lanes.stop
        factor_refs[2 * i][...] = gate_factor[:, lanes]
        factor_refs[2 * i + 1][...] = silu[:, lanes]
    for copy in copies[4:]:
        copy.wait()
    blocks = down_exp_ref.shape[0]
    per = down_ref.shape[0] // blocks
    for b in range(blocks):
        scale = jnp.exp2(down_exp_ref[b].astype(jnp.float32))
        codes = down_ref[pl.ds(b * per, per), :].astype(jnp.float32)
        weight_ref[pl.ds(b * per, per), :] = (codes * scale).astype(jnp.bfloat16)


def prepare(groups, count, *operands):
    units, width = operands[4].shape
    lanes = sum(map(len, groups)) * TILE
    factors = [pltpu.VMEM((units, len(group) * TILE), jnp.float32) for group in groups for _ in range(2)]
    weight, hidden, *factors = pl.pallas_call(
        functools.partial(prepare_kernel, groups, count),
        out_shape=(
            pltpu.VMEM((units, width), jnp.bfloat16),
            pltpu.VMEM((units, lanes), jnp.bfloat16),
            *factors,
        ),
        in_specs=[LEFT] * 6,
        out_specs=[WHOLE] * (2 + len(factors)),
        scratch_shapes=[pltpu.VMEM(operand.shape, operand.dtype) for operand in operands]
        + [pltpu.SemaphoreType.DMA((len(operands),))],
        compiler_params=PARAMS,
        cost_estimate=COST,
    )(*[pltpu.with_memory_space_constraint(operand, pltpu.HBM) for operand in operands])
    return weight, hidden, [factors[2 * i : 2 * i + 2] for i in range(len(groups))]


def restore(slot_refs, incoming_ref, count):
    free = TILE - count
    width = incoming_ref.shape[1]
    for i, slot_ref in enumerate(slot_refs):
        keep = slot_ref.shape[1]
        slot = slot_ref[...]
        low = slot[count:, :]
        parts = [low[:, at : at + width - keep] for at in range(0, keep, width - keep)]
        parts.append(jnp.zeros((free, width - keep), slot.dtype))
        incoming_ref[i * TILE : (i + 1) * TILE, :keep] = slot
        incoming_ref[i * TILE : (i + 1) * TILE, keep:] = jnp.concatenate(parts, axis=0)


def grads(group, count, slope, factor_refs, before_refs, grad_refs):
    where = spread(grad_refs[0].shape[1], group, count)
    for factor_ref, before_ref, grad_ref in zip(factor_refs, before_refs, grad_refs):
        grad = (slope * factor_ref[...]).astype(jnp.bfloat16)
        placed = lax.dot_general(grad, where, (((1,), (1,)), ((), ())), preferred_element_type=jnp.float32)
        if before_ref is not None:
            placed += before_ref[...].astype(jnp.float32)
        grad_ref[...] = placed.astype(jnp.bfloat16)


def stage_kernel(group, count, first, *refs):
    slot_refs, refs = refs[: len(group)], refs[len(group) :]
    weight_ref, factor_refs, refs = refs[0], refs[1:3], refs[3:]
    before_refs, refs = ((None, None), refs) if first else (refs[:2], refs[2:])
    incoming_ref, *grad_refs = refs
    restore(slot_refs, incoming_ref, count)
    slope = lax.dot_general(
        weight_ref[...], incoming_ref[...], (((1,), (1,)), ((), ())), preferred_element_type=jnp.float32
    )
    grads(group, count, slope, factor_refs, before_refs, grad_refs)


def stage(group, count, tokens, slots, weight, factors, before):
    units, width = weight.shape
    operands = (*slots, weight, *factors, *before)
    return pl.pallas_call(
        functools.partial(stage_kernel, group, count, len(before) == 0),
        out_shape=(
            pltpu.VMEM((len(group) * TILE, width), jnp.bfloat16),
            pltpu.VMEM((units, tokens), jnp.bfloat16),
            pltpu.VMEM((units, tokens), jnp.bfloat16),
        ),
        in_specs=[WHOLE] * len(operands),
        out_specs=[WHOLE] * 3,
        compiler_params=PARAMS,
        cost_estimate=COST,
    )(*operands)


def last_kernel(group, count, chunk, *refs):
    slot_refs, earlier_ref = refs[: len(group)], refs[len(group)]
    weight_ref, hidden_ref = refs[-12:-10]
    factor_refs, before_refs = refs[-10:-8], refs[-8:-6]
    down_ref, *grad_refs, newest_ref, tile_ref, sems = refs[-6:]
    width = weight_ref.shape[1]
    restore(slot_refs, newest_ref, count)
    hidden = hidden_ref[...]
    copies = []
    for at in range(0, width, chunk):
        incoming = jnp.concatenate([earlier_ref[:, at : at + chunk], newest_ref[:, at : at + chunk]], axis=0)
        down = jnp.dot(hidden, incoming, preferred_element_type=jnp.float32)
        tile_ref[:, at : at + chunk] = down.astype(jnp.bfloat16)
        copy = pltpu.make_async_copy(
            tile_ref.at[:, pl.ds(at, chunk)], down_ref.at[:, pl.ds(at, chunk)], sems.at[at // chunk]
        )
        copy.start()
        copies.append(copy)
    slope = lax.dot_general(
        weight_ref[...], newest_ref[...], (((1,), (1,)), ((), ())), preferred_element_type=jnp.float32
    )
    grads(group, count, slope, factor_refs, before_refs, grad_refs)
    for copy in copies:
        copy.wait()


def last(group, count, slots, earlier, weight, hidden, factors, before):
    units, width = weight.shape
    tokens = before[0].shape[1]
    chunk = width // 8
    operands = (*slots, earlier, weight, hidden, *factors, *before)
    return pl.pallas_call(
        functools.partial(last_kernel, group, count, chunk),
        out_shape=(
            jax.ShapeDtypeStruct((units, width), jnp.bfloat16),
            jax.ShapeDtypeStruct((units, tokens), jnp.bfloat16),
            jax.ShapeDtypeStruct((units, tokens), jnp.bfloat16),
        ),
        in_specs=[WHOLE] * len(operands),
        out_specs=[LEFT, WHOLE, WHOLE],
        scratch_shapes=[
            pltpu.VMEM((len(group) * TILE, width), jnp.bfloat16),
            pltpu.VMEM((units, width), jnp.bfloat16),
            pltpu.SemaphoreType.DMA((width // chunk,)),
        ],
        compiler_params=PARAMS,
        cost_estimate=COST,
    )(*operands)


def fanned(gate_codes, gate_exponents, up_codes, up_exponents, down_codes, down_exponents, grad_held):
    n = lax.axis_size("tp")
    count = grad_held.shape[1]
    p = pack(grad_held[0])
    groups = [[f for f in range(n) if f & (f - 1) == 0], [f for f in reversed(range(n)) if f & (f - 1)]]
    got = {}
    for flip in reversed(groups[0]):
        got[flip] = send(p, flip, 1)
    weight, hidden, factors = prepare(
        groups,
        count,
        gate_codes[0].T,
        gate_exponents.transpose(2, 0, 1),
        up_codes[0].T,
        up_exponents.transpose(2, 0, 1),
        down_codes[0],
        down_exponents.transpose(1, 0, 2),
    )
    for flip, tied in zip(groups[0][1:], lax.optimization_barrier((*[got[f] for f in groups[0][1:]], hidden))):
        got[flip] = tied
    for flip in sorted(groups[1], key=lambda f: -(f & 1) * f):
        step = flip & -flip
        if flip & 1 and flip - 1 not in groups[0]:
            step = flip - 1
        got[flip] = send(got[flip - step], step, 0)
    early = [got[j] for j in groups[0]]
    earlier, *before = stage(groups[0], count, n * count, early, weight, factors[0], [])
    late = [got[j] for j in groups[1]]
    down_grad, gate_grad, up_grad = last(groups[1], count, late, earlier, weight, hidden, factors[1], before)
    return down_grad[None], gate_grad.T[None], up_grad.T[None]


def dequantize(codes, exponents, target_axis):
    per = codes.shape[target_axis] // exponents.shape[target_axis]
    scales = jnp.exp2(jnp.repeat(exponents, per, axis=target_axis).astype(jnp.float32))
    return (codes.astype(jnp.float32) * scales).astype(jnp.bfloat16)


def ringed(gate_codes, gate_exponents, up_codes, up_exponents, down_codes, down_exponents, grad_held):
    gate = dequantize(gate_codes[0], gate_exponents[0], 1).astype(jnp.float32)
    up = dequantize(up_codes[0], up_exponents[0], 1).astype(jnp.float32)
    weight = dequantize(down_codes[0], down_exponents[0], 0)
    count = lax.axis_size("section")
    received = lax.ppermute(grad_held[0], "section", [(i, (i - 1) % count) for i in range(count)])
    incoming = lax.all_gather(received, "tp", axis=0, tiled=True)
    sigmoid = jax.nn.sigmoid(gate)
    silu = gate * sigmoid
    hidden = (silu * up).astype(jnp.bfloat16)
    down_grad = lax.dot_general(hidden, incoming, (((0,), (0,)), ((), ())), preferred_element_type=jnp.float32)
    slope = lax.dot_general(incoming, weight, (((1,), (1,)), ((), ())), preferred_element_type=jnp.float32)
    gate_grad = (slope * up * sigmoid * (1.0 + gate * (1.0 - sigmoid))).astype(jnp.bfloat16)
    up_grad = (slope * silu).astype(jnp.bfloat16)
    return down_grad.astype(jnp.bfloat16)[None], gate_grad[None], up_grad[None]


def body(*operands):
    n = lax.axis_size("tp")
    count, width = operands[-1].shape[1:]
    free = TILE - count
    small = n & (n - 1) == 0 and 4 <= n <= TILE
    fits = 0 < free < TILE and count % free == 0 and width * free % (TILE * 8 * 128) == 0
    return fanned(*operands) if small and fits else ringed(*operands)


def solution(mesh):
    wide, tall = P("section", None, "tp"), P("section", "tp", None)
    return jax.shard_map(
        body,
        mesh=mesh,
        in_specs=(wide, wide, wide, wide, tall, tall, tall),
        out_specs=(tall, wide, wide),
        check_vma=False,
    )
```

profile of v0, /device:TPU:0, one launch (start us, length us, event | category | flops | bytes accessed | tf_op | source)
XLA Modules:
  0.0 24.2 jit_solution(10234597708759007921)
XLA Ops:
  0.6 0.9 %shard_map.94 = bf16[16,3072]{1,0:T(8,128)(2,1)S(1)} custom-call(bf16[12,4096]{1,0:T(8,128)(2,1)} %bitcast.19), custom_call_target="tpu_custom_call" | custom-call | tf_op jit(solution)/shard_map/pallas_call | solution.py:49
  1.6 4.5 %collective-permute-start.2 = (bf16[16,3072]{1,0:T(8,128)(2,1)S(1)}, bf16[16,3072]{1,0:T(8,128)(2,1)S(1)}, u32[]{:S(2)}, u32[]{:S(2)}) collective-permute-start(bf16[16,3072]{1,0:T(8,128)(2,1)S(1)} %shard_map.94), channel_id=1, source_target_pairs={{0,28},{1,29},{2,30},{3,31},{4,24},{5,25},{6,26},{7,27},{8,4},{9,5... | collective-permute-start | bytes 294920 | tf_op jit(solution)/shard_map/ppermute | solution.py:26
  6.0 1.9 %collective-permute-start.1 = (bf16[16,3072]{1,0:T(8,128)(2,1)S(1)}, bf16[16,3072]{1,0:T(8,128)(2,1)S(1)}, u32[]{:S(2)}, u32[]{:S(2)}) collective-permute-start(bf16[16,3072]{1,0:T(8,128)(2,1)S(1)} %shard_map.94), channel_id=1, source_target_pairs={{0,26},{1,27},{2,24},{3,25},{4,30},{5,31},{6,28},{7,29},{8,2},{9,3... | collective-permute-start | bytes 294920 | tf_op jit(solution)/shard_map/ppermute | solution.py:26
  7.9 0.9 %collective-permute-start = (bf16[16,3072]{1,0:T(8,128)(2,1)S(1)}, bf16[16,3072]{1,0:T(8,128)(2,1)S(1)}, u32[]{:S(2)}, u32[]{:S(2)}) collective-permute-start(bf16[16,3072]{1,0:T(8,128)(2,1)S(1)} %shard_map.94), channel_id=1, source_target_pairs={{0,25},{1,24},{2,27},{3,26},{4,29},{5,28},{6,31},{7,30},{8,1},{9,0... | collective-permute-start | bytes 294920 | tf_op jit(solution)/shard_map/ppermute | solution.py:26
  8.8 0.8 %collective-permute-start.7 = (bf16[16,3072]{1,0:T(8,128)(2,1)S(1)}, bf16[16,3072]{1,0:T(8,128)(2,1)S(1)}, u32[]{:S(2)}, u32[]{:S(2)}) collective-permute-start(bf16[16,3072]{1,0:T(8,128)(2,1)S(1)} %shard_map.94), channel_id=1, source_target_pairs={{0,24},{1,25},{2,26},{3,27},{4,28},{5,29},{6,30},{7,31},{8,0},{9,1... | collective-permute-start | bytes 294920 | tf_op jit(solution)/shard_map/ppermute | solution.py:26
  9.7 1.7 %shard_map.95 = (bf16[160,4096]{1,0:T(8,128)(2,1)S(1)}, bf16[160,128]{1,0:T(8,128)(2,1)S(1)}, f32[160,64]{1,0:T(8,128)S(1)}, f32[160,64]{1,0:T(8,128)S(1)}, f32[...) custom-call(bf16[160,96]{1,0:T(8,128)(2,1)} %bitcast.21, s32[5,1,96]{2,1,0:T(1,128)} %bitcast.23, bf16[160,96]{1,0:T(8,128)(2,1)} %bitcast.22, ...), custom_call_target="tpu_custom_call" | custom-call | bytes 16777216 | tf_op jit(solution)/shard_map/pallas_call | solution.py:117
  11.4 0.0 collective-permute-done.2.refs_3_
  11.4 0.1 collective-permute-done.1.refs_2_
  11.5 0.5 %collective-permute-done.refs_1_ = bf16[16,3072]{1,0:T(8,128)(2,1)S(1)} collective-permute-done((bf16[16,3072]{1,0:T(8,128)(2,1)S(1)}, bf16[16,3072]{1,0:T(8,128)(2,1)S(1)}, u32[]{:S(2)}, u32[]{:S(2)}) %collective-permute-start) | collective-permute-done | bytes 98336 | tf_op jit(solution)/shard_map/ppermute | solution.py:26
  11.9 2.6 %collective-permute-start.3 = (bf16[16,3072]{1,0:T(8,128)(2,1)S(1)}, bf16[16,3072]{1,0:T(8,128)(2,1)S(1)}, u32[]{:S(2)}, u32[]{:S(2)}) collective-permute-start(bf16[16,3072]{1,0:T(8,128)(2,1)S(1)} %collective-permute-done.refs_1_), channel_id=1, source_target_pairs={{0,6},{1,7},{2,4},{3,5},{4,2},{5,3},{6,0},{7,1},{8,14},{9,15},{10,... | collective-permute-start | bytes 294920 | tf_op jit(solution)/shard_map/ppermute | solution.py:20
  14.6 1.5 %collective-permute-start.6 = (bf16[16,3072]{1,0:T(8,128)(2,1)S(1)}, bf16[16,3072]{1,0:T(8,128)(2,1)S(1)}, u32[]{:S(2)}, u32[]{:S(2)}) collective-permute-start(bf16[16,3072]{1,0:T(8,128)(2,1)S(1)} %collective-permute-done.1.refs_2_), channel_id=1, source_target_pairs={{0,1},{1,0},{2,3},{3,2},{4,5},{5,4},{6,7},{7,6},{8,9},{9,8},{10,11... | collective-permute-start | bytes 294920 | tf_op jit(solution)/shard_map/ppermute | solution.py:20
  16.1 0.5 %collective-permute-start.5 = (bf16[16,3072]{1,0:T(8,128)(2,1)S(1)}, bf16[16,3072]{1,0:T(8,128)(2,1)S(1)}, u32[]{:S(2)}, u32[]{:S(2)}) collective-permute-start(bf16[16,3072]{1,0:T(8,128)(2,1)S(1)} %collective-permute-done.2.refs_3_), channel_id=1, source_target_pairs={{0,1},{1,0},{2,3},{3,2},{4,5},{5,4},{6,7},{7,6},{8,9},{9,8},{10,11... | collective-permute-start | bytes 294920 | tf_op jit(solution)/shard_map/ppermute | solution.py:20
  16.6 0.0 collective-permute-start.4
  16.6 0.0 collective-permute-done.7.refs_0_
  16.6 0.6 %shard_map.96 = (bf16[64,4096]{1,0:T(8,128)(2,1)S(1)}, bf16[160,96]{1,0:T(8,128)(2,1)S(1)}, bf16[160,96]{1,0:T(8,128)(2,1)S(1)}) custom-call(bf16[16,3072]{1,0:T(8,128)(2,1)S(1)} %collective-permute-done.7.refs_0_, bf16[16,3072]{1,0:T(8,128)(2,1)S(1)} %collective-permute-done.refs_1_, bf16[16,3072]{1,0:T(8,128)(2,1)S(1)} %collective-permute-done.1.refs_2_, ...), custom_call_target="tpu_custom_call" | custom-call | bytes 16777216 | tf_op jit(solution)/shard_map/pallas_call | solution.py:172
  17.3 1.5 %collective-permute-done.3.refs_0_ = bf16[16,3072]{1,0:T(8,128)(2,1)S(1)} collective-permute-done((bf16[16,3072]{1,0:T(8,128)(2,1)S(1)}, bf16[16,3072]{1,0:T(8,128)(2,1)S(1)}, u32[]{:S(2)}, u32[]{:S(2)}) %collective-permute-start.3) | collective-permute-done | bytes 98336 | tf_op jit(solution)/shard_map/ppermute | solution.py:20
  18.8 1.4 %collective-permute-done.6.refs_3_ = bf16[16,3072]{1,0:T(8,128)(2,1)S(1)} collective-permute-done((bf16[16,3072]{1,0:T(8,128)(2,1)S(1)}, bf16[16,3072]{1,0:T(8,128)(2,1)S(1)}, u32[]{:S(2)}, u32[]{:S(2)}) %collective-permute-start.6) | collective-permute-done | bytes 98336 | tf_op jit(solution)/shard_map/ppermute | solution.py:20
  20.2 1.8 %collective-permute-done.5.refs_2_ = bf16[16,3072]{1,0:T(8,128)(2,1)S(1)} collective-permute-done((bf16[16,3072]{1,0:T(8,128)(2,1)S(1)}, bf16[16,3072]{1,0:T(8,128)(2,1)S(1)}, u32[]{:S(2)}, u32[]{:S(2)}) %collective-permute-start.5) | collective-permute-done | bytes 98336 | tf_op jit(solution)/shard_map/ppermute | solution.py:20
  21.9 0.0 collective-permute-done.4.refs_1_
  21.9 2.2 %shard_map.97 = (bf16[160,4096]{1,0:T(8,128)(2,1)}, bf16[160,96]{1,0:T(8,128)(2,1)}, bf16[160,96]{1,0:T(8,128)(2,1)}) custom-call(bf16[16,3072]{1,0:T(8,128)(2,1)S(1)} %collective-permute-done.3.refs_0_, bf16[16,3072]{1,0:T(8,128)(2,1)S(1)} %collective-permute-done.4.refs_1_, bf16[16,3072]{1,0:T(8,128)(2,1)S(1)} %collective-permute-done.5.refs_2_, ...), custom_call_target="tpu_custom_call" | custom-call | bytes 16777216 | tf_op jit(solution)/shard_map/pallas_call | solution.py:217
Async XLA Ops:
  1.6 9.8 %collective-permute-start.2 = (bf16[16,3072]{1,0:T(8,128)(2,1)S(1)}, bf16[16,3072]{1,0:T(8,128)(2,1)S(1)}, u32[]{:S(2)}, u32[]{:S(2)}) collective-permute-start(bf16[16,3072]{1,0:T(8,128)(2,1)S(1)} %shard_map.94), channel_id=1, source_target_pairs={{0,28},{1,29},{2,30},{3,31},{4,24},{5,25},{6,26},{7,27},{8,4},{9,5... | collective-permute-start | bytes 294920 | tf_op jit(solution)/shard_map/ppermute | solution.py:26
  6.0 5.4 %collective-permute-start.1 = (bf16[16,3072]{1,0:T(8,128)(2,1)S(1)}, bf16[16,3072]{1,0:T(8,128)(2,1)S(1)}, u32[]{:S(2)}, u32[]{:S(2)}) collective-permute-start(bf16[16,3072]{1,0:T(8,128)(2,1)S(1)} %shard_map.94), channel_id=1, source_target_pairs={{0,26},{1,27},{2,24},{3,25},{4,30},{5,31},{6,28},{7,29},{8,2},{9,3... | collective-permute-start | bytes 294920 | tf_op jit(solution)/shard_map/ppermute | solution.py:26
  7.9 4.1 %collective-permute-start = (bf16[16,3072]{1,0:T(8,128)(2,1)S(1)}, bf16[16,3072]{1,0:T(8,128)(2,1)S(1)}, u32[]{:S(2)}, u32[]{:S(2)}) collective-permute-start(bf16[16,3072]{1,0:T(8,128)(2,1)S(1)} %shard_map.94), channel_id=1, source_target_pairs={{0,25},{1,24},{2,27},{3,26},{4,29},{5,28},{6,31},{7,30},{8,1},{9,0... | collective-permute-start | bytes 294920 | tf_op jit(solution)/shard_map/ppermute | solution.py:26
  8.8 7.8 %collective-permute-start.7 = (bf16[16,3072]{1,0:T(8,128)(2,1)S(1)}, bf16[16,3072]{1,0:T(8,128)(2,1)S(1)}, u32[]{:S(2)}, u32[]{:S(2)}) collective-permute-start(bf16[16,3072]{1,0:T(8,128)(2,1)S(1)} %shard_map.94), channel_id=1, source_target_pairs={{0,24},{1,25},{2,26},{3,27},{4,28},{5,29},{6,30},{7,31},{8,0},{9,1... | collective-permute-start | bytes 294920 | tf_op jit(solution)/shard_map/ppermute | solution.py:26
  11.9 6.8 %collective-permute-start.3 = (bf16[16,3072]{1,0:T(8,128)(2,1)S(1)}, bf16[16,3072]{1,0:T(8,128)(2,1)S(1)}, u32[]{:S(2)}, u32[]{:S(2)}) collective-permute-start(bf16[16,3072]{1,0:T(8,128)(2,1)S(1)} %collective-permute-done.refs_1_), channel_id=1, source_target_pairs={{0,6},{1,7},{2,4},{3,5},{4,2},{5,3},{6,0},{7,1},{8,14},{9,15},{10,... | collective-permute-start | bytes 294920 | tf_op jit(solution)/shard_map/ppermute | solution.py:20
  14.6 5.6 %collective-permute-start.6 = (bf16[16,3072]{1,0:T(8,128)(2,1)S(1)}, bf16[16,3072]{1,0:T(8,128)(2,1)S(1)}, u32[]{:S(2)}, u32[]{:S(2)}) collective-permute-start(bf16[16,3072]{1,0:T(8,128)(2,1)S(1)} %collective-permute-done.1.refs_2_), channel_id=1, source_target_pairs={{0,1},{1,0},{2,3},{3,2},{4,5},{5,4},{6,7},{7,6},{8,9},{9,8},{10,11... | collective-permute-start | bytes 294920 | tf_op jit(solution)/shard_map/ppermute | solution.py:20
  16.1 5.8 %collective-permute-start.5 = (bf16[16,3072]{1,0:T(8,128)(2,1)S(1)}, bf16[16,3072]{1,0:T(8,128)(2,1)S(1)}, u32[]{:S(2)}, u32[]{:S(2)}) collective-permute-start(bf16[16,3072]{1,0:T(8,128)(2,1)S(1)} %collective-permute-done.2.refs_3_), channel_id=1, source_target_pairs={{0,1},{1,0},{2,3},{3,2},{4,5},{5,4},{6,7},{7,6},{8,9},{9,8},{10,11... | collective-permute-start | bytes 294920 | tf_op jit(solution)/shard_map/ppermute | solution.py:20
  16.6 5.3 %collective-permute-start.4 = (bf16[16,3072]{1,0:T(8,128)(2,1)S(1)}, bf16[16,3072]{1,0:T(8,128)(2,1)S(1)}, u32[]{:S(2)}, u32[]{:S(2)}) collective-permute-start(bf16[16,3072]{1,0:T(8,128)(2,1)S(1)} %collective-permute-done.2.refs_3_), channel_id=1, source_target_pairs={{0,2},{1,3},{2,0},{3,1},{4,6},{5,7},{6,4},{7,5},{8,10},{9,11},{10,... | collective-permute-start | bytes 294920 | tf_op jit(solution)/shard_map/ppermute | solution.py:20
where the time goes:
time: 24.3 us; the launch traced here: 24.2 us
  starting transfers between devices  12.8 us (53%)
  Pallas kernels  5.5 us (23%)
  waiting for transfers between devices  5.24 us (22%)
  between operations  0.67 us (3%)
    ppermute x4, starting transfers between devices, send(): return lax.ppermute(array, ('section', 'tp'), pairs)  8.09 us
    ppermute x4, waiting for transfers between devices, send(): return lax.ppermute(array, 'tp', [(t, t ^ flip) for t in range(count)])  4.67 us
    ppermute x4, starting transfers between devices, send(): return lax.ppermute(array, 'tp', [(t, t ^ flip) for t in range(count)])  4.67 us
    pallas_call x1, Pallas kernels, last(): pl.pallas_call(functools.partial(last_kernel, group, count, chunk), out_s...  2.23 us
    pallas_call x1, Pallas kernels, prepare(): pl.pallas_call(functools.partial(prepare_kernel, groups, count), out_shap...  1.69 us
    pallas_call x1, Pallas kernels, pack(): pl.pallas_call(pack_kernel, out_shape=pltpu.VMEM((TILE, width * count //...  0.93 us
    pallas_call x1, Pallas kernels, stage(): pl.pallas_call(functools.partial(stage_kernel, group, count, len(before)...  0.64 us
    ppermute x4, waiting for transfers between devices, send(): return lax.ppermute(array, ('section', 'tp'), pairs)  0.57 us
  transfers between devices with their start and end apart: 8, of which 5 were waited for; matrix products, arithmetic and copies ran while one was open for 0% of the time, Pallas kernels for 10%

commit v1 on v0

--- a/solution.py
+++ b/solution.py
@@ -26,11 +26,14 @@
     return lax.ppermute(array, ("section", "tp"), pairs)
 
 
+def started(source_ref, target_ref, sem):
+    copy = pltpu.make_async_copy(source_ref, target_ref, sem)
+    copy.start()
+    return [copy]
+
+
 def fetched(refs, held_refs, sems):
-    copies = [pltpu.make_async_copy(ref, held, sems.at[i]) for i, (ref, held) in enumerate(zip(refs, held_refs))]
-    for copy in copies:
-        copy.start()
-    return copies
+    return sum([started(ref, held, sems.at[i]) for i, (ref, held) in enumerate(zip(refs, held_refs))], [])
 
 
 def pack_kernel(held_ref, packed_ref, rows_ref, sems):
@@ -183,28 +186,26 @@
     )(*operands)
 
 
-def last_kernel(group, count, chunk, *refs):
+def last_kernel(group, count, parts, *refs):
     slot_refs, earlier_ref = refs[: len(group)], refs[len(group)]
-    weight_ref, hidden_ref = refs[-12:-10]
-    factor_refs, before_refs = refs[-10:-8], refs[-8:-6]
-    down_ref, *grad_refs, newest_ref, tile_ref, sems = refs[-6:]
-    width = weight_ref.shape[1]
+    weight_ref, hidden_ref, *factor_refs = refs[len(group) + 1 : len(group) + 5]
+    before_refs, out_refs = refs[len(group) + 5 : len(group) + 7], refs[len(group) + 7 : len(group) + 10]
+    newest_ref, *held_refs, sems = refs[len(group) + 10 :]
     restore(slot_refs, newest_ref, count)
-    hidden = hidden_ref[...]
+    incoming = jnp.concatenate([earlier_ref[...], newest_ref[...]], axis=0)
+    rows = hidden_ref.shape[0] // parts
     copies = []
-    for at in range(0, width, chunk):
-        incoming = jnp.concatenate([earlier_ref[:, at : at + chunk], newest_ref[:, at : at + chunk]], axis=0)
-        down = jnp.dot(hidden, incoming, preferred_element_type=jnp.float32)
-        tile_ref[:, at : at + chunk] = down.astype(jnp.bfloat16)
-        copy = pltpu.make_async_copy(
-            tile_ref.at[:, pl.ds(at, chunk)], down_ref.at[:, pl.ds(at, chunk)], sems.at[at // chunk]
-        )
-        copy.start()
-        copies.append(copy)
+    for i in range(parts):
+        here = pl.ds(i * rows, rows)
+        down = jnp.dot(hidden_ref[here, :], incoming, preferred_element_type=jnp.float32)
+        held_refs[0][here, :] = down.astype(jnp.bfloat16)
+        copies += started(held_refs[0].at[here, :], out_refs[0].at[here, :], sems.at[2 + i])
     slope = lax.dot_general(
         weight_ref[...], newest_ref[...], (((1,), (1,)), ((), ())), preferred_element_type=jnp.float32
     )
-    grads(group, count, slope, factor_refs, before_refs, grad_refs)
+    grads(group, count, slope, factor_refs, before_refs, held_refs[1:])
+    for i in range(2):
+        copies += started(held_refs[1 + i], out_refs[1 + i], sems.at[i])
     for copy in copies:
         copy.wait()
 
@@ -212,21 +213,18 @@
 def last(group, count, slots, earlier, weight, hidden, factors, before):
     units, width = weight.shape
     tokens = before[0].shape[1]
-    chunk = width // 8
+    parts = 2 if units % (2 * TILE) == 0 else 1
     operands = (*slots, earlier, weight, hidden, *factors, *before)
+    shapes = [(units, width), (units, tokens), (units, tokens)]
     return pl.pallas_call(
-        functools.partial(last_kernel, group, count, chunk),
-        out_shape=(
-            jax.ShapeDtypeStruct((units, width), jnp.bfloat16),
-            jax.ShapeDtypeStruct((units, tokens), jnp.bfloat16),
-            jax.ShapeDtypeStruct((units, tokens), jnp.bfloat16),
-        ),
+        functools.partial(last_kernel, group, count, parts),
+        out_shape=[jax.ShapeDtypeStruct(shape, jnp.bfloat16) for shape in shapes],
         in_specs=[WHOLE] * len(operands),
-        out_specs=[LEFT, WHOLE, WHOLE],
+        out_specs=[LEFT] * 3,
         scratch_shapes=[
             pltpu.VMEM((len(group) * TILE, width), jnp.bfloat16),
-            pltpu.VMEM((units, width), jnp.bfloat16),
-            pltpu.SemaphoreType.DMA((width // chunk,)),
+            *[pltpu.VMEM(shape, jnp.bfloat16) for shape in shapes],
+            pltpu.SemaphoreType.DMA((2 + parts,)),
         ],
         compiler_params=PARAMS,
         cost_estimate=COST,
@@ -237,9 +235,10 @@
     n = lax.axis_size("tp")
     count = grad_held.shape[1]
     p = pack(grad_held[0])
-    groups = [[f for f in range(n) if f & (f - 1) == 0], [f for f in reversed(range(n)) if f & (f - 1)]]
+    first = [f for f in range(n) if f & (f - 1) == 0]
+    groups = [[*first, 3], [f for f in range(5, n) if f not in first]]
     got = {}
-    for flip in reversed(groups[0]):
+    for flip in reversed(first):
         got[flip] = send(p, flip, 1)
     weight, hidden, factors = prepare(
         groups,
@@ -251,15 +250,15 @@
         down_codes[0],
         down_exponents.transpose(1, 0, 2),
     )
-    for flip, tied in zip(groups[0][1:], lax.optimization_barrier((*[got[f] for f in groups[0][1:]], hidden))):
-        got[flip] = tied
-    for flip in sorted(groups[1], key=lambda f: -(f & 1) * f):
-        step = flip & -flip
-        if flip & 1 and flip - 1 not in groups[0]:
-            step = flip - 1
-        got[flip] = send(got[flip - step], step, 0)
+    got[3] = send(got[2], 1, 0)
+    got[n // 2], *_ = lax.optimization_barrier((got[n // 2], hidden))
     early = [got[j] for j in groups[0]]
     earlier, *before = stage(groups[0], count, n * count, early, weight, factors[0], [])
+    for flip in groups[1]:
+        step = 1 if flip - 1 in first else 2
+        if flip & 1 and step == 2:
+            got[flip - step], *_ = lax.optimization_barrier((got[flip - step], earlier))
+        got[flip] = send(got[flip - step], step, 0)
     late = [got[j] for j in groups[1]]
     down_grad, gate_grad, up_grad = last(groups[1], count, late, earlier, weight, hidden, factors[1], before)
     return down_grad[None], gate_grad.T[None], up_grad.T[None]

time: 24.3 us -> 24.6 us (1.012)
  waiting for transfers between devices: 5.24 us -> 7.91 us
  starting transfers between devices: 12.8 us -> 10.9 us
  Pallas kernels: 5.5 us -> 4.93 us
    ppermute x4, waiting for transfers between devices: 4.67 us -> 7.31 us  [send(): return lax.ppermute(array, 'tp', [(t, t ^ flip) for t in range(count)])]
    ppermute x4, starting transfers between devices: 4.67 us -> 2.83 us  [send(): return lax.ppermute(array, 'tp', [(t, t ^ flip) for t in range(count)])]
    pallas_call x1, Pallas kernels: 2.23 us -> 1.65 us  [last(): pl.pallas_call(functools.partial(last_kernel, group, count, parts), out_s...]
where the time goes in v1:
time: 24.6 us; the launch traced here: 24.4 us
  starting transfers between devices  10.9 us (44%)
  waiting for transfers between devices  7.91 us (32%)
  Pallas kernels  4.93 us (20%)
  between operations  0.67 us (3%)
    ppermute x4, starting transfers between devices, send(): return lax.ppermute(array, ('section', 'tp'), pairs)  8.09 us
    ppermute x4, waiting for transfers between devices, send(): return lax.ppermute(array, 'tp', [(t, t ^ flip) for t in range(count)])  7.31 us
    ppermute x4, starting transfers between devices, send(): return lax.ppermute(array, 'tp', [(t, t ^ flip) for t in range(count)])  2.83 us
    pallas_call x1, Pallas kernels, prepare(): pl.pallas_call(functools.partial(prepare_kernel, groups, count), out_shap...  1.69 us
    pallas_call x1, Pallas kernels, last(): pl.pallas_call(functools.partial(last_kernel, group, count, parts), out_s...  1.65 us
    pallas_call x1, Pallas kernels, pack(): pl.pallas_call(pack_kernel, out_shape=pltpu.VMEM((TILE, width * count //...  0.93 us
    pallas_call x1, Pallas kernels, stage(): pl.pallas_call(functools.partial(stage_kernel, group, count, len(before)...  0.66 us
    ppermute x4, waiting for transfers between devices, send(): return lax.ppermute(array, ('section', 'tp'), pairs)  0.59 us
  transfers between devices with their start and end apart: 8, of which 5 were waited for; matrix products, arithmetic and copies ran while one was open for 0% of the time, Pallas kernels for 10%

profile of v1, /device:TPU:0, one launch (start us, length us, event | category | flops | bytes accessed | tf_op | source)
XLA Modules:
  0.0 24.4 jit_solution(14700049132179879044)
XLA Ops:
  0.6 0.9 %shard_map.94 = bf16[16,3072]{1,0:T(8,128)(2,1)S(1)} custom-call(bf16[12,4096]{1,0:T(8,128)(2,1)} %bitcast.19), custom_call_target="tpu_custom_call" | custom-call | tf_op jit(solution)/shard_map/pallas_call | solution.py:52
  1.6 3.4 %collective-permute-start.4 = (bf16[16,3072]{1,0:T(8,128)(2,1)S(1)}, bf16[16,3072]{1,0:T(8,128)(2,1)S(1)}, u32[]{:S(2)}, u32[]{:S(2)}) collective-permute-start(bf16[16,3072]{1,0:T(8,128)(2,1)S(1)} %shard_map.94), channel_id=1, source_target_pairs={{0,26},{1,27},{2,24},{3,25},{4,30},{5,31},{6,28},{7,29},{8,2},{9,3... | collective-permute-start | bytes 294920 | tf_op jit(solution)/shard_map/ppermute | solution.py:26
  5.0 2.9 %collective-permute-start = (bf16[16,3072]{1,0:T(8,128)(2,1)S(1)}, bf16[16,3072]{1,0:T(8,128)(2,1)S(1)}, u32[]{:S(2)}, u32[]{:S(2)}) collective-permute-start(bf16[16,3072]{1,0:T(8,128)(2,1)S(1)} %shard_map.94), channel_id=1, source_target_pairs={{0,28},{1,29},{2,30},{3,31},{4,24},{5,25},{6,26},{7,27},{8,4},{9,5... | collective-permute-start | bytes 294920 | tf_op jit(solution)/shard_map/ppermute | solution.py:26
  7.9 0.9 %collective-permute-start.3 = (bf16[16,3072]{1,0:T(8,128)(2,1)S(1)}, bf16[16,3072]{1,0:T(8,128)(2,1)S(1)}, u32[]{:S(2)}, u32[]{:S(2)}) collective-permute-start(bf16[16,3072]{1,0:T(8,128)(2,1)S(1)} %shard_map.94), channel_id=1, source_target_pairs={{0,25},{1,24},{2,27},{3,26},{4,29},{5,28},{6,31},{7,30},{8,1},{9,0... | collective-permute-start | bytes 294920 | tf_op jit(solution)/shard_map/ppermute | solution.py:26
  8.8 0.8 %collective-permute-start.2 = (bf16[16,3072]{1,0:T(8,128)(2,1)S(1)}, bf16[16,3072]{1,0:T(8,128)(2,1)S(1)}, u32[]{:S(2)}, u32[]{:S(2)}) collective-permute-start(bf16[16,3072]{1,0:T(8,128)(2,1)S(1)} %shard_map.94), channel_id=1, source_target_pairs={{0,24},{1,25},{2,26},{3,27},{4,28},{5,29},{6,30},{7,31},{8,0},{9,1... | collective-permute-start | bytes 294920 | tf_op jit(solution)/shard_map/ppermute | solution.py:26
  9.7 1.7 %shard_map.95 = (bf16[160,4096]{1,0:T(8,128)(2,1)S(1)}, bf16[160,128]{1,0:T(8,128)(2,1)S(1)}, f32[160,80]{1,0:T(8,128)S(1)}, f32[160,80]{1,0:T(8,128)S(1)}, f32[...) custom-call(bf16[160,96]{1,0:T(8,128)(2,1)} %bitcast.21, s32[5,1,96]{2,1,0:T(1,128)} %bitcast.23, bf16[160,96]{1,0:T(8,128)(2,1)} %bitcast.22, ...), custom_call_target="tpu_custom_call" | custom-call | bytes 16777216 | tf_op jit(solution)/shard_map/pallas_call | solution.py:120
  11.4 0.0 collective-permute-done.4.refs_2_
  11.4 0.6 %collective-permute-start.5 = (bf16[16,3072]{1,0:T(8,128)(2,1)S(1)}, bf16[16,3072]{1,0:T(8,128)(2,1)S(1)}, u32[]{:S(2)}, u32[]{:S(2)}) collective-permute-start(bf16[16,3072]{1,0:T(8,128)(2,1)S(1)} %collective-permute-done.4.refs_2_), channel_id=1, source_target_pairs={{0,1},{1,0},{2,3},{3,2},{4,5},{5,4},{6,7},{7,6},{8,9},{9,8},{10,11... | collective-permute-start | bytes 294920 | tf_op jit(solution)/shard_map/ppermute | solution.py:20
  11.9 0.6 %collective-permute-done.refs_3_ = bf16[16,3072]{1,0:T(8,128)(2,1)S(1)} collective-permute-done((bf16[16,3072]{1,0:T(8,128)(2,1)S(1)}, bf16[16,3072]{1,0:T(8,128)(2,1)S(1)}, u32[]{:S(2)}, u32[]{:S(2)}) %collective-permute-start) | collective-permute-done | bytes 98336 | tf_op jit(solution)/shard_map/ppermute | solution.py:26
  12.5 1.5 %collective-permute-start.1 = (bf16[16,3072]{1,0:T(8,128)(2,1)S(1)}, bf16[16,3072]{1,0:T(8,128)(2,1)S(1)}, u32[]{:S(2)}, u32[]{:S(2)}) collective-permute-start(bf16[16,3072]{1,0:T(8,128)(2,1)S(1)} %collective-permute-done.refs_3_), channel_id=1, source_target_pairs={{0,1},{1,0},{2,3},{3,2},{4,5},{5,4},{6,7},{7,6},{8,9},{9,8},{10,11... | collective-permute-start | bytes 294920 | tf_op jit(solution)/shard_map/ppermute | solution.py:20
  14.0 0.3 %collective-permute-start.6 = (bf16[16,3072]{1,0:T(8,128)(2,1)S(1)}, bf16[16,3072]{1,0:T(8,128)(2,1)S(1)}, u32[]{:S(2)}, u32[]{:S(2)}) collective-permute-start(bf16[16,3072]{1,0:T(8,128)(2,1)S(1)} %collective-permute-done.refs_3_), channel_id=1, source_target_pairs={{0,2},{1,3},{2,0},{3,1},{4,6},{5,7},{6,4},{7,5},{8,10},{9,11},{10,... | collective-permute-start | bytes 294920 | tf_op jit(solution)/shard_map/ppermute | solution.py:20
  14.3 0.0 collective-permute-done.3.refs_1_
  14.3 0.0 collective-permute-done.2.refs_0_
  14.3 1.9 %collective-permute-done.5.refs_4_ = bf16[16,3072]{1,0:T(8,128)(2,1)S(1)} collective-permute-done((bf16[16,3072]{1,0:T(8,128)(2,1)S(1)}, bf16[16,3072]{1,0:T(8,128)(2,1)S(1)}, u32[]{:S(2)}, u32[]{:S(2)}) %collective-permute-start.5) | collective-permute-done | bytes 98336 | tf_op jit(solution)/shard_map/ppermute | solution.py:20
  16.3 0.7 %shard_map.96 = (bf16[80,4096]{1,0:T(8,128)(2,1)S(1)}, bf16[160,96]{1,0:T(8,128)(2,1)S(1)}, bf16[160,96]{1,0:T(8,128)(2,1)S(1)}) custom-call(bf16[16,3072]{1,0:T(8,128)(2,1)S(1)} %collective-permute-done.2.refs_0_, bf16[16,3072]{1,0:T(8,128)(2,1)S(1)} %collective-permute-done.3.refs_1_, bf16[16,3072]{1,0:T(8,128)(2,1)S(1)} %collective-permute-done.4.refs_2_, ...), custom_call_target="tpu_custom_call" | custom-call | bytes 16777216 | tf_op jit(solution)/shard_map/pallas_call | solution.py:175
  16.9 1.2 %collective-permute-done.1.refs_0_ = bf16[16,3072]{1,0:T(8,128)(2,1)S(1)} collective-permute-done((bf16[16,3072]{1,0:T(8,128)(2,1)S(1)}, bf16[16,3072]{1,0:T(8,128)(2,1)S(1)}, u32[]{:S(2)}, u32[]{:S(2)}) %collective-permute-start.1) | collective-permute-done | bytes 98336 | tf_op jit(solution)/shard_map/ppermute | solution.py:20
  18.2 0.4 %collective-permute-start.7 = (bf16[16,3072]{1,0:T(8,128)(2,1)S(1)}, bf16[16,3072]{1,0:T(8,128)(2,1)S(1)}, u32[]{:S(2)}, u32[]{:S(2)}) collective-permute-start(bf16[16,3072]{1,0:T(8,128)(2,1)S(1)} %collective-permute-done.1.refs_0_), channel_id=1, source_target_pairs={{0,2},{1,3},{2,0},{3,1},{4,6},{5,7},{6,4},{7,5},{8,10},{9,11},{10,... | collective-permute-start | bytes 294920 | tf_op jit(solution)/shard_map/ppermute | solution.py:20
  18.6 0.5 %collective-permute-done.6.refs_1_ = bf16[16,3072]{1,0:T(8,128)(2,1)S(1)} collective-permute-done((bf16[16,3072]{1,0:T(8,128)(2,1)S(1)}, bf16[16,3072]{1,0:T(8,128)(2,1)S(1)}, u32[]{:S(2)}, u32[]{:S(2)}) %collective-permute-start.6) | collective-permute-done | bytes 98336 | tf_op jit(solution)/shard_map/ppermute | solution.py:20
  19.1 3.7 %collective-permute-done.7.refs_2_ = bf16[16,3072]{1,0:T(8,128)(2,1)S(1)} collective-permute-done((bf16[16,3072]{1,0:T(8,128)(2,1)S(1)}, bf16[16,3072]{1,0:T(8,128)(2,1)S(1)}, u32[]{:S(2)}, u32[]{:S(2)}) %collective-permute-start.7) | collective-permute-done | bytes 98336 | tf_op jit(solution)/shard_map/ppermute | solution.py:20
  22.8 1.7 %shard_map.97 = (bf16[160,4096]{1,0:T(8,128)(2,1)}, bf16[160,96]{1,0:T(8,128)(2,1)}, bf16[160,96]{1,0:T(8,128)(2,1)}) custom-call(bf16[16,3072]{1,0:T(8,128)(2,1)S(1)} %collective-permute-done.1.refs_0_, bf16[16,3072]{1,0:T(8,128)(2,1)S(1)} %collective-permute-done.6.refs_1_, bf16[16,3072]{1,0:T(8,128)(2,1)S(1)} %collective-permute-done.7.refs_2_, ...), custom_call_target="tpu_custom_call" | custom-call | bytes 16777216 | tf_op jit(solution)/shard_map/pallas_call | solution.py:219
Async XLA Ops:
  1.6 9.8 %collective-permute-start.4 = (bf16[16,3072]{1,0:T(8,128)(2,1)S(1)}, bf16[16,3072]{1,0:T(8,128)(2,1)S(1)}, u32[]{:S(2)}, u32[]{:S(2)}) collective-permute-start(bf16[16,3072]{1,0:T(8,128)(2,1)S(1)} %shard_map.94), channel_id=1, source_target_pairs={{0,26},{1,27},{2,24},{3,25},{4,30},{5,31},{6,28},{7,29},{8,2},{9,3... | collective-permute-start | bytes 294920 | tf_op jit(solution)/shard_map/ppermute | solution.py:26
  5.0 7.5 %collective-permute-start = (bf16[16,3072]{1,0:T(8,128)(2,1)S(1)}, bf16[16,3072]{1,0:T(8,128)(2,1)S(1)}, u32[]{:S(2)}, u32[]{:S(2)}) collective-permute-start(bf16[16,3072]{1,0:T(8,128)(2,1)S(1)} %shard_map.94), channel_id=1, source_target_pairs={{0,28},{1,29},{2,30},{3,31},{4,24},{5,25},{6,26},{7,27},{8,4},{9,5... | collective-permute-start | bytes 294920 | tf_op jit(solution)/shard_map/ppermute | solution.py:26
  7.9 6.5 %collective-permute-start.3 = (bf16[16,3072]{1,0:T(8,128)(2,1)S(1)}, bf16[16,3072]{1,0:T(8,128)(2,1)S(1)}, u32[]{:S(2)}, u32[]{:S(2)}) collective-permute-start(bf16[16,3072]{1,0:T(8,128)(2,1)S(1)} %shard_map.94), channel_id=1, source_target_pairs={{0,25},{1,24},{2,27},{3,26},{4,29},{5,28},{6,31},{7,30},{8,1},{9,0... | collective-permute-start | bytes 294920 | tf_op jit(solution)/shard_map/ppermute | solution.py:26
  8.8 5.5 %collective-permute-start.2 = (bf16[16,3072]{1,0:T(8,128)(2,1)S(1)}, bf16[16,3072]{1,0:T(8,128)(2,1)S(1)}, u32[]{:S(2)}, u32[]{:S(2)}) collective-permute-start(bf16[16,3072]{1,0:T(8,128)(2,1)S(1)} %shard_map.94), channel_id=1, source_target_pairs={{0,24},{1,25},{2,26},{3,27},{4,28},{5,29},{6,30},{7,31},{8,0},{9,1... | collective-permute-start | bytes 294920 | tf_op jit(solution)/shard_map/ppermute | solution.py:26
  11.4 4.9 %collective-permute-start.5 = (bf16[16,3072]{1,0:T(8,128)(2,1)S(1)}, bf16[16,3072]{1,0:T(8,128)(2,1)S(1)}, u32[]{:S(2)}, u32[]{:S(2)}) collective-permute-start(bf16[16,3072]{1,0:T(8,128)(2,1)S(1)} %collective-permute-done.4.refs_2_), channel_id=1, source_target_pairs={{0,1},{1,0},{2,3},{3,2},{4,5},{5,4},{6,7},{7,6},{8,9},{9,8},{10,11... | collective-permute-start | bytes 294920 | tf_op jit(solution)/shard_map/ppermute | solution.py:20
  12.5 5.6 %collective-permute-start.1 = (bf16[16,3072]{1,0:T(8,128)(2,1)S(1)}, bf16[16,3072]{1,0:T(8,128)(2,1)S(1)}, u32[]{:S(2)}, u32[]{:S(2)}) collective-permute-start(bf16[16,3072]{1,0:T(8,128)(2,1)S(1)} %collective-permute-done.refs_3_), channel_id=1, source_target_pairs={{0,1},{1,0},{2,3},{3,2},{4,5},{5,4},{6,7},{7,6},{8,9},{9,8},{10,11... | collective-permute-start | bytes 294920 | tf_op jit(solution)/shard_map/ppermute | solution.py:20
  14.0 5.1 %collective-permute-start.6 = (bf16[16,3072]{1,0:T(8,128)(2,1)S(1)}, bf16[16,3072]{1,0:T(8,128)(2,1)S(1)}, u32[]{:S(2)}, u32[]{:S(2)}) collective-permute-start(bf16[16,3072]{1,0:T(8,128)(2,1)S(1)} %collective-permute-done.refs_3_), channel_id=1, source_target_pairs={{0,2},{1,3},{2,0},{3,1},{4,6},{5,7},{6,4},{7,5},{8,10},{9,11},{10,... | collective-permute-start | bytes 294920 | tf_op jit(solution)/shard_map/ppermute | solution.py:20
  18.2 4.6 %collective-permute-start.7 = (bf16[16,3072]{1,0:T(8,128)(2,1)S(1)}, bf16[16,3072]{1,0:T(8,128)(2,1)S(1)}, u32[]{:S(2)}, u32[]{:S(2)}) collective-permute-start(bf16[16,3072]{1,0:T(8,128)(2,1)S(1)} %collective-permute-done.1.refs_0_), channel_id=1, source_target_pairs={{0,2},{1,3},{2,0},{3,1},{4,6},{5,7},{6,4},{7,5},{8,10},{9,11},{10,... | collective-permute-start | bytes 294920 | tf_op jit(solution)/shard_map/ppermute | solution.py:20

commit v2 on v1

--- a/solution.py
+++ b/solution.py
@@ -236,10 +236,15 @@
     count = grad_held.shape[1]
     p = pack(grad_held[0])
     first = [f for f in range(n) if f & (f - 1) == 0]
-    groups = [[*first, 3], [f for f in range(5, n) if f not in first]]
+    groups = [first, [f for f in range(n) if f not in first]]
     got = {}
     for flip in reversed(first):
         got[flip] = send(p, flip, 1)
+    for flip in reversed(groups[1]):
+        step = flip & -flip
+        if flip & 1 and flip - 1 not in first:
+            step = flip - 1
+        got[flip] = send(got[flip - step], step, 0)
     weight, hidden, factors = prepare(
         groups,
         count,
@@ -250,15 +255,8 @@
         down_codes[0],
         down_exponents.transpose(1, 0, 2),
     )
-    got[3] = send(got[2], 1, 0)
-    got[n // 2], *_ = lax.optimization_barrier((got[n // 2], hidden))
     early = [got[j] for j in groups[0]]
     earlier, *before = stage(groups[0], count, n * count, early, weight, factors[0], [])
-    for flip in groups[1]:
-        step = 1 if flip - 1 in first else 2
-        if flip & 1 and step == 2:
-            got[flip - step], *_ = lax.optimization_barrier((got[flip - step], earlier))
-        got[flip] = send(got[flip - step], step, 0)
     late = [got[j] for j in groups[1]]
     down_grad, gate_grad, up_grad = last(groups[1], count, late, earlier, weight, hidden, factors[1], before)
     return down_grad[None], gate_grad.T[None], up_grad.T[None]

time: 24.6 us -> 22.3 us (0.907)
  waiting for transfers between devices: 7.91 us -> 3.04 us
  starting transfers between devices: 10.9 us -> 13.5 us
    ppermute x4, waiting for transfers between devices: 7.31 us -> 2.2 us  [send(): return lax.ppermute(array, 'tp', [(t, t ^ flip) for t in range(count)])]
    ppermute x4, starting transfers between devices: 2.83 us -> 5.36 us  [send(): return lax.ppermute(array, 'tp', [(t, t ^ flip) for t in range(count)])]
    ppermute x4, waiting for transfers between devices: 0.59 us -> 0.84 us  [send(): return lax.ppermute(array, ('section', 'tp'), pairs)]
  transfers between devices with their start and end apart: 8 -> 8, of which waited for: 5 -> 4; matrix products, arithmetic and copies ran while one was open for 0% -> 0% of each run, Pallas kernels for 10% -> 11%
where the time goes in v2:
time: 22.3 us; the launch traced here: 22.1 us
  starting transfers between devices  13.5 us (61%)
  Pallas kernels  4.92 us (22%)
  waiting for transfers between devices  3.04 us (14%)
  between operations  0.68 us (3%)
    ppermute x4, starting transfers between devices, send(): return lax.ppermute(array, ('section', 'tp'), pairs)  8.09 us
    ppermute x4, starting transfers between devices, send(): return lax.ppermute(array, 'tp', [(t, t ^ flip) for t in range(count)])  5.36 us
    ppermute x4, waiting for transfers between devices, send(): return lax.ppermute(array, 'tp', [(t, t ^ flip) for t in range(count)])  2.2 us
    pallas_call x1, Pallas kernels, prepare(): pl.pallas_call(functools.partial(prepare_kernel, groups, count), out_shap...  1.69 us
    pallas_call x1, Pallas kernels, last(): pl.pallas_call(functools.partial(last_kernel, group, count, parts), out_s...  1.65 us
    pallas_call x1, Pallas kernels, pack(): pl.pallas_call(pack_kernel, out_shape=pltpu.VMEM((TILE, width * count //...  0.93 us
    ppermute x4, waiting for transfers between devices, send(): return lax.ppermute(array, ('section', 'tp'), pairs)  0.84 us
    pallas_call x1, Pallas kernels, stage(): pl.pallas_call(functools.partial(stage_kernel, group, count, len(before)...  0.65 us
  transfers between devices with their start and end apart: 8, of which 4 were waited for; matrix products, arithmetic and copies ran while one was open for 0% of the time, Pallas kernels for 11%

profile of v2, /device:TPU:0, one launch (start us, length us, event | category | flops | bytes accessed | tf_op | source)
XLA Modules:
  0.0 22.1 jit_solution(12040604055265992224)
XLA Ops:
  0.6 0.9 %shard_map.94 = bf16[16,3072]{1,0:T(8,128)(2,1)S(1)} custom-call(bf16[12,4096]{1,0:T(8,128)(2,1)} %bitcast.19), custom_call_target="tpu_custom_call" | custom-call | tf_op jit(solution)/shard_map/pallas_call | solution.py:52
  1.6 3.4 %collective-permute-start.5 = (bf16[16,3072]{1,0:T(8,128)(2,1)S(1)}, bf16[16,3072]{1,0:T(8,128)(2,1)S(1)}, u32[]{:S(2)}, u32[]{:S(2)}) collective-permute-start(bf16[16,3072]{1,0:T(8,128)(2,1)S(1)} %shard_map.94), channel_id=1, source_target_pairs={{0,25},{1,24},{2,27},{3,26},{4,29},{5,28},{6,31},{7,30},{8,1},{9,0... | collective-permute-start | bytes 294920 | tf_op jit(solution)/shard_map/ppermute | solution.py:26
  5.0 2.9 %collective-permute-start.2 = (bf16[16,3072]{1,0:T(8,128)(2,1)S(1)}, bf16[16,3072]{1,0:T(8,128)(2,1)S(1)}, u32[]{:S(2)}, u32[]{:S(2)}) collective-permute-start(bf16[16,3072]{1,0:T(8,128)(2,1)S(1)} %shard_map.94), channel_id=1, source_target_pairs={{0,28},{1,29},{2,30},{3,31},{4,24},{5,25},{6,26},{7,27},{8,4},{9,5... | collective-permute-start | bytes 294920 | tf_op jit(solution)/shard_map/ppermute | solution.py:26
  7.8 1.0 %collective-permute-start = (bf16[16,3072]{1,0:T(8,128)(2,1)S(1)}, bf16[16,3072]{1,0:T(8,128)(2,1)S(1)}, u32[]{:S(2)}, u32[]{:S(2)}) collective-permute-start(bf16[16,3072]{1,0:T(8,128)(2,1)S(1)} %shard_map.94), channel_id=1, source_target_pairs={{0,26},{1,27},{2,24},{3,25},{4,30},{5,31},{6,28},{7,29},{8,2},{9,3... | collective-permute-start | bytes 294920 | tf_op jit(solution)/shard_map/ppermute | solution.py:26
  8.8 0.8 %collective-permute-start.7 = (bf16[16,3072]{1,0:T(8,128)(2,1)S(1)}, bf16[16,3072]{1,0:T(8,128)(2,1)S(1)}, u32[]{:S(2)}, u32[]{:S(2)}) collective-permute-start(bf16[16,3072]{1,0:T(8,128)(2,1)S(1)} %shard_map.94), channel_id=1, source_target_pairs={{0,24},{1,25},{2,26},{3,27},{4,28},{5,29},{6,30},{7,31},{8,0},{9,1... | collective-permute-start | bytes 294920 | tf_op jit(solution)/shard_map/ppermute | solution.py:26
  9.7 0.0 collective-permute-done.5.refs_1_
  9.7 1.1 %collective-permute-start.6 = (bf16[16,3072]{1,0:T(8,128)(2,1)S(1)}, bf16[16,3072]{1,0:T(8,128)(2,1)S(1)}, u32[]{:S(2)}, u32[]{:S(2)}) collective-permute-start(bf16[16,3072]{1,0:T(8,128)(2,1)S(1)} %collective-permute-done.5.refs_1_), channel_id=1, source_target_pairs={{0,6},{1,7},{2,4},{3,5},{4,2},{5,3},{6,0},{7,1},{8,14},{9,15},{10,... | collective-permute-start | bytes 294920 | tf_op jit(solution)/shard_map/ppermute | solution.py:20
  10.8 0.8 %collective-permute-done.2.refs_3_ = bf16[16,3072]{1,0:T(8,128)(2,1)S(1)} collective-permute-done((bf16[16,3072]{1,0:T(8,128)(2,1)S(1)}, bf16[16,3072]{1,0:T(8,128)(2,1)S(1)}, u32[]{:S(2)}, u32[]{:S(2)}) %collective-permute-start.2) | collective-permute-done | bytes 98336 | tf_op jit(solution)/shard_map/ppermute | solution.py:26
  11.6 2.2 %collective-permute-start.4 = (bf16[16,3072]{1,0:T(8,128)(2,1)S(1)}, bf16[16,3072]{1,0:T(8,128)(2,1)S(1)}, u32[]{:S(2)}, u32[]{:S(2)}) collective-permute-start(bf16[16,3072]{1,0:T(8,128)(2,1)S(1)} %collective-permute-done.2.refs_3_), channel_id=1, source_target_pairs={{0,2},{1,3},{2,0},{3,1},{4,6},{5,7},{6,4},{7,5},{8,10},{9,11},{10,... | collective-permute-start | bytes 294920 | tf_op jit(solution)/shard_map/ppermute | solution.py:20
  13.8 0.5 %collective-permute-start.3 = (bf16[16,3072]{1,0:T(8,128)(2,1)S(1)}, bf16[16,3072]{1,0:T(8,128)(2,1)S(1)}, u32[]{:S(2)}, u32[]{:S(2)}) collective-permute-start(bf16[16,3072]{1,0:T(8,128)(2,1)S(1)} %collective-permute-done.2.refs_3_), channel_id=1, source_target_pairs={{0,1},{1,0},{2,3},{3,2},{4,5},{5,4},{6,7},{7,6},{8,9},{9,8},{10,11... | collective-permute-start | bytes 294920 | tf_op jit(solution)/shard_map/ppermute | solution.py:20
  14.3 0.0 collective-permute-done.refs_2_
  14.3 1.5 %collective-permute-start.1 = (bf16[16,3072]{1,0:T(8,128)(2,1)S(1)}, bf16[16,3072]{1,0:T(8,128)(2,1)S(1)}, u32[]{:S(2)}, u32[]{:S(2)}) collective-permute-start(bf16[16,3072]{1,0:T(8,128)(2,1)S(1)} %collective-permute-done.refs_2_), channel_id=1, source_target_pairs={{0,1},{1,0},{2,3},{3,2},{4,5},{5,4},{6,7},{7,6},{8,9},{9,8},{10,11... | collective-permute-start | bytes 294920 | tf_op jit(solution)/shard_map/ppermute | solution.py:20
  15.9 1.7 %shard_map.95 = (bf16[160,4096]{1,0:T(8,128)(2,1)S(1)}, bf16[160,128]{1,0:T(8,128)(2,1)S(1)}, f32[160,64]{1,0:T(8,128)S(1)}, f32[160,64]{1,0:T(8,128)S(1)}, f32[...) custom-call(bf16[160,96]{1,0:T(8,128)(2,1)} %bitcast.21, s32[5,1,96]{2,1,0:T(1,128)} %bitcast.23, bf16[160,96]{1,0:T(8,128)(2,1)} %bitcast.22, ...), custom_call_target="tpu_custom_call" | custom-call | bytes 16777216 | tf_op jit(solution)/shard_map/pallas_call | solution.py:120
  17.6 0.0 collective-permute-done.7.refs_0_
  17.6 0.6 %shard_map.96 = (bf16[64,4096]{1,0:T(8,128)(2,1)S(1)}, bf16[160,96]{1,0:T(8,128)(2,1)S(1)}, bf16[160,96]{1,0:T(8,128)(2,1)S(1)}) custom-call(bf16[16,3072]{1,0:T(8,128)(2,1)S(1)} %collective-permute-done.7.refs_0_, bf16[16,3072]{1,0:T(8,128)(2,1)S(1)} %collective-permute-done.5.refs_1_, bf16[16,3072]{1,0:T(8,128)(2,1)S(1)} %collective-permute-done.refs_2_, ...), custom_call_target="tpu_custom_call" | custom-call | bytes 16777216 | tf_op jit(solution)/shard_map/pallas_call | solution.py:175
  18.2 0.0 collective-permute-done.6.refs_3_
  18.2 0.1 collective-permute-done.4.refs_2_
  18.3 1.0 %collective-permute-done.3.refs_1_ = bf16[16,3072]{1,0:T(8,128)(2,1)S(1)} collective-permute-done((bf16[16,3072]{1,0:T(8,128)(2,1)S(1)}, bf16[16,3072]{1,0:T(8,128)(2,1)S(1)}, u32[]{:S(2)}, u32[]{:S(2)}) %collective-permute-start.3) | collective-permute-done | bytes 98336 | tf_op jit(solution)/shard_map/ppermute | solution.py:20
  19.4 1.1 %collective-permute-done.1.refs_0_ = bf16[16,3072]{1,0:T(8,128)(2,1)S(1)} collective-permute-done((bf16[16,3072]{1,0:T(8,128)(2,1)S(1)}, bf16[16,3072]{1,0:T(8,128)(2,1)S(1)}, u32[]{:S(2)}, u32[]{:S(2)}) %collective-permute-start.1) | collective-permute-done | bytes 98336 | tf_op jit(solution)/shard_map/ppermute | solution.py:20
  20.4 1.7 %shard_map.97 = (bf16[160,4096]{1,0:T(8,128)(2,1)}, bf16[160,96]{1,0:T(8,128)(2,1)}, bf16[160,96]{1,0:T(8,128)(2,1)}) custom-call(bf16[16,3072]{1,0:T(8,128)(2,1)S(1)} %collective-permute-done.1.refs_0_, bf16[16,3072]{1,0:T(8,128)(2,1)S(1)} %collective-permute-done.3.refs_1_, bf16[16,3072]{1,0:T(8,128)(2,1)S(1)} %collective-permute-done.4.refs_2_, ...), custom_call_target="tpu_custom_call" | custom-call | bytes 16777216 | tf_op jit(solution)/shard_map/pallas_call | solution.py:219
Async XLA Ops:
  1.6 8.1 %collective-permute-start.5 = (bf16[16,3072]{1,0:T(8,128)(2,1)S(1)}, bf16[16,3072]{1,0:T(8,128)(2,1)S(1)}, u32[]{:S(2)}, u32[]{:S(2)}) collective-permute-start(bf16[16,3072]{1,0:T(8,128)(2,1)S(1)} %shard_map.94), channel_id=1, source_target_pairs={{0,25},{1,24},{2,27},{3,26},{4,29},{5,28},{6,31},{7,30},{8,1},{9,0... | collective-permute-start | bytes 294920 | tf_op jit(solution)/shard_map/ppermute | solution.py:26
  5.0 6.7 %collective-permute-start.2 = (bf16[16,3072]{1,0:T(8,128)(2,1)S(1)}, bf16[16,3072]{1,0:T(8,128)(2,1)S(1)}, u32[]{:S(2)}, u32[]{:S(2)}) collective-permute-start(bf16[16,3072]{1,0:T(8,128)(2,1)S(1)} %shard_map.94), channel_id=1, source_target_pairs={{0,28},{1,29},{2,30},{3,31},{4,24},{5,25},{6,26},{7,27},{8,4},{9,5... | collective-permute-start | bytes 294920 | tf_op jit(solution)/shard_map/ppermute | solution.py:26
  7.8 6.5 %collective-permute-start = (bf16[16,3072]{1,0:T(8,128)(2,1)S(1)}, bf16[16,3072]{1,0:T(8,128)(2,1)S(1)}, u32[]{:S(2)}, u32[]{:S(2)}) collective-permute-start(bf16[16,3072]{1,0:T(8,128)(2,1)S(1)} %shard_map.94), channel_id=1, source_target_pairs={{0,26},{1,27},{2,24},{3,25},{4,30},{5,31},{6,28},{7,29},{8,2},{9,3... | collective-permute-start | bytes 294920 | tf_op jit(solution)/shard_map/ppermute | solution.py:26
  8.8 8.8 %collective-permute-start.7 = (bf16[16,3072]{1,0:T(8,128)(2,1)S(1)}, bf16[16,3072]{1,0:T(8,128)(2,1)S(1)}, u32[]{:S(2)}, u32[]{:S(2)}) collective-permute-start(bf16[16,3072]{1,0:T(8,128)(2,1)S(1)} %shard_map.94), channel_id=1, source_target_pairs={{0,24},{1,25},{2,26},{3,27},{4,28},{5,29},{6,30},{7,31},{8,0},{9,1... | collective-permute-start | bytes 294920 | tf_op jit(solution)/shard_map/ppermute | solution.py:26
  9.7 8.6 %collective-permute-start.6 = (bf16[16,3072]{1,0:T(8,128)(2,1)S(1)}, bf16[16,3072]{1,0:T(8,128)(2,1)S(1)}, u32[]{:S(2)}, u32[]{:S(2)}) collective-permute-start(bf16[16,3072]{1,0:T(8,128)(2,1)S(1)} %collective-permute-done.5.refs_1_), channel_id=1, source_target_pairs={{0,6},{1,7},{2,4},{3,5},{4,2},{5,3},{6,0},{7,1},{8,14},{9,15},{10,... | collective-permute-start | bytes 294920 | tf_op jit(solution)/shard_map/ppermute | solution.py:20
  11.6 6.7 %collective-permute-start.4 = (bf16[16,3072]{1,0:T(8,128)(2,1)S(1)}, bf16[16,3072]{1,0:T(8,128)(2,1)S(1)}, u32[]{:S(2)}, u32[]{:S(2)}) collective-permute-start(bf16[16,3072]{1,0:T(8,128)(2,1)S(1)} %collective-permute-done.2.refs_3_), channel_id=1, source_target_pairs={{0,2},{1,3},{2,0},{3,1},{4,6},{5,7},{6,4},{7,5},{8,10},{9,11},{10,... | collective-permute-start | bytes 294920 | tf_op jit(solution)/shard_map/ppermute | solution.py:20
  13.8 5.6 %collective-permute-start.3 = (bf16[16,3072]{1,0:T(8,128)(2,1)S(1)}, bf16[16,3072]{1,0:T(8,128)(2,1)S(1)}, u32[]{:S(2)}, u32[]{:S(2)}) collective-permute-start(bf16[16,3072]{1,0:T(8,128)(2,1)S(1)} %collective-permute-done.2.refs_3_), channel_id=1, source_target_pairs={{0,1},{1,0},{2,3},{3,2},{4,5},{5,4},{6,7},{7,6},{8,9},{9,8},{10,11... | collective-permute-start | bytes 294920 | tf_op jit(solution)/shard_map/ppermute | solution.py:20
  14.3 6.1 %collective-permute-start.1 = (bf16[16,3072]{1,0:T(8,128)(2,1)S(1)}, bf16[16,3072]{1,0:T(8,128)(2,1)S(1)}, u32[]{:S(2)}, u32[]{:S(2)}) collective-permute-start(bf16[16,3072]{1,0:T(8,128)(2,1)S(1)} %collective-permute-done.refs_2_), channel_id=1, source_target_pairs={{0,1},{1,0},{2,3},{3,2},{4,5},{5,4},{6,7},{7,6},{8,9},{9,8},{10,11... | collective-permute-start | bytes 294920 | tf_op jit(solution)/shard_map/ppermute | solution.py:20

commit v3 on v2

--- a/solution.py
+++ b/solution.py
@@ -186,20 +186,19 @@
     )(*operands)
 
 
-def last_kernel(group, count, parts, *refs):
-    slot_refs, earlier_ref = refs[: len(group)], refs[len(group)]
-    weight_ref, hidden_ref, *factor_refs = refs[len(group) + 1 : len(group) + 5]
-    before_refs, out_refs = refs[len(group) + 5 : len(group) + 7], refs[len(group) + 7 : len(group) + 10]
-    newest_ref, *held_refs, sems = refs[len(group) + 10 :]
+def last_kernel(slots, group, count, parts, *refs):
+    slot_refs, earlier_refs, refs = refs[: len(group)], refs[len(group) : slots], refs[slots:]
+    weight_ref, hidden_ref, *factor_refs = refs[:4]
+    before_refs, out_refs, (newest_ref, *held_refs, sems) = refs[4:6], refs[6:9], refs[9:]
     restore(slot_refs, newest_ref, count)
-    incoming = jnp.concatenate([earlier_ref[...], newest_ref[...]], axis=0)
-    rows = hidden_ref.shape[0] // parts
+    chunk = weight_ref.shape[1] // parts
     copies = []
     for i in range(parts):
-        here = pl.ds(i * rows, rows)
-        down = jnp.dot(hidden_ref[here, :], incoming, preferred_element_type=jnp.float32)
-        held_refs[0][here, :] = down.astype(jnp.bfloat16)
-        copies += started(held_refs[0].at[here, :], out_refs[0].at[here, :], sems.at[2 + i])
+        here = pl.ds(i * chunk, chunk)
+        incoming = jnp.concatenate([ref[:, here] for ref in (*earlier_refs, newest_ref)], axis=0)
+        down = jnp.dot(hidden_ref[...], incoming, preferred_element_type=jnp.float32)
+        held_refs[0][:, here] = down.astype(jnp.bfloat16)
+        copies += started(held_refs[0].at[:, here], out_refs[0].at[:, here], sems.at[2 + i])
     slope = lax.dot_general(
         weight_ref[...], newest_ref[...], (((1,), (1,)), ((), ())), preferred_element_type=jnp.float32
     )
@@ -213,11 +212,11 @@
 def last(group, count, slots, earlier, weight, hidden, factors, before):
     units, width = weight.shape
     tokens = before[0].shape[1]
-    parts = 2 if units % (2 * TILE) == 0 else 1
-    operands = (*slots, earlier, weight, hidden, *factors, *before)
+    parts = 4
+    operands = (*slots, *earlier, weight, hidden, *factors, *before)
     shapes = [(units, width), (units, tokens), (units, tokens)]
     return pl.pallas_call(
-        functools.partial(last_kernel, group, count, parts),
+        functools.partial(last_kernel, len(slots) + len(earlier), group, count, parts),
         out_shape=[jax.ShapeDtypeStruct(shape, jnp.bfloat16) for shape in shapes],
         in_specs=[WHOLE] * len(operands),
         out_specs=[LEFT] * 3,
@@ -236,11 +235,13 @@
     count = grad_held.shape[1]
     p = pack(grad_held[0])
     first = [f for f in range(n) if f & (f - 1) == 0]
-    groups = [first, [f for f in range(n) if f not in first]]
+    rest = [f for f in range(n) if f not in first]
+    late = [f for f in rest if f - n // 2 in first]
+    groups = [group for group in (first[::-1], [f for f in reversed(rest) if f not in late], late[::-1]) if group]
     got = {}
     for flip in reversed(first):
         got[flip] = send(p, flip, 1)
-    for flip in reversed(groups[1]):
+    for flip in reversed(rest):
         step = flip & -flip
         if flip & 1 and flip - 1 not in first:
             step = flip - 1
@@ -255,10 +256,12 @@
         down_codes[0],
         down_exponents.transpose(1, 0, 2),
     )
-    early = [got[j] for j in groups[0]]
-    earlier, *before = stage(groups[0], count, n * count, early, weight, factors[0], [])
-    late = [got[j] for j in groups[1]]
-    down_grad, gate_grad, up_grad = last(groups[1], count, late, earlier, weight, hidden, factors[1], before)
+    earlier, before = [], []
+    for group, pair in zip(groups[:-1], factors):
+        incoming, *before = stage(group, count, n * count, [got[j] for j in group], weight, pair, before)
+        earlier.append(incoming)
+    arrived = [got[j] for j in groups[-1]]
+    down_grad, gate_grad, up_grad = last(groups[-1], count, arrived, earlier, weight, hidden, factors[-1], before)
     return down_grad[None], gate_grad.T[None], up_grad.T[None]
 
 
@@ -290,7 +293,7 @@
     count, width = operands[-1].shape[1:]
     free = TILE - count
     small = n & (n - 1) == 0 and 4 <= n <= TILE
-    fits = 0 < free < TILE and count % free == 0 and width * free % (TILE * 8 * 128) == 0
+    fits = 0 < free < TILE and count % free == 0 and width * free % (TILE * 128) == 0 and width % (4 * 128) == 0
     return fanned(*operands) if small and fits else ringed(*operands)
 
 

time: 22.3 us -> 24 us (1.076)
  waiting for transfers between devices: 3.04 us -> 5.33 us
  starting transfers between devices: 13.5 us -> 12.2 us
  Pallas kernels: 4.92 us -> 5.58 us
    ppermute x4, waiting for transfers between devices: 0.84 us -> 3.49 us  [send(): return lax.ppermute(array, ('section', 'tp'), pairs)]
    ppermute x4, starting transfers between devices: 5.36 us -> 4.13 us  [send(): return lax.ppermute(array, 'tp', [(t, t ^ flip) for t in range(count)])]
    pallas_call x1 -> x2, Pallas kernels: 0.65 us -> 1.28 us  [stage(): pl.pallas_call(functools.partial(stage_kernel, group, count, len(before)...]
    ppermute x4, waiting for transfers between devices: 2.2 us -> 1.84 us  [send(): return lax.ppermute(array, 'tp', [(t, t ^ flip) for t in range(count)])]
  transfers between devices with their start and end apart: 8 -> 8, of which waited for: 4 -> 2; matrix products, arithmetic and copies ran while one was open for 0% -> 0% of each run, Pallas kernels for 11% -> 12%
where the time goes in v3:
time: 24 us; the launch traced here: 23.8 us
  starting transfers between devices  12.2 us (51%)
  Pallas kernels  5.58 us (23%)
  waiting for transfers between devices  5.33 us (22%)
  between operations  0.69 us (3%)
    ppermute x4, starting transfers between devices, send(): return lax.ppermute(array, ('section', 'tp'), pairs)  8.09 us
    ppermute x4, starting transfers between devices, send(): return lax.ppermute(array, 'tp', [(t, t ^ flip) for t in range(count)])  4.13 us
    ppermute x4, waiting for transfers between devices, send(): return lax.ppermute(array, ('section', 'tp'), pairs)  3.49 us
    ppermute x4, waiting for transfers between devices, send(): return lax.ppermute(array, 'tp', [(t, t ^ flip) for t in range(count)])  1.84 us
    pallas_call x1, Pallas kernels, prepare(): pl.pallas_call(functools.partial(prepare_kernel, groups, count), out_shap...  1.69 us
    pallas_call x1, Pallas kernels, last(): pl.pallas_call(functools.partial(last_kernel, len(slots) + len(earlier),...  1.68 us
    pallas_call x2, Pallas kernels, stage(): pl.pallas_call(functools.partial(stage_kernel, group, count, len(before)...  1.28 us
    pallas_call x1, Pallas kernels, pack(): pl.pallas_call(pack_kernel, out_shape=pltpu.VMEM((TILE, width * count //...  0.93 us
  transfers between devices with their start and end apart: 8, of which 2 were waited for; matrix products, arithmetic and copies ran while one was open for 0% of the time, Pallas kernels for 12%

profile of v3, /device:TPU:0, one launch (start us, length us, event | category | flops | bytes accessed | tf_op | source)
XLA Modules:
  0.0 23.8 jit_solution(10381698744254526921)
XLA Ops:
  0.6 0.9 %shard_map.94 = bf16[16,3072]{1,0:T(8,128)(2,1)S(1)} custom-call(bf16[12,4096]{1,0:T(8,128)(2,1)} %bitcast.19), custom_call_target="tpu_custom_call" | custom-call | tf_op jit(solution)/shard_map/pallas_call | solution.py:52
  1.6 3.4 %collective-permute-start.4 = (bf16[16,3072]{1,0:T(8,128)(2,1)S(1)}, bf16[16,3072]{1,0:T(8,128)(2,1)S(1)}, u32[]{:S(2)}, u32[]{:S(2)}) collective-permute-start(bf16[16,3072]{1,0:T(8,128)(2,1)S(1)} %shard_map.94), channel_id=1, source_target_pairs={{0,25},{1,24},{2,27},{3,26},{4,29},{5,28},{6,31},{7,30},{8,1},{9,0... | collective-permute-start | bytes 294920 | tf_op jit(solution)/shard_map/ppermute | solution.py:26
  5.0 1.9 %collective-permute-start.3 = (bf16[16,3072]{1,0:T(8,128)(2,1)S(1)}, bf16[16,3072]{1,0:T(8,128)(2,1)S(1)}, u32[]{:S(2)}, u32[]{:S(2)}) collective-permute-start(bf16[16,3072]{1,0:T(8,128)(2,1)S(1)} %shard_map.94), channel_id=1, source_target_pairs={{0,26},{1,27},{2,24},{3,25},{4,30},{5,31},{6,28},{7,29},{8,2},{9,3... | collective-permute-start | bytes 294920 | tf_op jit(solution)/shard_map/ppermute | solution.py:26
  6.8 2.0 %collective-permute-start = (bf16[16,3072]{1,0:T(8,128)(2,1)S(1)}, bf16[16,3072]{1,0:T(8,128)(2,1)S(1)}, u32[]{:S(2)}, u32[]{:S(2)}) collective-permute-start(bf16[16,3072]{1,0:T(8,128)(2,1)S(1)} %shard_map.94), channel_id=1, source_target_pairs={{0,28},{1,29},{2,30},{3,31},{4,24},{5,25},{6,26},{7,27},{8,4},{9,5... | collective-permute-start | bytes 294920 | tf_op jit(solution)/shard_map/ppermute | solution.py:26
  8.8 0.8 %collective-permute-start.5 = (bf16[16,3072]{1,0:T(8,128)(2,1)S(1)}, bf16[16,3072]{1,0:T(8,128)(2,1)S(1)}, u32[]{:S(2)}, u32[]{:S(2)}) collective-permute-start(bf16[16,3072]{1,0:T(8,128)(2,1)S(1)} %shard_map.94), channel_id=1, source_target_pairs={{0,24},{1,25},{2,26},{3,27},{4,28},{5,29},{6,30},{7,31},{8,0},{9,1... | collective-permute-start | bytes 294920 | tf_op jit(solution)/shard_map/ppermute | solution.py:26
  9.7 0.0 collective-permute-done.4.refs_2_
  9.7 1.1 %collective-permute-start.6 = (bf16[16,3072]{1,0:T(8,128)(2,1)S(1)}, bf16[16,3072]{1,0:T(8,128)(2,1)S(1)}, u32[]{:S(2)}, u32[]{:S(2)}) collective-permute-start(bf16[16,3072]{1,0:T(8,128)(2,1)S(1)} %collective-permute-done.4.refs_2_), channel_id=1, source_target_pairs={{0,6},{1,7},{2,4},{3,5},{4,2},{5,3},{6,0},{7,1},{8,14},{9,15},{10,... | collective-permute-start | bytes 294920 | tf_op jit(solution)/shard_map/ppermute | solution.py:20
  10.8 0.0 collective-permute-done.3.refs_1_
  10.8 2.5 %collective-permute-start.7 = (bf16[16,3072]{1,0:T(8,128)(2,1)S(1)}, bf16[16,3072]{1,0:T(8,128)(2,1)S(1)}, u32[]{:S(2)}, u32[]{:S(2)}) collective-permute-start(bf16[16,3072]{1,0:T(8,128)(2,1)S(1)} %collective-permute-done.3.refs_1_), channel_id=1, source_target_pairs={{0,1},{1,0},{2,3},{3,2},{4,5},{5,4},{6,7},{7,6},{8,9},{9,8},{10,11... | collective-permute-start | bytes 294920 | tf_op jit(solution)/shard_map/ppermute | solution.py:20
  13.3 3.5 %collective-permute-done.refs_0_ = bf16[16,3072]{1,0:T(8,128)(2,1)S(1)} collective-permute-done((bf16[16,3072]{1,0:T(8,128)(2,1)S(1)}, bf16[16,3072]{1,0:T(8,128)(2,1)S(1)}, u32[]{:S(2)}, u32[]{:S(2)}) %collective-permute-start) | collective-permute-done | bytes 98336 | tf_op jit(solution)/shard_map/ppermute | solution.py:26
  16.8 0.5 %collective-permute-start.2 = (bf16[16,3072]{1,0:T(8,128)(2,1)S(1)}, bf16[16,3072]{1,0:T(8,128)(2,1)S(1)}, u32[]{:S(2)}, u32[]{:S(2)}) collective-permute-start(bf16[16,3072]{1,0:T(8,128)(2,1)S(1)} %collective-permute-done.refs_0_), channel_id=1, source_target_pairs={{0,1},{1,0},{2,3},{3,2},{4,5},{5,4},{6,7},{7,6},{8,9},{9,8},{10,11... | collective-permute-start | bytes 294920 | tf_op jit(solution)/shard_map/ppermute | solution.py:20
  17.3 0.0 collective-permute-start.1
  17.3 1.7 %shard_map.95 = (bf16[160,4096]{1,0:T(8,128)(2,1)S(1)}, bf16[160,128]{1,0:T(8,128)(2,1)S(1)}, f32[160,64]{1,0:T(8,128)S(1)}, f32[160,64]{1,0:T(8,128)S(1)}, f32[...) custom-call(bf16[160,96]{1,0:T(8,128)(2,1)} %bitcast.21, ...), custom_call_target="tpu_custom_call" | custom-call | bytes 16777216 | tf_op jit(solution)/shard_map/pallas_call | solution.py:120
  19.0 0.0 collective-permute-done.5.refs_3_
  19.0 0.6 %shard_map.96 = (bf16[64,4096]{1,0:T(8,128)(2,1)S(1)}, bf16[160,96]{1,0:T(8,128)(2,1)S(1)}, bf16[160,96]{1,0:T(8,128)(2,1)S(1)}) custom-call(bf16[16,3072]{1,0:T(8,128)(2,1)S(1)} %collective-permute-done.refs_0_, bf16[16,3072]{1,0:T(8,128)(2,1)S(1)} %collective-permute-done.3.refs_1_, bf16[16,3072]{1,0:T(8,128)(2,1)S(1)} %collective-permute-done.4.refs_2_, ...), custom_call_target="tpu_custom_call" | custom-call | bytes 16777216 | tf_op jit(solution)/shard_map/pallas_call | solution.py:175
  19.6 0.0 collective-permute-done.6.refs_0_
  19.7 0.0 collective-permute-done.7.refs_1_
  19.7 0.6 %shard_map.97 = (bf16[32,4096]{1,0:T(8,128)(2,1)S(1)}, bf16[160,96]{1,0:T(8,128)(2,1)S(1)}, bf16[160,96]{1,0:T(8,128)(2,1)S(1)}) custom-call(bf16[16,3072]{1,0:T(8,128)(2,1)S(1)} %collective-permute-done.6.refs_0_, bf16[16,3072]{1,0:T(8,128)(2,1)S(1)} %collective-permute-done.7.refs_1_, bf16[160,4096]{1,0:T(8,128)(2,1)S(1)} %get-tuple-element.20.refs_4_.refs_2_, ...), custom_call_target="tpu_custom_call" | custom-call | bytes 16777216 | tf_op jit(solution)/shard_map/pallas_call | solution.py:175
  20.3 1.8 %collective-permute-done.2.refs_1_ = bf16[16,3072]{1,0:T(8,128)(2,1)S(1)} collective-permute-done((bf16[16,3072]{1,0:T(8,128)(2,1)S(1)}, bf16[16,3072]{1,0:T(8,128)(2,1)S(1)}, u32[]{:S(2)}, u32[]{:S(2)}) %collective-permute-start.2) | collective-permute-done | bytes 98336 | tf_op jit(solution)/shard_map/ppermute | solution.py:20
  22.1 0.0 collective-permute-done.1.refs_0_
  22.2 1.7 %shard_map.98 = (bf16[160,4096]{1,0:T(8,128)(2,1)}, bf16[160,96]{1,0:T(8,128)(2,1)}, bf16[160,96]{1,0:T(8,128)(2,1)}) custom-call(bf16[16,3072]{1,0:T(8,128)(2,1)S(1)} %collective-permute-done.1.refs_0_, bf16[16,3072]{1,0:T(8,128)(2,1)S(1)} %collective-permute-done.2.refs_1_, bf16[64,4096]{1,0:T(8,128)(2,1)S(1)} %get-tuple-element.23.refs_2_, ...), custom_call_target="tpu_custom_call" | custom-call | bytes 16777216 | tf_op jit(solution)/shard_map/pallas_call | solution.py:218
Async XLA Ops:
  1.6 8.1 %collective-permute-start.4 = (bf16[16,3072]{1,0:T(8,128)(2,1)S(1)}, bf16[16,3072]{1,0:T(8,128)(2,1)S(1)}, u32[]{:S(2)}, u32[]{:S(2)}) collective-permute-start(bf16[16,3072]{1,0:T(8,128)(2,1)S(1)} %shard_map.94), channel_id=1, source_target_pairs={{0,25},{1,24},{2,27},{3,26},{4,29},{5,28},{6,31},{7,30},{8,1},{9,0... | collective-permute-start | bytes 294920 | tf_op jit(solution)/shard_map/ppermute | solution.py:26
  5.0 5.8 %collective-permute-start.3 = (bf16[16,3072]{1,0:T(8,128)(2,1)S(1)}, bf16[16,3072]{1,0:T(8,128)(2,1)S(1)}, u32[]{:S(2)}, u32[]{:S(2)}) collective-permute-start(bf16[16,3072]{1,0:T(8,128)(2,1)S(1)} %shard_map.94), channel_id=1, source_target_pairs={{0,26},{1,27},{2,24},{3,25},{4,30},{5,31},{6,28},{7,29},{8,2},{9,3... | collective-permute-start | bytes 294920 | tf_op jit(solution)/shard_map/ppermute | solution.py:26
  6.8 10.0 %collective-permute-start = (bf16[16,3072]{1,0:T(8,128)(2,1)S(1)}, bf16[16,3072]{1,0:T(8,128)(2,1)S(1)}, u32[]{:S(2)}, u32[]{:S(2)}) collective-permute-start(bf16[16,3072]{1,0:T(8,128)(2,1)S(1)} %shard_map.94), channel_id=1, source_target_pairs={{0,28},{1,29},{2,30},{3,31},{4,24},{5,25},{6,26},{7,27},{8,4},{9,5... | collective-permute-start | bytes 294920 | tf_op jit(solution)/shard_map/ppermute | solution.py:26
  8.8 10.2 %collective-permute-start.5 = (bf16[16,3072]{1,0:T(8,128)(2,1)S(1)}, bf16[16,3072]{1,0:T(8,128)(2,1)S(1)}, u32[]{:S(2)}, u32[]{:S(2)}) collective-permute-start(bf16[16,3072]{1,0:T(8,128)(2,1)S(1)} %shard_map.94), channel_id=1, source_target_pairs={{0,24},{1,25},{2,26},{3,27},{4,28},{5,29},{6,30},{7,31},{8,0},{9,1... | collective-permute-start | bytes 294920 | tf_op jit(solution)/shard_map/ppermute | solution.py:26
  9.7 10.0 %collective-permute-start.6 = (bf16[16,3072]{1,0:T(8,128)(2,1)S(1)}, bf16[16,3072]{1,0:T(8,128)(2,1)S(1)}, u32[]{:S(2)}, u32[]{:S(2)}) collective-permute-start(bf16[16,3072]{1,0:T(8,128)(2,1)S(1)} %collective-permute-done.4.refs_2_), channel_id=1, source_target_pairs={{0,6},{1,7},{2,4},{3,5},{4,2},{5,3},{6,0},{7,1},{8,14},{9,15},{10,... | collective-permute-start | bytes 294920 | tf_op jit(solution)/shard_map/ppermute | solution.py:20
  10.8 8.9 %collective-permute-start.7 = (bf16[16,3072]{1,0:T(8,128)(2,1)S(1)}, bf16[16,3072]{1,0:T(8,128)(2,1)S(1)}, u32[]{:S(2)}, u32[]{:S(2)}) collective-permute-start(bf16[16,3072]{1,0:T(8,128)(2,1)S(1)} %collective-permute-done.3.refs_1_), channel_id=1, source_target_pairs={{0,1},{1,0},{2,3},{3,2},{4,5},{5,4},{6,7},{7,6},{8,9},{9,8},{10,11... | collective-permute-start | bytes 294920 | tf_op jit(solution)/shard_map/ppermute | solution.py:20
  16.8 5.4 %collective-permute-start.2 = (bf16[16,3072]{1,0:T(8,128)(2,1)S(1)}, bf16[16,3072]{1,0:T(8,128)(2,1)S(1)}, u32[]{:S(2)}, u32[]{:S(2)}) collective-permute-start(bf16[16,3072]{1,0:T(8,128)(2,1)S(1)} %collective-permute-done.refs_0_), channel_id=1, source_target_pairs={{0,1},{1,0},{2,3},{3,2},{4,5},{5,4},{6,7},{7,6},{8,9},{9,8},{10,11... | collective-permute-start | bytes 294920 | tf_op jit(solution)/shard_map/ppermute | solution.py:20
  17.3 4.9 %collective-permute-start.1 = (bf16[16,3072]{1,0:T(8,128)(2,1)S(1)}, bf16[16,3072]{1,0:T(8,128)(2,1)S(1)}, u32[]{:S(2)}, u32[]{:S(2)}) collective-permute-start(bf16[16,3072]{1,0:T(8,128)(2,1)S(1)} %collective-permute-done.refs_0_), channel_id=1, source_target_pairs={{0,2},{1,3},{2,0},{3,1},{4,6},{5,7},{6,4},{7,5},{8,10},{9,11},{10,... | collective-permute-start | bytes 294920 | tf_op jit(solution)/shard_map/ppermute | solution.py:20

commit v4 on v3

--- a/solution.py
+++ b/solution.py
@@ -26,9 +26,9 @@
     return lax.ppermute(array, ("section", "tp"), pairs)
 
 
-def started(source_ref, target_ref, sem):
+def started(source_ref, target_ref, sem, priority=0):
     copy = pltpu.make_async_copy(source_ref, target_ref, sem)
-    copy.start()
+    copy.start(priority=priority)
     return [copy]
 
 
@@ -198,7 +198,7 @@
         incoming = jnp.concatenate([ref[:, here] for ref in (*earlier_refs, newest_ref)], axis=0)
         down = jnp.dot(hidden_ref[...], incoming, preferred_element_type=jnp.float32)
         held_refs[0][:, here] = down.astype(jnp.bfloat16)
-        copies += started(held_refs[0].at[:, here], out_refs[0].at[:, here], sems.at[2 + i])
+        copies += started(held_refs[0].at[:, here], out_refs[0].at[:, here], sems.at[2 + i], i % 2)
     slope = lax.dot_general(
         weight_ref[...], newest_ref[...], (((1,), (1,)), ((), ())), preferred_element_type=jnp.float32
     )
@@ -236,11 +236,12 @@
     p = pack(grad_held[0])
     first = [f for f in range(n) if f & (f - 1) == 0]
     rest = [f for f in range(n) if f not in first]
-    late = [f for f in rest if f - n // 2 in first]
-    groups = [group for group in (first[::-1], [f for f in reversed(rest) if f not in late], late[::-1]) if group]
+    groups = [first, [n - 1], rest[-2::-1]] if len(rest) > 1 else [first, rest]
     got = {}
     for flip in reversed(first):
         got[flip] = send(p, flip, 1)
+    for flip, tied in zip(first[2:], lax.optimization_barrier([got[f] for f in first[2:]])):
+        got[flip] = tied
     for flip in reversed(rest):
         step = flip & -flip
         if flip & 1 and flip - 1 not in first:

time: 24 us -> 22.5 us (0.938)
  waiting for transfers between devices: 5.33 us -> 4.07 us
  starting transfers between devices: 12.2 us -> 11.9 us
    ppermute x4, waiting for transfers between devices: 1.84 us -> 1.06 us  [send(): return lax.ppermute(array, 'tp', [(t, t ^ flip) for t in range(count)])]
    ppermute x4, waiting for transfers between devices: 3.49 us -> 3.02 us  [send(): return lax.ppermute(array, ('section', 'tp'), pairs)]
    ppermute x4, starting transfers between devices: 4.13 us -> 3.85 us  [send(): return lax.ppermute(array, 'tp', [(t, t ^ flip) for t in range(count)])]
  transfers between devices with their start and end apart: 8 -> 8, of which waited for: 2 -> 3; matrix products, arithmetic and copies ran while one was open for 0% -> 0% of each run, Pallas kernels for 12% -> 13%
where the time goes in v4:
time: 22.5 us; the launch traced here: 22.3 us
  starting transfers between devices  11.9 us (53%)
  Pallas kernels  5.62 us (25%)
  waiting for transfers between devices  4.07 us (18%)
  between operations  0.69 us (3%)
    ppermute x4, starting transfers between devices, send(): return lax.ppermute(array, ('section', 'tp'), pairs)  8.09 us
    ppermute x4, starting transfers between devices, send(): return lax.ppermute(array, 'tp', [(t, t ^ flip) for t in range(count)])  3.85 us
    ppermute x4, waiting for transfers between devices, send(): return lax.ppermute(array, ('section', 'tp'), pairs)  3.02 us
    pallas_call x1, Pallas kernels, last(): pl.pallas_call(functools.partial(last_kernel, len(slots) + len(earlier),...  1.7 us
    pallas_call x1, Pallas kernels, prepare(): pl.pallas_call(functools.partial(prepare_kernel, groups, count), out_shap...  1.69 us
    pallas_call x2, Pallas kernels, stage(): pl.pallas_call(functools.partial(stage_kernel, group, count, len(before)...  1.3 us
    ppermute x4, waiting for transfers between devices, send(): return lax.ppermute(array, 'tp', [(t, t ^ flip) for t in range(count)])  1.06 us
    pallas_call x1, Pallas kernels, pack(): pl.pallas_call(pack_kernel, out_shape=pltpu.VMEM((TILE, width * count //...  0.93 us
  transfers between devices with their start and end apart: 8, of which 3 were waited for; matrix products, arithmetic and copies ran while one was open for 0% of the time, Pallas kernels for 13%

profile of v4, /device:TPU:0, one launch (start us, length us, event | category | flops | bytes accessed | tf_op | source)
XLA Modules:
  0.0 22.3 jit_solution(2754206794696789894)
XLA Ops:
  0.6 0.9 %shard_map.94 = bf16[16,3072]{1,0:T(8,128)(2,1)S(1)} custom-call(bf16[12,4096]{1,0:T(8,128)(2,1)} %bitcast.19), custom_call_target="tpu_custom_call" | custom-call | tf_op jit(solution)/shard_map/pallas_call | solution.py:52
  1.6 3.4 %collective-permute-start.6 = (bf16[16,3072]{1,0:T(8,128)(2,1)S(1)}, bf16[16,3072]{1,0:T(8,128)(2,1)S(1)}, u32[]{:S(2)}, u32[]{:S(2)}) collective-permute-start(bf16[16,3072]{1,0:T(8,128)(2,1)S(1)} %shard_map.94), channel_id=1, source_target_pairs={{0,25},{1,24},{2,27},{3,26},{4,29},{5,28},{6,31},{7,30},{8,1},{9,0... | collective-permute-start | bytes 294920 | tf_op jit(solution)/shard_map/ppermute | solution.py:26
  5.0 2.9 %collective-permute-start.1 = (bf16[16,3072]{1,0:T(8,128)(2,1)S(1)}, bf16[16,3072]{1,0:T(8,128)(2,1)S(1)}, u32[]{:S(2)}, u32[]{:S(2)}) collective-permute-start(bf16[16,3072]{1,0:T(8,128)(2,1)S(1)} %shard_map.94), channel_id=1, source_target_pairs={{0,28},{1,29},{2,30},{3,31},{4,24},{5,25},{6,26},{7,27},{8,4},{9,5... | collective-permute-start | bytes 294920 | tf_op jit(solution)/shard_map/ppermute | solution.py:26
  7.8 1.0 %collective-permute-start = (bf16[16,3072]{1,0:T(8,128)(2,1)S(1)}, bf16[16,3072]{1,0:T(8,128)(2,1)S(1)}, u32[]{:S(2)}, u32[]{:S(2)}) collective-permute-start(bf16[16,3072]{1,0:T(8,128)(2,1)S(1)} %shard_map.94), channel_id=1, source_target_pairs={{0,26},{1,27},{2,24},{3,25},{4,30},{5,31},{6,28},{7,29},{8,2},{9,3... | collective-permute-start | bytes 294920 | tf_op jit(solution)/shard_map/ppermute | solution.py:26
  8.8 0.8 %collective-permute-start.5 = (bf16[16,3072]{1,0:T(8,128)(2,1)S(1)}, bf16[16,3072]{1,0:T(8,128)(2,1)S(1)}, u32[]{:S(2)}, u32[]{:S(2)}) collective-permute-start(bf16[16,3072]{1,0:T(8,128)(2,1)S(1)} %shard_map.94), channel_id=1, source_target_pairs={{0,24},{1,25},{2,26},{3,27},{4,28},{5,29},{6,30},{7,31},{8,0},{9,1... | collective-permute-start | bytes 294920 | tf_op jit(solution)/shard_map/ppermute | solution.py:26
  9.7 0.0 collective-permute-done.6.refs_1_
  9.7 1.1 %collective-permute-start.7 = (bf16[16,3072]{1,0:T(8,128)(2,1)S(1)}, bf16[16,3072]{1,0:T(8,128)(2,1)S(1)}, u32[]{:S(2)}, u32[]{:S(2)}) collective-permute-start(bf16[16,3072]{1,0:T(8,128)(2,1)S(1)} %collective-permute-done.6.refs_1_), channel_id=1, source_target_pairs={{0,6},{1,7},{2,4},{3,5},{4,2},{5,3},{6,0},{7,1},{8,14},{9,15},{10,... | collective-permute-start | bytes 294920 | tf_op jit(solution)/shard_map/ppermute | solution.py:20
  10.8 0.8 %collective-permute-done.1.refs_3_ = bf16[16,3072]{1,0:T(8,128)(2,1)S(1)} collective-permute-done((bf16[16,3072]{1,0:T(8,128)(2,1)S(1)}, bf16[16,3072]{1,0:T(8,128)(2,1)S(1)}, u32[]{:S(2)}, u32[]{:S(2)}) %collective-permute-start.1) | collective-permute-done | bytes 98336 | tf_op jit(solution)/shard_map/ppermute | solution.py:26
  11.6 2.2 %collective-permute-done.refs_2_ = bf16[16,3072]{1,0:T(8,128)(2,1)S(1)} collective-permute-done((bf16[16,3072]{1,0:T(8,128)(2,1)S(1)}, bf16[16,3072]{1,0:T(8,128)(2,1)S(1)}, u32[]{:S(2)}, u32[]{:S(2)}) %collective-permute-start) | collective-permute-done | bytes 98336 | tf_op jit(solution)/shard_map/ppermute | solution.py:26
  13.8 0.5 %collective-permute-start.4 = (bf16[16,3072]{1,0:T(8,128)(2,1)S(1)}, bf16[16,3072]{1,0:T(8,128)(2,1)S(1)}, u32[]{:S(2)}, u32[]{:S(2)}) collective-permute-start(bf16[16,3072]{1,0:T(8,128)(2,1)S(1)} %collective-permute-done.refs_2_), channel_id=1, source_target_pairs={{0,1},{1,0},{2,3},{3,2},{4,5},{5,4},{6,7},{7,6},{8,9},{9,8},{10,11... | collective-permute-start | bytes 294920 | tf_op jit(solution)/shard_map/ppermute | solution.py:20
  14.3 1.5 %collective-permute-start.3 = (bf16[16,3072]{1,0:T(8,128)(2,1)S(1)}, bf16[16,3072]{1,0:T(8,128)(2,1)S(1)}, u32[]{:S(2)}, u32[]{:S(2)}) collective-permute-start(bf16[16,3072]{1,0:T(8,128)(2,1)S(1)} %collective-permute-done.1.refs_3_), channel_id=1, source_target_pairs={{0,1},{1,0},{2,3},{3,2},{4,5},{5,4},{6,7},{7,6},{8,9},{9,8},{10,11... | collective-permute-start | bytes 294920 | tf_op jit(solution)/shard_map/ppermute | solution.py:20
  15.8 0.7 %collective-permute-start.2 = (bf16[16,3072]{1,0:T(8,128)(2,1)S(1)}, bf16[16,3072]{1,0:T(8,128)(2,1)S(1)}, u32[]{:S(2)}, u32[]{:S(2)}) collective-permute-start(bf16[16,3072]{1,0:T(8,128)(2,1)S(1)} %collective-permute-done.1.refs_3_), channel_id=1, source_target_pairs={{0,2},{1,3},{2,0},{3,1},{4,6},{5,7},{6,4},{7,5},{8,10},{9,11},{10,... | collective-permute-start | bytes 294920 | tf_op jit(solution)/shard_map/ppermute | solution.py:20
  16.5 1.7 %shard_map.95 = (bf16[160,4096]{1,0:T(8,128)(2,1)S(1)}, bf16[160,128]{1,0:T(8,128)(2,1)S(1)}, f32[160,64]{1,0:T(8,128)S(1)}, f32[160,64]{1,0:T(8,128)S(1)}, f32[...) custom-call(bf16[160,96]{1,0:T(8,128)(2,1)} %bitcast.21, ...), custom_call_target="tpu_custom_call" | custom-call | bytes 16777216 | tf_op jit(solution)/shard_map/pallas_call | solution.py:120
  18.2 0.0 collective-permute-done.5.refs_0_
  18.2 0.6 %shard_map.96 = (bf16[64,4096]{1,0:T(8,128)(2,1)S(1)}, bf16[160,96]{1,0:T(8,128)(2,1)S(1)}, bf16[160,96]{1,0:T(8,128)(2,1)S(1)}) custom-call(bf16[16,3072]{1,0:T(8,128)(2,1)S(1)} %collective-permute-done.5.refs_0_, bf16[16,3072]{1,0:T(8,128)(2,1)S(1)} %collective-permute-done.6.refs_1_, bf16[16,3072]{1,0:T(8,128)(2,1)S(1)} %collective-permute-done.refs_2_, ...), custom_call_target="tpu_custom_call" | custom-call | bytes 16777216 | tf_op jit(solution)/shard_map/pallas_call | solution.py:175
  18.9 0.0 collective-permute-done.7.refs_0_
  18.9 0.7 %shard_map.97 = (bf16[16,4096]{1,0:T(8,128)(2,1)S(1)}, bf16[160,96]{1,0:T(8,128)(2,1)S(1)}, bf16[160,96]{1,0:T(8,128)(2,1)S(1)}) custom-call(bf16[16,3072]{1,0:T(8,128)(2,1)S(1)} %collective-permute-done.7.refs_0_, bf16[160,4096]{1,0:T(8,128)(2,1)S(1)} %get-tuple-element.24.refs_4_.refs_1_.refs_5_, f32[160,16]{1,0:T(8,128)S(1)} %get-tuple-element.28.refs_2_, ...), custom_call_target="tpu_custom_call" | custom-call | bytes 16777216 | tf_op jit(solution)/shard_map/pallas_call | solution.py:175
  19.6 0.0 collective-permute-done.4.refs_2_
  19.6 1.0 %collective-permute-done.3.refs_1_ = bf16[16,3072]{1,0:T(8,128)(2,1)S(1)} collective-permute-done((bf16[16,3072]{1,0:T(8,128)(2,1)S(1)}, bf16[16,3072]{1,0:T(8,128)(2,1)S(1)}, u32[]{:S(2)}, u32[]{:S(2)}) %collective-permute-start.3) | collective-permute-done | bytes 98336 | tf_op jit(solution)/shard_map/ppermute | solution.py:20
  20.6 0.0 collective-permute-done.2.refs_0_
  20.6 1.7 %shard_map.98 = (bf16[160,4096]{1,0:T(8,128)(2,1)}, bf16[160,96]{1,0:T(8,128)(2,1)}, bf16[160,96]{1,0:T(8,128)(2,1)}) custom-call(bf16[16,3072]{1,0:T(8,128)(2,1)S(1)} %collective-permute-done.2.refs_0_, bf16[16,3072]{1,0:T(8,128)(2,1)S(1)} %collective-permute-done.3.refs_1_, bf16[16,3072]{1,0:T(8,128)(2,1)S(1)} %collective-permute-done.4.refs_2_, ...), custom_call_target="tpu_custom_call" | custom-call | bytes 16777216 | tf_op jit(solution)/shard_map/pallas_call | solution.py:218
Async XLA Ops:
  1.6 8.1 %collective-permute-start.6 = (bf16[16,3072]{1,0:T(8,128)(2,1)S(1)}, bf16[16,3072]{1,0:T(8,128)(2,1)S(1)}, u32[]{:S(2)}, u32[]{:S(2)}) collective-permute-start(bf16[16,3072]{1,0:T(8,128)(2,1)S(1)} %shard_map.94), channel_id=1, source_target_pairs={{0,25},{1,24},{2,27},{3,26},{4,29},{5,28},{6,31},{7,30},{8,1},{9,0... | collective-permute-start | bytes 294920 | tf_op jit(solution)/shard_map/ppermute | solution.py:26
  5.0 6.7 %collective-permute-start.1 = (bf16[16,3072]{1,0:T(8,128)(2,1)S(1)}, bf16[16,3072]{1,0:T(8,128)(2,1)S(1)}, u32[]{:S(2)}, u32[]{:S(2)}) collective-permute-start(bf16[16,3072]{1,0:T(8,128)(2,1)S(1)} %shard_map.94), channel_id=1, source_target_pairs={{0,28},{1,29},{2,30},{3,31},{4,24},{5,25},{6,26},{7,27},{8,4},{9,5... | collective-permute-start | bytes 294920 | tf_op jit(solution)/shard_map/ppermute | solution.py:26
  7.8 6.0 %collective-permute-start = (bf16[16,3072]{1,0:T(8,128)(2,1)S(1)}, bf16[16,3072]{1,0:T(8,128)(2,1)S(1)}, u32[]{:S(2)}, u32[]{:S(2)}) collective-permute-start(bf16[16,3072]{1,0:T(8,128)(2,1)S(1)} %shard_map.94), channel_id=1, source_target_pairs={{0,26},{1,27},{2,24},{3,25},{4,30},{5,31},{6,28},{7,29},{8,2},{9,3... | collective-permute-start | bytes 294920 | tf_op jit(solution)/shard_map/ppermute | solution.py:26
  8.8 9.4 %collective-permute-start.5 = (bf16[16,3072]{1,0:T(8,128)(2,1)S(1)}, bf16[16,3072]{1,0:T(8,128)(2,1)S(1)}, u32[]{:S(2)}, u32[]{:S(2)}) collective-permute-start(bf16[16,3072]{1,0:T(8,128)(2,1)S(1)} %shard_map.94), channel_id=1, source_target_pairs={{0,24},{1,25},{2,26},{3,27},{4,28},{5,29},{6,30},{7,31},{8,0},{9,1... | collective-permute-start | bytes 294920 | tf_op jit(solution)/shard_map/ppermute | solution.py:26
  9.7 9.2 %collective-permute-start.7 = (bf16[16,3072]{1,0:T(8,128)(2,1)S(1)}, bf16[16,3072]{1,0:T(8,128)(2,1)S(1)}, u32[]{:S(2)}, u32[]{:S(2)}) collective-permute-start(bf16[16,3072]{1,0:T(8,128)(2,1)S(1)} %collective-permute-done.6.refs_1_), channel_id=1, source_target_pairs={{0,6},{1,7},{2,4},{3,5},{4,2},{5,3},{6,0},{7,1},{8,14},{9,15},{10,... | collective-permute-start | bytes 294920 | tf_op jit(solution)/shard_map/ppermute | solution.py:20
  13.8 5.8 %collective-permute-start.4 = (bf16[16,3072]{1,0:T(8,128)(2,1)S(1)}, bf16[16,3072]{1,0:T(8,128)(2,1)S(1)}, u32[]{:S(2)}, u32[]{:S(2)}) collective-permute-start(bf16[16,3072]{1,0:T(8,128)(2,1)S(1)} %collective-permute-done.refs_2_), channel_id=1, source_target_pairs={{0,1},{1,0},{2,3},{3,2},{4,5},{5,4},{6,7},{7,6},{8,9},{9,8},{10,11... | collective-permute-start | bytes 294920 | tf_op jit(solution)/shard_map/ppermute | solution.py:20
  14.3 6.3 %collective-permute-start.3 = (bf16[16,3072]{1,0:T(8,128)(2,1)S(1)}, bf16[16,3072]{1,0:T(8,128)(2,1)S(1)}, u32[]{:S(2)}, u32[]{:S(2)}) collective-permute-start(bf16[16,3072]{1,0:T(8,128)(2,1)S(1)} %collective-permute-done.1.refs_3_), channel_id=1, source_target_pairs={{0,1},{1,0},{2,3},{3,2},{4,5},{5,4},{6,7},{7,6},{8,9},{9,8},{10,11... | collective-permute-start | bytes 294920 | tf_op jit(solution)/shard_map/ppermute | solution.py:20
  15.8 4.8 %collective-permute-start.2 = (bf16[16,3072]{1,0:T(8,128)(2,1)S(1)}, bf16[16,3072]{1,0:T(8,128)(2,1)S(1)}, u32[]{:S(2)}, u32[]{:S(2)}) collective-permute-start(bf16[16,3072]{1,0:T(8,128)(2,1)S(1)} %collective-permute-done.1.refs_3_), channel_id=1, source_target_pairs={{0,2},{1,3},{2,0},{3,1},{4,6},{5,7},{6,4},{7,5},{8,10},{9,11},{10,... | collective-permute-start | bytes 294920 | tf_op jit(solution)/shard_map/ppermute | solution.py:20

commit v5 on v4

--- a/solution.py
+++ b/solution.py
@@ -234,17 +234,13 @@
     n = lax.axis_size("tp")
     count = grad_held.shape[1]
     p = pack(grad_held[0])
-    first = [f for f in range(n) if f & (f - 1) == 0]
-    rest = [f for f in range(n) if f not in first]
-    groups = [first, [n - 1], rest[-2::-1]] if len(rest) > 1 else [first, rest]
+    groups = [[f for f in range(n) if f & (f - 1) == 0 or f == 3], [f for f in range(n - 2, 4, -1) if f & (f - 1)] + [n - 1]]
     got = {}
-    for flip in reversed(first):
+    for flip in reversed(groups[0]):
         got[flip] = send(p, flip, 1)
-    for flip, tied in zip(first[2:], lax.optimization_barrier([got[f] for f in first[2:]])):
-        got[flip] = tied
-    for flip in reversed(rest):
+    for flip in reversed(groups[1]):
         step = flip & -flip
-        if flip & 1 and flip - 1 not in first:
+        if flip & 1 and flip - 1 & flip - 2:
             step = flip - 1
         got[flip] = send(got[flip - step], step, 0)
     weight, hidden, factors = prepare(
@@ -293,7 +289,7 @@
     n = lax.axis_size("tp")
     count, width = operands[-1].shape[1:]
     free = TILE - count
-    small = n & (n - 1) == 0 and 4 <= n <= TILE
+    small = n & (n - 1) == 0 and 8 <= n <= TILE
     fits = 0 < free < TILE and count % free == 0 and width * free % (TILE * 128) == 0 and width % (4 * 128) == 0
     return fanned(*operands) if small and fits else ringed(*operands)
 

time: 22.5 us -> 22.3 us (level)
  Pallas kernels: 5.62 us -> 4.97 us
  starting transfers between devices: 11.9 us -> 12.4 us
    ppermute x4 -> x3, waiting for transfers between devices: 1.06 us -> 2.65 us  [send(): return lax.ppermute(array, 'tp', [(t, t ^ flip) for t in range(count)])]
    ppermute x4 -> x5, waiting for transfers between devices: 3.02 us -> 1.46 us  [send(): return lax.ppermute(array, ('section', 'tp'), pairs)]
    ppermute x4 -> x5, starting transfers between devices: 8.09 us -> 8.85 us  [send(): return lax.ppermute(array, ('section', 'tp'), pairs)]
    pallas_call x2 -> x1, Pallas kernels: 1.3 us -> 0.65 us  [stage(): pl.pallas_call(functools.partial(stage_kernel, group, count, len(before)...]
    ppermute x4 -> x3, starting transfers between devices: 3.85 us -> 3.53 us  [send(): return lax.ppermute(array, 'tp', [(t, t ^ flip) for t in range(count)])]
  transfers between devices with their start and end apart: 8 -> 8, of which waited for: 3 -> 3; matrix products, arithmetic and copies ran while one was open for 0% -> 0% of each run, Pallas kernels for 13% -> 11%
where the time goes in v5:
time: 22.3 us; the launch traced here: 22.1 us
  starting transfers between devices  12.4 us (56%)
  Pallas kernels  4.97 us (22%)
  waiting for transfers between devices  4.11 us (18%)
  between operations  0.68 us (3%)
    ppermute x5, starting transfers between devices, send(): return lax.ppermute(array, ('section', 'tp'), pairs)  8.85 us
    ppermute x3, starting transfers between devices, send(): return lax.ppermute(array, 'tp', [(t, t ^ flip) for t in range(count)])  3.53 us
    ppermute x3, waiting for transfers between devices, send(): return lax.ppermute(array, 'tp', [(t, t ^ flip) for t in range(count)])  2.65 us
    pallas_call x1, Pallas kernels, last(): pl.pallas_call(functools.partial(last_kernel, len(slots) + len(earlier),...  1.7 us
    pallas_call x1, Pallas kernels, prepare(): pl.pallas_call(functools.partial(prepare_kernel, groups, count), out_shap...  1.69 us
    ppermute x5, waiting for transfers between devices, send(): return lax.ppermute(array, ('section', 'tp'), pairs)  1.46 us
    pallas_call x1, Pallas kernels, pack(): pl.pallas_call(pack_kernel, out_shape=pltpu.VMEM((TILE, width * count //...  0.93 us
    pallas_call x1, Pallas kernels, stage(): pl.pallas_call(functools.partial(stage_kernel, group, count, len(before)...  0.65 us
  transfers between devices with their start and end apart: 8, of which 3 were waited for; matrix products, arithmetic and copies ran while one was open for 0% of the time, Pallas kernels for 11%

profile of v5, /device:TPU:0, one launch (start us, length us, event | category | flops | bytes accessed | tf_op | source)
XLA Modules:
  0.0 22.1 jit_solution(8661586788973323251)
XLA Ops:
  0.6 0.9 %shard_map.94 = bf16[16,3072]{1,0:T(8,128)(2,1)S(1)} custom-call(bf16[12,4096]{1,0:T(8,128)(2,1)} %bitcast.19), custom_call_target="tpu_custom_call" | custom-call | tf_op jit(solution)/shard_map/pallas_call | solution.py:52
  1.6 3.4 %collective-permute-start.3 = (bf16[16,3072]{1,0:T(8,128)(2,1)S(1)}, bf16[16,3072]{1,0:T(8,128)(2,1)S(1)}, u32[]{:S(2)}, u32[]{:S(2)}) collective-permute-start(bf16[16,3072]{1,0:T(8,128)(2,1)S(1)} %shard_map.94), channel_id=1, source_target_pairs={{0,25},{1,24},{2,27},{3,26},{4,29},{5,28},{6,31},{7,30},{8,1},{9,0... | collective-permute-start | bytes 294920 | tf_op jit(solution)/shard_map/ppermute | solution.py:26
  5.0 2.9 %collective-permute-start = (bf16[16,3072]{1,0:T(8,128)(2,1)S(1)}, bf16[16,3072]{1,0:T(8,128)(2,1)S(1)}, u32[]{:S(2)}, u32[]{:S(2)}) collective-permute-start(bf16[16,3072]{1,0:T(8,128)(2,1)S(1)} %shard_map.94), channel_id=1, source_target_pairs={{0,28},{1,29},{2,30},{3,31},{4,24},{5,25},{6,26},{7,27},{8,4},{9,5... | collective-permute-start | bytes 294920 | tf_op jit(solution)/shard_map/ppermute | solution.py:26
  7.8 1.1 %collective-permute-start.7 = (bf16[16,3072]{1,0:T(8,128)(2,1)S(1)}, bf16[16,3072]{1,0:T(8,128)(2,1)S(1)}, u32[]{:S(2)}, u32[]{:S(2)}) collective-permute-start(bf16[16,3072]{1,0:T(8,128)(2,1)S(1)} %shard_map.94), channel_id=1, source_target_pairs={{0,27},{1,26},{2,25},{3,24},{4,31},{5,30},{6,29},{7,28},{8,3},{9,2... | collective-permute-start | bytes 294920 | tf_op jit(solution)/shard_map/ppermute | solution.py:26
  8.9 0.6 %collective-permute-start.6 = (bf16[16,3072]{1,0:T(8,128)(2,1)S(1)}, bf16[16,3072]{1,0:T(8,128)(2,1)S(1)}, u32[]{:S(2)}, u32[]{:S(2)}) collective-permute-start(bf16[16,3072]{1,0:T(8,128)(2,1)S(1)} %shard_map.94), channel_id=1, source_target_pairs={{0,26},{1,27},{2,24},{3,25},{4,30},{5,31},{6,28},{7,29},{8,2},{9,3... | collective-permute-start | bytes 294920 | tf_op jit(solution)/shard_map/ppermute | solution.py:26
  9.5 0.9 %collective-permute-start.5 = (bf16[16,3072]{1,0:T(8,128)(2,1)S(1)}, bf16[16,3072]{1,0:T(8,128)(2,1)S(1)}, u32[]{:S(2)}, u32[]{:S(2)}) collective-permute-start(bf16[16,3072]{1,0:T(8,128)(2,1)S(1)} %shard_map.94), channel_id=1, source_target_pairs={{0,24},{1,25},{2,26},{3,27},{4,28},{5,29},{6,30},{7,31},{8,0},{9,1... | collective-permute-start | bytes 294920 | tf_op jit(solution)/shard_map/ppermute | solution.py:26
  10.4 0.0 collective-permute-done.3.refs_1_
  10.4 1.3 %collective-permute-start.4 = (bf16[16,3072]{1,0:T(8,128)(2,1)S(1)}, bf16[16,3072]{1,0:T(8,128)(2,1)S(1)}, u32[]{:S(2)}, u32[]{:S(2)}) collective-permute-start(bf16[16,3072]{1,0:T(8,128)(2,1)S(1)} %collective-permute-done.3.refs_1_), channel_id=1, source_target_pairs={{0,6},{1,7},{2,4},{3,5},{4,2},{5,3},{6,0},{7,1},{8,14},{9,15},{10,... | collective-permute-start | bytes 294920 | tf_op jit(solution)/shard_map/ppermute | solution.py:20
  11.8 0.0 collective-permute-done.refs_4_
  11.8 1.5 %collective-permute-start.2 = (bf16[16,3072]{1,0:T(8,128)(2,1)S(1)}, bf16[16,3072]{1,0:T(8,128)(2,1)S(1)}, u32[]{:S(2)}, u32[]{:S(2)}) collective-permute-start(bf16[16,3072]{1,0:T(8,128)(2,1)S(1)} %collective-permute-done.refs_4_), channel_id=1, source_target_pairs={{0,1},{1,0},{2,3},{3,2},{4,5},{5,4},{6,7},{7,6},{8,9},{9,8},{10,11... | collective-permute-start | bytes 294920 | tf_op jit(solution)/shard_map/ppermute | solution.py:20
  13.3 1.4 %collective-permute-done.7.refs_3_ = bf16[16,3072]{1,0:T(8,128)(2,1)S(1)} collective-permute-done((bf16[16,3072]{1,0:T(8,128)(2,1)S(1)}, bf16[16,3072]{1,0:T(8,128)(2,1)S(1)}, u32[]{:S(2)}, u32[]{:S(2)}) %collective-permute-start.7) | collective-permute-done | bytes 98336 | tf_op jit(solution)/shard_map/ppermute | solution.py:26
  14.7 0.7 %collective-permute-start.1 = (bf16[16,3072]{1,0:T(8,128)(2,1)S(1)}, bf16[16,3072]{1,0:T(8,128)(2,1)S(1)}, u32[]{:S(2)}, u32[]{:S(2)}) collective-permute-start(bf16[16,3072]{1,0:T(8,128)(2,1)S(1)} %collective-permute-done.refs_4_), channel_id=1, source_target_pairs={{0,2},{1,3},{2,0},{3,1},{4,6},{5,7},{6,4},{7,5},{8,10},{9,11},{10,... | collective-permute-start | bytes 294920 | tf_op jit(solution)/shard_map/ppermute | solution.py:20
  15.4 1.7 %shard_map.95 = (bf16[160,4096]{1,0:T(8,128)(2,1)S(1)}, bf16[160,128]{1,0:T(8,128)(2,1)S(1)}, f32[160,80]{1,0:T(8,128)S(1)}, f32[160,80]{1,0:T(8,128)S(1)}, f32[...) custom-call(bf16[160,96]{1,0:T(8,128)(2,1)} %bitcast.21, s32[5,1,96]{2,1,0:T(1,128)} %bitcast.23, bf16[160,96]{1,0:T(8,128)(2,1)} %bitcast.22, ...), custom_call_target="tpu_custom_call" | custom-call | bytes 16777216 | tf_op jit(solution)/shard_map/pallas_call | solution.py:120
  17.1 0.0 collective-permute-done.6.refs_2_
  17.1 0.0 collective-permute-done.5.refs_0_
  17.1 0.7 %shard_map.96 = (bf16[80,4096]{1,0:T(8,128)(2,1)S(1)}, bf16[160,96]{1,0:T(8,128)(2,1)S(1)}, bf16[160,96]{1,0:T(8,128)(2,1)S(1)}) custom-call(bf16[16,3072]{1,0:T(8,128)(2,1)S(1)} %collective-permute-done.5.refs_0_, bf16[16,3072]{1,0:T(8,128)(2,1)S(1)} %collective-permute-done.3.refs_1_, bf16[16,3072]{1,0:T(8,128)(2,1)S(1)} %collective-permute-done.6.refs_2_, ...), custom_call_target="tpu_custom_call" | custom-call | bytes 16777216 | tf_op jit(solution)/shard_map/pallas_call | solution.py:175
  17.8 0.6 %collective-permute-done.4.refs_2_ = bf16[16,3072]{1,0:T(8,128)(2,1)S(1)} collective-permute-done((bf16[16,3072]{1,0:T(8,128)(2,1)S(1)}, bf16[16,3072]{1,0:T(8,128)(2,1)S(1)}, u32[]{:S(2)}, u32[]{:S(2)}) %collective-permute-start.4) | collective-permute-done | bytes 98336 | tf_op jit(solution)/shard_map/ppermute | solution.py:20
  18.4 0.0 collective-permute-done.2.refs_1_
  18.4 2.0 %collective-permute-done.1.refs_0_ = bf16[16,3072]{1,0:T(8,128)(2,1)S(1)} collective-permute-done((bf16[16,3072]{1,0:T(8,128)(2,1)S(1)}, bf16[16,3072]{1,0:T(8,128)(2,1)S(1)}, u32[]{:S(2)}, u32[]{:S(2)}) %collective-permute-start.1) | collective-permute-done | bytes 98336 | tf_op jit(solution)/shard_map/ppermute | solution.py:20
  20.4 1.7 %shard_map.97 = (bf16[160,4096]{1,0:T(8,128)(2,1)}, bf16[160,96]{1,0:T(8,128)(2,1)}, bf16[160,96]{1,0:T(8,128)(2,1)}) custom-call(bf16[16,3072]{1,0:T(8,128)(2,1)S(1)} %collective-permute-done.1.refs_0_, bf16[16,3072]{1,0:T(8,128)(2,1)S(1)} %collective-permute-done.2.refs_1_, bf16[16,3072]{1,0:T(8,128)(2,1)S(1)} %collective-permute-done.4.refs_2_, ...), custom_call_target="tpu_custom_call" | custom-call | bytes 16777216 | tf_op jit(solution)/shard_map/pallas_call | solution.py:218
Async XLA Ops:
  1.6 8.9 %collective-permute-start.3 = (bf16[16,3072]{1,0:T(8,128)(2,1)S(1)}, bf16[16,3072]{1,0:T(8,128)(2,1)S(1)}, u32[]{:S(2)}, u32[]{:S(2)}) collective-permute-start(bf16[16,3072]{1,0:T(8,128)(2,1)S(1)} %shard_map.94), channel_id=1, source_target_pairs={{0,25},{1,24},{2,27},{3,26},{4,29},{5,28},{6,31},{7,30},{8,1},{9,0... | collective-permute-start | bytes 294920 | tf_op jit(solution)/shard_map/ppermute | solution.py:26
  5.0 6.8 %collective-permute-start = (bf16[16,3072]{1,0:T(8,128)(2,1)S(1)}, bf16[16,3072]{1,0:T(8,128)(2,1)S(1)}, u32[]{:S(2)}, u32[]{:S(2)}) collective-permute-start(bf16[16,3072]{1,0:T(8,128)(2,1)S(1)} %shard_map.94), channel_id=1, source_target_pairs={{0,28},{1,29},{2,30},{3,31},{4,24},{5,25},{6,26},{7,27},{8,4},{9,5... | collective-permute-start | bytes 294920 | tf_op jit(solution)/shard_map/ppermute | solution.py:26
  7.8 6.9 %collective-permute-start.7 = (bf16[16,3072]{1,0:T(8,128)(2,1)S(1)}, bf16[16,3072]{1,0:T(8,128)(2,1)S(1)}, u32[]{:S(2)}, u32[]{:S(2)}) collective-permute-start(bf16[16,3072]{1,0:T(8,128)(2,1)S(1)} %shard_map.94), channel_id=1, source_target_pairs={{0,27},{1,26},{2,25},{3,24},{4,31},{5,30},{6,29},{7,28},{8,3},{9,2... | collective-permute-start | bytes 294920 | tf_op jit(solution)/shard_map/ppermute | solution.py:26
  8.9 8.2 %collective-permute-start.6 = (bf16[16,3072]{1,0:T(8,128)(2,1)S(1)}, bf16[16,3072]{1,0:T(8,128)(2,1)S(1)}, u32[]{:S(2)}, u32[]{:S(2)}) collective-permute-start(bf16[16,3072]{1,0:T(8,128)(2,1)S(1)} %shard_map.94), channel_id=1, source_target_pairs={{0,26},{1,27},{2,24},{3,25},{4,30},{5,31},{6,28},{7,29},{8,2},{9,3... | collective-permute-start | bytes 294920 | tf_op jit(solution)/shard_map/ppermute | solution.py:26
  9.5 7.6 %collective-permute-start.5 = (bf16[16,3072]{1,0:T(8,128)(2,1)S(1)}, bf16[16,3072]{1,0:T(8,128)(2,1)S(1)}, u32[]{:S(2)}, u32[]{:S(2)}) collective-permute-start(bf16[16,3072]{1,0:T(8,128)(2,1)S(1)} %shard_map.94), channel_id=1, source_target_pairs={{0,24},{1,25},{2,26},{3,27},{4,28},{5,29},{6,30},{7,31},{8,0},{9,1... | collective-permute-start | bytes 294920 | tf_op jit(solution)/shard_map/ppermute | solution.py:26
  10.4 8.0 %collective-permute-start.4 = (bf16[16,3072]{1,0:T(8,128)(2,1)S(1)}, bf16[16,3072]{1,0:T(8,128)(2,1)S(1)}, u32[]{:S(2)}, u32[]{:S(2)}) collective-permute-start(bf16[16,3072]{1,0:T(8,128)(2,1)S(1)} %collective-permute-done.3.refs_1_), channel_id=1, source_target_pairs={{0,6},{1,7},{2,4},{3,5},{4,2},{5,3},{6,0},{7,1},{8,14},{9,15},{10,... | collective-permute-start | bytes 294920 | tf_op jit(solution)/shard_map/ppermute | solution.py:20
  11.8 6.6 %collective-permute-start.2 = (bf16[16,3072]{1,0:T(8,128)(2,1)S(1)}, bf16[16,3072]{1,0:T(8,128)(2,1)S(1)}, u32[]{:S(2)}, u32[]{:S(2)}) collective-permute-start(bf16[16,3072]{1,0:T(8,128)(2,1)S(1)} %collective-permute-done.refs_4_), channel_id=1, source_target_pairs={{0,1},{1,0},{2,3},{3,2},{4,5},{5,4},{6,7},{7,6},{8,9},{9,8},{10,11... | collective-permute-start | bytes 294920 | tf_op jit(solution)/shard_map/ppermute | solution.py:20
  14.7 5.7 %collective-permute-start.1 = (bf16[16,3072]{1,0:T(8,128)(2,1)S(1)}, bf16[16,3072]{1,0:T(8,128)(2,1)S(1)}, u32[]{:S(2)}, u32[]{:S(2)}) collective-permute-start(bf16[16,3072]{1,0:T(8,128)(2,1)S(1)} %collective-permute-done.refs_4_), channel_id=1, source_target_pairs={{0,2},{1,3},{2,0},{3,1},{4,6},{5,7},{6,4},{7,5},{8,10},{9,11},{10,... | collective-permute-start | bytes 294920 | tf_op jit(solution)/shard_map/ppermute | solution.py:20

commit v6 on v5

--- a/solution.py
+++ b/solution.py
@@ -234,7 +234,7 @@
     n = lax.axis_size("tp")
     count = grad_held.shape[1]
     p = pack(grad_held[0])
-    groups = [[f for f in range(n) if f & (f - 1) == 0 or f == 3], [f for f in range(n - 2, 4, -1) if f & (f - 1)] + [n - 1]]
+    groups = [[f for f in range(1, n // 2) if f & (f - 1) == 0 or f == 3] + [0, n // 2], [f for f in range(5, n) if f & (f - 1)]]
     got = {}
     for flip in reversed(groups[0]):
         got[flip] = send(p, flip, 1)

time: 22.3 us -> 22.2 us (level)
  waiting for transfers between devices: 4.11 us -> 3.57 us
  starting transfers between devices: 12.4 us -> 12.8 us
    ppermute x5, waiting for transfers between devices: 1.46 us -> 0.01 us  [send(): return lax.ppermute(array, ('section', 'tp'), pairs)]
    ppermute x3, waiting for transfers between devices: 2.65 us -> 3.56 us  [send(): return lax.ppermute(array, 'tp', [(t, t ^ flip) for t in range(count)])]
    ppermute x3, starting transfers between devices: 3.53 us -> 3.94 us  [send(): return lax.ppermute(array, 'tp', [(t, t ^ flip) for t in range(count)])]
  transfers between devices with their start and end apart: 8 -> 8, of which waited for: 3 -> 2; matrix products, arithmetic and copies ran while one was open for 0% -> 0% of each run, Pallas kernels for 11% -> 11%
where the time goes in v6:
time: 22.2 us; the launch traced here: 22 us
  starting transfers between devices  12.8 us (58%)
  Pallas kernels  4.97 us (22%)
  waiting for transfers between devices  3.57 us (16%)
  between operations  0.68 us (3%)
    ppermute x5, starting transfers between devices, send(): return lax.ppermute(array, ('section', 'tp'), pairs)  8.85 us
    ppermute x3, starting transfers between devices, send(): return lax.ppermute(array, 'tp', [(t, t ^ flip) for t in range(count)])  3.94 us
    ppermute x3, waiting for transfers between devices, send(): return lax.ppermute(array, 'tp', [(t, t ^ flip) for t in range(count)])  3.56 us
    pallas_call x1, Pallas kernels, last(): pl.pallas_call(functools.partial(last_kernel, len(slots) + len(earlier),...  1.7 us
    pallas_call x1, Pallas kernels, prepare(): pl.pallas_call(functools.partial(prepare_kernel, groups, count), out_shap...  1.69 us
    pallas_call x1, Pallas kernels, pack(): pl.pallas_call(pack_kernel, out_shape=pltpu.VMEM((TILE, width * count //...  0.93 us
    pallas_call x1, Pallas kernels, stage(): pl.pallas_call(functools.partial(stage_kernel, group, count, len(before)...  0.65 us
  transfers between devices with their start and end apart: 8, of which 2 were waited for; matrix products, arithmetic and copies ran while one was open for 0% of the time, Pallas kernels for 11%

profile of v6, /device:TPU:0, one launch (start us, length us, event | category | flops | bytes accessed | tf_op | source)
XLA Modules:
  0.0 22.0 jit_solution(4786345013991015912)
XLA Ops:
  0.6 0.9 %shard_map.94 = bf16[16,3072]{1,0:T(8,128)(2,1)S(1)} custom-call(bf16[12,4096]{1,0:T(8,128)(2,1)} %bitcast.19), custom_call_target="tpu_custom_call" | custom-call | tf_op jit(solution)/shard_map/pallas_call | solution.py:52
  1.6 3.4 %collective-permute-start.3 = (bf16[16,3072]{1,0:T(8,128)(2,1)S(1)}, bf16[16,3072]{1,0:T(8,128)(2,1)S(1)}, u32[]{:S(2)}, u32[]{:S(2)}) collective-permute-start(bf16[16,3072]{1,0:T(8,128)(2,1)S(1)} %shard_map.94), channel_id=1, source_target_pairs={{0,25},{1,24},{2,27},{3,26},{4,29},{5,28},{6,31},{7,30},{8,1},{9,0... | collective-permute-start | bytes 294920 | tf_op jit(solution)/shard_map/ppermute | solution.py:26
  5.0 2.9 %collective-permute-start = (bf16[16,3072]{1,0:T(8,128)(2,1)S(1)}, bf16[16,3072]{1,0:T(8,128)(2,1)S(1)}, u32[]{:S(2)}, u32[]{:S(2)}) collective-permute-start(bf16[16,3072]{1,0:T(8,128)(2,1)S(1)} %shard_map.94), channel_id=1, source_target_pairs={{0,28},{1,29},{2,30},{3,31},{4,24},{5,25},{6,26},{7,27},{8,4},{9,5... | collective-permute-start | bytes 294920 | tf_op jit(solution)/shard_map/ppermute | solution.py:26
  7.8 0.0 collective-permute-start.7
  7.8 1.6 %collective-permute-start.6 = (bf16[16,3072]{1,0:T(8,128)(2,1)S(1)}, bf16[16,3072]{1,0:T(8,128)(2,1)S(1)}, u32[]{:S(2)}, u32[]{:S(2)}) collective-permute-start(bf16[16,3072]{1,0:T(8,128)(2,1)S(1)} %shard_map.94), channel_id=1, source_target_pairs={{0,27},{1,26},{2,25},{3,24},{4,31},{5,30},{6,29},{7,28},{8,3},{9,2... | collective-permute-start | bytes 294920 | tf_op jit(solution)/shard_map/ppermute | solution.py:26
  9.4 1.0 %collective-permute-start.5 = (bf16[16,3072]{1,0:T(8,128)(2,1)S(1)}, bf16[16,3072]{1,0:T(8,128)(2,1)S(1)}, u32[]{:S(2)}, u32[]{:S(2)}) collective-permute-start(bf16[16,3072]{1,0:T(8,128)(2,1)S(1)} %shard_map.94), channel_id=1, source_target_pairs={{0,26},{1,27},{2,24},{3,25},{4,30},{5,31},{6,28},{7,29},{8,2},{9,3... | collective-permute-start | bytes 294920 | tf_op jit(solution)/shard_map/ppermute | solution.py:26
  10.4 0.0 collective-permute-done.3.refs_0_
  10.4 1.3 %collective-permute-start.4 = (bf16[16,3072]{1,0:T(8,128)(2,1)S(1)}, bf16[16,3072]{1,0:T(8,128)(2,1)S(1)}, u32[]{:S(2)}, u32[]{:S(2)}) collective-permute-start(bf16[16,3072]{1,0:T(8,128)(2,1)S(1)} %collective-permute-done.3.refs_0_), channel_id=1, source_target_pairs={{0,6},{1,7},{2,4},{3,5},{4,2},{5,3},{6,0},{7,1},{8,14},{9,15},{10,... | collective-permute-start | bytes 294920 | tf_op jit(solution)/shard_map/ppermute | solution.py:20
  11.8 0.0 collective-permute-done.refs_4_
  11.8 2.1 %collective-permute-start.2 = (bf16[16,3072]{1,0:T(8,128)(2,1)S(1)}, bf16[16,3072]{1,0:T(8,128)(2,1)S(1)}, u32[]{:S(2)}, u32[]{:S(2)}) collective-permute-start(bf16[16,3072]{1,0:T(8,128)(2,1)S(1)} %collective-permute-done.refs_4_), channel_id=1, source_target_pairs={{0,2},{1,3},{2,0},{3,1},{4,6},{5,7},{6,4},{7,5},{8,10},{9,11},{10,... | collective-permute-start | bytes 294920 | tf_op jit(solution)/shard_map/ppermute | solution.py:20
  13.9 0.0 collective-permute-done.7.refs_3_
  13.9 0.5 %collective-permute-start.1 = (bf16[16,3072]{1,0:T(8,128)(2,1)S(1)}, bf16[16,3072]{1,0:T(8,128)(2,1)S(1)}, u32[]{:S(2)}, u32[]{:S(2)}) collective-permute-start(bf16[16,3072]{1,0:T(8,128)(2,1)S(1)} %collective-permute-done.refs_4_), channel_id=1, source_target_pairs={{0,1},{1,0},{2,3},{3,2},{4,5},{5,4},{6,7},{7,6},{8,9},{9,8},{10,11... | collective-permute-start | bytes 294920 | tf_op jit(solution)/shard_map/ppermute | solution.py:20
  14.4 1.7 %shard_map.95 = (bf16[160,4096]{1,0:T(8,128)(2,1)S(1)}, bf16[160,128]{1,0:T(8,128)(2,1)S(1)}, f32[160,80]{1,0:T(8,128)S(1)}, f32[160,80]{1,0:T(8,128)S(1)}, f32[...) custom-call(bf16[160,96]{1,0:T(8,128)(2,1)} %bitcast.21, s32[5,1,96]{2,1,0:T(1,128)} %bitcast.23, bf16[160,96]{1,0:T(8,128)(2,1)} %bitcast.22, ...), custom_call_target="tpu_custom_call" | custom-call | bytes 16777216 | tf_op jit(solution)/shard_map/pallas_call | solution.py:120
  16.1 0.0 collective-permute-done.6.refs_2_
  16.1 0.0 collective-permute-done.5.refs_1_
  16.1 0.7 %shard_map.96 = (bf16[80,4096]{1,0:T(8,128)(2,1)S(1)}, bf16[160,96]{1,0:T(8,128)(2,1)S(1)}, bf16[160,96]{1,0:T(8,128)(2,1)S(1)}) custom-call(bf16[16,3072]{1,0:T(8,128)(2,1)S(1)} %collective-permute-done.3.refs_0_, bf16[16,3072]{1,0:T(8,128)(2,1)S(1)} %collective-permute-done.5.refs_1_, bf16[16,3072]{1,0:T(8,128)(2,1)S(1)} %collective-permute-done.6.refs_2_, ...), custom_call_target="tpu_custom_call" | custom-call | bytes 16777216 | tf_op jit(solution)/shard_map/pallas_call | solution.py:175
  16.7 2.4 %collective-permute-done.4.refs_2_ = bf16[16,3072]{1,0:T(8,128)(2,1)S(1)} collective-permute-done((bf16[16,3072]{1,0:T(8,128)(2,1)S(1)}, bf16[16,3072]{1,0:T(8,128)(2,1)S(1)}, u32[]{:S(2)}, u32[]{:S(2)}) %collective-permute-start.4) | collective-permute-done | bytes 98336 | tf_op jit(solution)/shard_map/ppermute | solution.py:20
  19.2 1.1 %collective-permute-done.2.refs_1_ = bf16[16,3072]{1,0:T(8,128)(2,1)S(1)} collective-permute-done((bf16[16,3072]{1,0:T(8,128)(2,1)S(1)}, bf16[16,3072]{1,0:T(8,128)(2,1)S(1)}, u32[]{:S(2)}, u32[]{:S(2)}) %collective-permute-start.2) | collective-permute-done | bytes 98336 | tf_op jit(solution)/shard_map/ppermute | solution.py:20
  20.3 0.0 collective-permute-done.1.refs_0_
  20.3 1.7 %shard_map.97 = (bf16[160,4096]{1,0:T(8,128)(2,1)}, bf16[160,96]{1,0:T(8,128)(2,1)}, bf16[160,96]{1,0:T(8,128)(2,1)}) custom-call(bf16[16,3072]{1,0:T(8,128)(2,1)S(1)} %collective-permute-done.1.refs_0_, bf16[16,3072]{1,0:T(8,128)(2,1)S(1)} %collective-permute-done.2.refs_1_, bf16[16,3072]{1,0:T(8,128)(2,1)S(1)} %collective-permute-done.4.refs_2_, ...), custom_call_target="tpu_custom_call" | custom-call | bytes 16777216 | tf_op jit(solution)/shard_map/pallas_call | solution.py:218
Async XLA Ops:
  1.6 8.9 %collective-permute-start.3 = (bf16[16,3072]{1,0:T(8,128)(2,1)S(1)}, bf16[16,3072]{1,0:T(8,128)(2,1)S(1)}, u32[]{:S(2)}, u32[]{:S(2)}) collective-permute-start(bf16[16,3072]{1,0:T(8,128)(2,1)S(1)} %shard_map.94), channel_id=1, source_target_pairs={{0,25},{1,24},{2,27},{3,26},{4,29},{5,28},{6,31},{7,30},{8,1},{9,0... | collective-permute-start | bytes 294920 | tf_op jit(solution)/shard_map/ppermute | solution.py:26
  5.0 6.8 %collective-permute-start = (bf16[16,3072]{1,0:T(8,128)(2,1)S(1)}, bf16[16,3072]{1,0:T(8,128)(2,1)S(1)}, u32[]{:S(2)}, u32[]{:S(2)}) collective-permute-start(bf16[16,3072]{1,0:T(8,128)(2,1)S(1)} %shard_map.94), channel_id=1, source_target_pairs={{0,28},{1,29},{2,30},{3,31},{4,24},{5,25},{6,26},{7,27},{8,4},{9,5... | collective-permute-start | bytes 294920 | tf_op jit(solution)/shard_map/ppermute | solution.py:26
  7.8 6.0 %collective-permute-start.7 = (bf16[16,3072]{1,0:T(8,128)(2,1)S(1)}, bf16[16,3072]{1,0:T(8,128)(2,1)S(1)}, u32[]{:S(2)}, u32[]{:S(2)}) collective-permute-start(bf16[16,3072]{1,0:T(8,128)(2,1)S(1)} %shard_map.94), channel_id=1, source_target_pairs={{0,24},{1,25},{2,26},{3,27},{4,28},{5,29},{6,30},{7,31},{8,0},{9,1... | collective-permute-start | bytes 294920 | tf_op jit(solution)/shard_map/ppermute | solution.py:26
  7.8 8.2 %collective-permute-start.6 = (bf16[16,3072]{1,0:T(8,128)(2,1)S(1)}, bf16[16,3072]{1,0:T(8,128)(2,1)S(1)}, u32[]{:S(2)}, u32[]{:S(2)}) collective-permute-start(bf16[16,3072]{1,0:T(8,128)(2,1)S(1)} %shard_map.94), channel_id=1, source_target_pairs={{0,27},{1,26},{2,25},{3,24},{4,31},{5,30},{6,29},{7,28},{8,3},{9,2... | collective-permute-start | bytes 294920 | tf_op jit(solution)/shard_map/ppermute | solution.py:26
  9.4 6.6 %collective-permute-start.5 = (bf16[16,3072]{1,0:T(8,128)(2,1)S(1)}, bf16[16,3072]{1,0:T(8,128)(2,1)S(1)}, u32[]{:S(2)}, u32[]{:S(2)}) collective-permute-start(bf16[16,3072]{1,0:T(8,128)(2,1)S(1)} %shard_map.94), channel_id=1, source_target_pairs={{0,26},{1,27},{2,24},{3,25},{4,30},{5,31},{6,28},{7,29},{8,2},{9,3... | collective-permute-start | bytes 294920 | tf_op jit(solution)/shard_map/ppermute | solution.py:26
  10.4 8.7 %collective-permute-start.4 = (bf16[16,3072]{1,0:T(8,128)(2,1)S(1)}, bf16[16,3072]{1,0:T(8,128)(2,1)S(1)}, u32[]{:S(2)}, u32[]{:S(2)}) collective-permute-start(bf16[16,3072]{1,0:T(8,128)(2,1)S(1)} %collective-permute-done.3.refs_0_), channel_id=1, source_target_pairs={{0,6},{1,7},{2,4},{3,5},{4,2},{5,3},{6,0},{7,1},{8,14},{9,15},{10,... | collective-permute-start | bytes 294920 | tf_op jit(solution)/shard_map/ppermute | solution.py:20
  11.8 8.5 %collective-permute-start.2 = (bf16[16,3072]{1,0:T(8,128)(2,1)S(1)}, bf16[16,3072]{1,0:T(8,128)(2,1)S(1)}, u32[]{:S(2)}, u32[]{:S(2)}) collective-permute-start(bf16[16,3072]{1,0:T(8,128)(2,1)S(1)} %collective-permute-done.refs_4_), channel_id=1, source_target_pairs={{0,2},{1,3},{2,0},{3,1},{4,6},{5,7},{6,4},{7,5},{8,10},{9,11},{10,... | collective-permute-start | bytes 294920 | tf_op jit(solution)/shard_map/ppermute | solution.py:20
  13.9 6.4 %collective-permute-start.1 = (bf16[16,3072]{1,0:T(8,128)(2,1)S(1)}, bf16[16,3072]{1,0:T(8,128)(2,1)S(1)}, u32[]{:S(2)}, u32[]{:S(2)}) collective-permute-start(bf16[16,3072]{1,0:T(8,128)(2,1)S(1)} %collective-permute-done.refs_4_), channel_id=1, source_target_pairs={{0,1},{1,0},{2,3},{3,2},{4,5},{5,4},{6,7},{7,6},{8,9},{9,8},{10,11... | collective-permute-start | bytes 294920 | tf_op jit(solution)/shard_map/ppermute | solution.py:20

commit v7 on v4

--- a/solution.py
+++ b/solution.py
@@ -236,12 +236,11 @@
     p = pack(grad_held[0])
     first = [f for f in range(n) if f & (f - 1) == 0]
     rest = [f for f in range(n) if f not in first]
-    groups = [first, [n - 1], rest[-2::-1]] if len(rest) > 1 else [first, rest]
+    late = [f for f in rest if f - n // 2 in first]
+    groups = [first, [f for f in rest[:-1] if f not in late] + late[::-1] + rest[-1:]]
     got = {}
     for flip in reversed(first):
         got[flip] = send(p, flip, 1)
-    for flip, tied in zip(first[2:], lax.optimization_barrier([got[f] for f in first[2:]])):
-        got[flip] = tied
     for flip in reversed(rest):
         step = flip & -flip
         if flip & 1 and flip - 1 not in first:

time: 22.5 us -> 21.2 us (0.942)
  waiting for transfers between devices: 4.07 us -> 1.98 us
  starting transfers between devices: 11.9 us -> 13.5 us
  Pallas kernels: 5.62 us -> 4.97 us
    ppermute x4, waiting for transfers between devices: 3.02 us -> 0.84 us  [send(): return lax.ppermute(array, ('section', 'tp'), pairs)]
    ppermute x4, starting transfers between devices: 3.85 us -> 5.36 us  [send(): return lax.ppermute(array, 'tp', [(t, t ^ flip) for t in range(count)])]
    pallas_call x2 -> x1, Pallas kernels: 1.3 us -> 0.65 us  [stage(): pl.pallas_call(functools.partial(stage_kernel, group, count, len(before)...]
  transfers between devices with their start and end apart: 8 -> 8, of which waited for: 3 -> 3; matrix products, arithmetic and copies ran while one was open for 0% -> 0% of each run, Pallas kernels for 13% -> 11%
where the time goes in v7:
time: 21.2 us; the launch traced here: 21.1 us
  starting transfers between devices  13.5 us (64%)
  Pallas kernels  4.97 us (23%)
  waiting for transfers between devices  1.98 us (9%)
  between operations  0.68 us (3%)
    ppermute x4, starting transfers between devices, send(): return lax.ppermute(array, ('section', 'tp'), pairs)  8.09 us
    ppermute x4, starting transfers between devices, send(): return lax.ppermute(array, 'tp', [(t, t ^ flip) for t in range(count)])  5.36 us
    pallas_call x1, Pallas kernels, last(): pl.pallas_call(functools.partial(last_kernel, len(slots) + len(earlier),...  1.7 us
    pallas_call x1, Pallas kernels, prepare(): pl.pallas_call(functools.partial(prepare_kernel, groups, count), out_shap...  1.69 us
    ppermute x4, waiting for transfers between devices, send(): return lax.ppermute(array, 'tp', [(t, t ^ flip) for t in range(count)])  1.14 us
    pallas_call x1, Pallas kernels, pack(): pl.pallas_call(pack_kernel, out_shape=pltpu.VMEM((TILE, width * count //...  0.93 us
    ppermute x4, waiting for transfers between devices, send(): return lax.ppermute(array, ('section', 'tp'), pairs)  0.84 us
    pallas_call x1, Pallas kernels, stage(): pl.pallas_call(functools.partial(stage_kernel, group, count, len(before)...  0.65 us
  transfers between devices with their start and end apart: 8, of which 3 were waited for; matrix products, arithmetic and copies ran while one was open for 0% of the time, Pallas kernels for 11%

profile of v7, /device:TPU:0, one launch (start us, length us, event | category | flops | bytes accessed | tf_op | source)
XLA Modules:
  0.0 21.1 jit_solution(11676602261897154003)
XLA Ops:
  0.6 0.9 %shard_map.94 = bf16[16,3072]{1,0:T(8,128)(2,1)S(1)} custom-call(bf16[12,4096]{1,0:T(8,128)(2,1)} %bitcast.19), custom_call_target="tpu_custom_call" | custom-call | tf_op jit(solution)/shard_map/pallas_call | solution.py:52
  1.6 3.4 %collective-permute-start.5 = (bf16[16,3072]{1,0:T(8,128)(2,1)S(1)}, bf16[16,3072]{1,0:T(8,128)(2,1)S(1)}, u32[]{:S(2)}, u32[]{:S(2)}) collective-permute-start(bf16[16,3072]{1,0:T(8,128)(2,1)S(1)} %shard_map.94), channel_id=1, source_target_pairs={{0,25},{1,24},{2,27},{3,26},{4,29},{5,28},{6,31},{7,30},{8,1},{9,0... | collective-permute-start | bytes 294920 | tf_op jit(solution)/shard_map/ppermute | solution.py:26
  5.0 2.9 %collective-permute-start.2 = (bf16[16,3072]{1,0:T(8,128)(2,1)S(1)}, bf16[16,3072]{1,0:T(8,128)(2,1)S(1)}, u32[]{:S(2)}, u32[]{:S(2)}) collective-permute-start(bf16[16,3072]{1,0:T(8,128)(2,1)S(1)} %shard_map.94), channel_id=1, source_target_pairs={{0,28},{1,29},{2,30},{3,31},{4,24},{5,25},{6,26},{7,27},{8,4},{9,5... | collective-permute-start | bytes 294920 | tf_op jit(solution)/shard_map/ppermute | solution.py:26
  7.8 1.0 %collective-permute-start = (bf16[16,3072]{1,0:T(8,128)(2,1)S(1)}, bf16[16,3072]{1,0:T(8,128)(2,1)S(1)}, u32[]{:S(2)}, u32[]{:S(2)}) collective-permute-start(bf16[16,3072]{1,0:T(8,128)(2,1)S(1)} %shard_map.94), channel_id=1, source_target_pairs={{0,26},{1,27},{2,24},{3,25},{4,30},{5,31},{6,28},{7,29},{8,2},{9,3... | collective-permute-start | bytes 294920 | tf_op jit(solution)/shard_map/ppermute | solution.py:26
  8.8 0.8 %collective-permute-start.7 = (bf16[16,3072]{1,0:T(8,128)(2,1)S(1)}, bf16[16,3072]{1,0:T(8,128)(2,1)S(1)}, u32[]{:S(2)}, u32[]{:S(2)}) collective-permute-start(bf16[16,3072]{1,0:T(8,128)(2,1)S(1)} %shard_map.94), channel_id=1, source_target_pairs={{0,24},{1,25},{2,26},{3,27},{4,28},{5,29},{6,30},{7,31},{8,0},{9,1... | collective-permute-start | bytes 294920 | tf_op jit(solution)/shard_map/ppermute | solution.py:26
  9.7 0.0 collective-permute-done.5.refs_1_
  9.7 1.1 %collective-permute-start.6 = (bf16[16,3072]{1,0:T(8,128)(2,1)S(1)}, bf16[16,3072]{1,0:T(8,128)(2,1)S(1)}, u32[]{:S(2)}, u32[]{:S(2)}) collective-permute-start(bf16[16,3072]{1,0:T(8,128)(2,1)S(1)} %collective-permute-done.5.refs_1_), channel_id=1, source_target_pairs={{0,6},{1,7},{2,4},{3,5},{4,2},{5,3},{6,0},{7,1},{8,14},{9,15},{10,... | collective-permute-start | bytes 294920 | tf_op jit(solution)/shard_map/ppermute | solution.py:20
  10.8 0.8 %collective-permute-done.2.refs_3_ = bf16[16,3072]{1,0:T(8,128)(2,1)S(1)} collective-permute-done((bf16[16,3072]{1,0:T(8,128)(2,1)S(1)}, bf16[16,3072]{1,0:T(8,128)(2,1)S(1)}, u32[]{:S(2)}, u32[]{:S(2)}) %collective-permute-start.2) | collective-permute-done | bytes 98336 | tf_op jit(solution)/shard_map/ppermute | solution.py:26
  11.6 1.7 %collective-permute-start.4 = (bf16[16,3072]{1,0:T(8,128)(2,1)S(1)}, bf16[16,3072]{1,0:T(8,128)(2,1)S(1)}, u32[]{:S(2)}, u32[]{:S(2)}) collective-permute-start(bf16[16,3072]{1,0:T(8,128)(2,1)S(1)} %collective-permute-done.2.refs_3_), channel_id=1, source_target_pairs={{0,1},{1,0},{2,3},{3,2},{4,5},{5,4},{6,7},{7,6},{8,9},{9,8},{10,11... | collective-permute-start | bytes 294920 | tf_op jit(solution)/shard_map/ppermute | solution.py:20
  13.3 1.0 %collective-permute-start.3 = (bf16[16,3072]{1,0:T(8,128)(2,1)S(1)}, bf16[16,3072]{1,0:T(8,128)(2,1)S(1)}, u32[]{:S(2)}, u32[]{:S(2)}) collective-permute-start(bf16[16,3072]{1,0:T(8,128)(2,1)S(1)} %collective-permute-done.2.refs_3_), channel_id=1, source_target_pairs={{0,2},{1,3},{2,0},{3,1},{4,6},{5,7},{6,4},{7,5},{8,10},{9,11},{10,... | collective-permute-start | bytes 294920 | tf_op jit(solution)/shard_map/ppermute | solution.py:20
  14.3 0.0 collective-permute-done.refs_2_
  14.3 1.5 %collective-permute-start.1 = (bf16[16,3072]{1,0:T(8,128)(2,1)S(1)}, bf16[16,3072]{1,0:T(8,128)(2,1)S(1)}, u32[]{:S(2)}, u32[]{:S(2)}) collective-permute-start(bf16[16,3072]{1,0:T(8,128)(2,1)S(1)} %collective-permute-done.refs_2_), channel_id=1, source_target_pairs={{0,1},{1,0},{2,3},{3,2},{4,5},{5,4},{6,7},{7,6},{8,9},{9,8},{10,11... | collective-permute-start | bytes 294920 | tf_op jit(solution)/shard_map/ppermute | solution.py:20
  15.9 1.7 %shard_map.95 = (bf16[160,4096]{1,0:T(8,128)(2,1)S(1)}, bf16[160,128]{1,0:T(8,128)(2,1)S(1)}, f32[160,64]{1,0:T(8,128)S(1)}, f32[160,64]{1,0:T(8,128)S(1)}, f32[...) custom-call(bf16[160,96]{1,0:T(8,128)(2,1)} %bitcast.21, s32[5,1,96]{2,1,0:T(1,128)} %bitcast.23, bf16[160,96]{1,0:T(8,128)(2,1)} %bitcast.22, ...), custom_call_target="tpu_custom_call" | custom-call | bytes 16777216 | tf_op jit(solution)/shard_map/pallas_call | solution.py:120
  17.6 0.0 collective-permute-done.7.refs_0_
  17.6 0.6 %shard_map.96 = (bf16[64,4096]{1,0:T(8,128)(2,1)S(1)}, bf16[160,96]{1,0:T(8,128)(2,1)S(1)}, bf16[160,96]{1,0:T(8,128)(2,1)S(1)}) custom-call(bf16[16,3072]{1,0:T(8,128)(2,1)S(1)} %collective-permute-done.7.refs_0_, bf16[16,3072]{1,0:T(8,128)(2,1)S(1)} %collective-permute-done.5.refs_1_, bf16[16,3072]{1,0:T(8,128)(2,1)S(1)} %collective-permute-done.refs_2_, ...), custom_call_target="tpu_custom_call" | custom-call | bytes 16777216 | tf_op jit(solution)/shard_map/pallas_call | solution.py:175
  18.2 0.0 collective-permute-done.6.refs_3_
  18.2 0.0 collective-permute-done.4.refs_2_
  18.2 0.2 collective-permute-done.3.refs_1_
  18.4 1.0 %collective-permute-done.1.refs_0_ = bf16[16,3072]{1,0:T(8,128)(2,1)S(1)} collective-permute-done((bf16[16,3072]{1,0:T(8,128)(2,1)S(1)}, bf16[16,3072]{1,0:T(8,128)(2,1)S(1)}, u32[]{:S(2)}, u32[]{:S(2)}) %collective-permute-start.1) | collective-permute-done | bytes 98336 | tf_op jit(solution)/shard_map/ppermute | solution.py:20
  19.4 1.7 %shard_map.97 = (bf16[160,4096]{1,0:T(8,128)(2,1)}, bf16[160,96]{1,0:T(8,128)(2,1)}, bf16[160,96]{1,0:T(8,128)(2,1)}) custom-call(bf16[16,3072]{1,0:T(8,128)(2,1)S(1)} %collective-permute-done.1.refs_0_, bf16[16,3072]{1,0:T(8,128)(2,1)S(1)} %collective-permute-done.3.refs_1_, bf16[16,3072]{1,0:T(8,128)(2,1)S(1)} %collective-permute-done.4.refs_2_, ...), custom_call_target="tpu_custom_call" | custom-call | bytes 16777216 | tf_op jit(solution)/shard_map/pallas_call | solution.py:218
Async XLA Ops:
  1.6 8.1 %collective-permute-start.5 = (bf16[16,3072]{1,0:T(8,128)(2,1)S(1)}, bf16[16,3072]{1,0:T(8,128)(2,1)S(1)}, u32[]{:S(2)}, u32[]{:S(2)}) collective-permute-start(bf16[16,3072]{1,0:T(8,128)(2,1)S(1)} %shard_map.94), channel_id=1, source_target_pairs={{0,25},{1,24},{2,27},{3,26},{4,29},{5,28},{6,31},{7,30},{8,1},{9,0... | collective-permute-start | bytes 294920 | tf_op jit(solution)/shard_map/ppermute | solution.py:26
  5.0 6.7 %collective-permute-start.2 = (bf16[16,3072]{1,0:T(8,128)(2,1)S(1)}, bf16[16,3072]{1,0:T(8,128)(2,1)S(1)}, u32[]{:S(2)}, u32[]{:S(2)}) collective-permute-start(bf16[16,3072]{1,0:T(8,128)(2,1)S(1)} %shard_map.94), channel_id=1, source_target_pairs={{0,28},{1,29},{2,30},{3,31},{4,24},{5,25},{6,26},{7,27},{8,4},{9,5... | collective-permute-start | bytes 294920 | tf_op jit(solution)/shard_map/ppermute | solution.py:26
  7.8 6.5 %collective-permute-start = (bf16[16,3072]{1,0:T(8,128)(2,1)S(1)}, bf16[16,3072]{1,0:T(8,128)(2,1)S(1)}, u32[]{:S(2)}, u32[]{:S(2)}) collective-permute-start(bf16[16,3072]{1,0:T(8,128)(2,1)S(1)} %shard_map.94), channel_id=1, source_target_pairs={{0,26},{1,27},{2,24},{3,25},{4,30},{5,31},{6,28},{7,29},{8,2},{9,3... | collective-permute-start | bytes 294920 | tf_op jit(solution)/shard_map/ppermute | solution.py:26
  8.8 8.8 %collective-permute-start.7 = (bf16[16,3072]{1,0:T(8,128)(2,1)S(1)}, bf16[16,3072]{1,0:T(8,128)(2,1)S(1)}, u32[]{:S(2)}, u32[]{:S(2)}) collective-permute-start(bf16[16,3072]{1,0:T(8,128)(2,1)S(1)} %shard_map.94), channel_id=1, source_target_pairs={{0,24},{1,25},{2,26},{3,27},{4,28},{5,29},{6,30},{7,31},{8,0},{9,1... | collective-permute-start | bytes 294920 | tf_op jit(solution)/shard_map/ppermute | solution.py:26
  9.7 8.6 %collective-permute-start.6 = (bf16[16,3072]{1,0:T(8,128)(2,1)S(1)}, bf16[16,3072]{1,0:T(8,128)(2,1)S(1)}, u32[]{:S(2)}, u32[]{:S(2)}) collective-permute-start(bf16[16,3072]{1,0:T(8,128)(2,1)S(1)} %collective-permute-done.5.refs_1_), channel_id=1, source_target_pairs={{0,6},{1,7},{2,4},{3,5},{4,2},{5,3},{6,0},{7,1},{8,14},{9,15},{10,... | collective-permute-start | bytes 294920 | tf_op jit(solution)/shard_map/ppermute | solution.py:20
  11.6 6.6 %collective-permute-start.4 = (bf16[16,3072]{1,0:T(8,128)(2,1)S(1)}, bf16[16,3072]{1,0:T(8,128)(2,1)S(1)}, u32[]{:S(2)}, u32[]{:S(2)}) collective-permute-start(bf16[16,3072]{1,0:T(8,128)(2,1)S(1)} %collective-permute-done.2.refs_3_), channel_id=1, source_target_pairs={{0,1},{1,0},{2,3},{3,2},{4,5},{5,4},{6,7},{7,6},{8,9},{9,8},{10,11... | collective-permute-start | bytes 294920 | tf_op jit(solution)/shard_map/ppermute | solution.py:20
  13.3 5.1 %collective-permute-start.3 = (bf16[16,3072]{1,0:T(8,128)(2,1)S(1)}, bf16[16,3072]{1,0:T(8,128)(2,1)S(1)}, u32[]{:S(2)}, u32[]{:S(2)}) collective-permute-start(bf16[16,3072]{1,0:T(8,128)(2,1)S(1)} %collective-permute-done.2.refs_3_), channel_id=1, source_target_pairs={{0,2},{1,3},{2,0},{3,1},{4,6},{5,7},{6,4},{7,5},{8,10},{9,11},{10,... | collective-permute-start | bytes 294920 | tf_op jit(solution)/shard_map/ppermute | solution.py:20
  14.3 5.1 %collective-permute-start.1 = (bf16[16,3072]{1,0:T(8,128)(2,1)S(1)}, bf16[16,3072]{1,0:T(8,128)(2,1)S(1)}, u32[]{:S(2)}, u32[]{:S(2)}) collective-permute-start(bf16[16,3072]{1,0:T(8,128)(2,1)S(1)} %collective-permute-done.refs_2_), channel_id=1, source_target_pairs={{0,1},{1,0},{2,3},{3,2},{4,5},{5,4},{6,7},{7,6},{8,9},{9,8},{10,11... | collective-permute-start | bytes 294920 | tf_op jit(solution)/shard_map/ppermute | solution.py:20

commit v8 on v7

--- a/solution.py
+++ b/solution.py
@@ -236,16 +236,11 @@
     p = pack(grad_held[0])
     first = [f for f in range(n) if f & (f - 1) == 0]
     rest = [f for f in range(n) if f not in first]
-    late = [f for f in rest if f - n // 2 in first]
-    groups = [first, [f for f in rest[:-1] if f not in late] + late[::-1] + rest[-1:]]
+    late = [f for f in rest[:-1] if f - n // 2 in first]
+    groups = [first, [n - 1], [f for f in rest[:-1] if f not in late] + late[::-1]]
     got = {}
     for flip in reversed(first):
         got[flip] = send(p, flip, 1)
-    for flip in reversed(rest):
-        step = flip & -flip
-        if flip & 1 and flip - 1 not in first:
-            step = flip - 1
-        got[flip] = send(got[flip - step], step, 0)
     weight, hidden, factors = prepare(
         groups,
         count,
@@ -256,6 +251,12 @@
         down_codes[0],
         down_exponents.transpose(1, 0, 2),
     )
+    got[1], _ = lax.optimization_barrier((got[1], hidden))
+    for flip in reversed(rest):
+        step = flip & -flip
+        if flip & 1 and flip - 1 not in first:
+            step = flip - 1
+        got[flip] = send(got[flip - step], step, 0)
     earlier, before = [], []
     for group, pair in zip(groups[:-1], factors):
         incoming, *before = stage(group, count, n * count, [got[j] for j in group], weight, pair, before)
@@ -292,7 +293,7 @@
     n = lax.axis_size("tp")
     count, width = operands[-1].shape[1:]
     free = TILE - count
-    small = n & (n - 1) == 0 and 4 <= n <= TILE
+    small = n & (n - 1) == 0 and 8 <= n <= TILE
     fits = 0 < free < TILE and count % free == 0 and width * free % (TILE * 128) == 0 and width % (4 * 128) == 0
     return fanned(*operands) if small and fits else ringed(*operands)
 

time: 21.2 us -> 21.9 us (1.033)
  starting transfers between devices: 13.5 us -> 12.6 us
  waiting for transfers between devices: 1.98 us -> 2.83 us
  Pallas kernels: 4.97 us -> 5.62 us
    ppermute x4, waiting for transfers between devices: 1.14 us -> 2.82 us  [send(): return lax.ppermute(array, 'tp', [(t, t ^ flip) for t in range(count)])]
    ppermute x4, starting transfers between devices: 5.36 us -> 4.49 us  [send(): return lax.ppermute(array, 'tp', [(t, t ^ flip) for t in range(count)])]
    ppermute x4, waiting for transfers between devices: 0.84 us -> 0.01 us  [send(): return lax.ppermute(array, ('section', 'tp'), pairs)]
    pallas_call x1 -> x2, Pallas kernels: 0.65 us -> 1.29 us  [stage(): pl.pallas_call(functools.partial(stage_kernel, group, count, len(before)...]
  transfers between devices with their start and end apart: 8 -> 8, of which waited for: 3 -> 2; matrix products, arithmetic and copies ran while one was open for 0% -> 0% of each run, Pallas kernels for 11% -> 14%
where the time goes in v8:
time: 21.9 us; the launch traced here: 21.7 us
  starting transfers between devices  12.6 us (58%)
  Pallas kernels  5.62 us (26%)
  waiting for transfers between devices  2.83 us (13%)
  between operations  0.68 us (3%)
    ppermute x4, starting transfers between devices, send(): return lax.ppermute(array, ('section', 'tp'), pairs)  8.09 us
    ppermute x4, starting transfers between devices, send(): return lax.ppermute(array, 'tp', [(t, t ^ flip) for t in range(count)])  4.49 us
    ppermute x4, waiting for transfers between devices, send(): return lax.ppermute(array, 'tp', [(t, t ^ flip) for t in range(count)])  2.82 us
    pallas_call x1, Pallas kernels, last(): pl.pallas_call(functools.partial(last_kernel, len(slots) + len(earlier),...  1.7 us
    pallas_call x1, Pallas kernels, prepare(): pl.pallas_call(functools.partial(prepare_kernel, groups, count), out_shap...  1.69 us
    pallas_call x2, Pallas kernels, stage(): pl.pallas_call(functools.partial(stage_kernel, group, count, len(before)...  1.29 us
    pallas_call x1, Pallas kernels, pack(): pl.pallas_call(pack_kernel, out_shape=pltpu.VMEM((TILE, width * count //...  0.93 us
  transfers between devices with their start and end apart: 8, of which 2 were waited for; matrix products, arithmetic and copies ran while one was open for 0% of the time, Pallas kernels for 14%

profile of v8, /device:TPU:0, one launch (start us, length us, event | category | flops | bytes accessed | tf_op | source)
XLA Modules:
  0.0 21.7 jit_solution(10140722448300780353)
XLA Ops:
  0.6 0.9 %shard_map.94 = bf16[16,3072]{1,0:T(8,128)(2,1)S(1)} custom-call(bf16[12,4096]{1,0:T(8,128)(2,1)} %bitcast.19), custom_call_target="tpu_custom_call" | custom-call | tf_op jit(solution)/shard_map/pallas_call | solution.py:52
  1.6 3.4 %collective-permute-start.6 = (bf16[16,3072]{1,0:T(8,128)(2,1)S(1)}, bf16[16,3072]{1,0:T(8,128)(2,1)S(1)}, u32[]{:S(2)}, u32[]{:S(2)}) collective-permute-start(bf16[16,3072]{1,0:T(8,128)(2,1)S(1)} %shard_map.94), channel_id=1, source_target_pairs={{0,25},{1,24},{2,27},{3,26},{4,29},{5,28},{6,31},{7,30},{8,1},{9,0... | collective-permute-start | bytes 294920 | tf_op jit(solution)/shard_map/ppermute | solution.py:26
  5.0 2.9 %collective-permute-start.2 = (bf16[16,3072]{1,0:T(8,128)(2,1)S(1)}, bf16[16,3072]{1,0:T(8,128)(2,1)S(1)}, u32[]{:S(2)}, u32[]{:S(2)}) collective-permute-start(bf16[16,3072]{1,0:T(8,128)(2,1)S(1)} %shard_map.94), channel_id=1, source_target_pairs={{0,28},{1,29},{2,30},{3,31},{4,24},{5,25},{6,26},{7,27},{8,4},{9,5... | collective-permute-start | bytes 294920 | tf_op jit(solution)/shard_map/ppermute | solution.py:26
  7.8 1.0 %collective-permute-start = (bf16[16,3072]{1,0:T(8,128)(2,1)S(1)}, bf16[16,3072]{1,0:T(8,128)(2,1)S(1)}, u32[]{:S(2)}, u32[]{:S(2)}) collective-permute-start(bf16[16,3072]{1,0:T(8,128)(2,1)S(1)} %shard_map.94), channel_id=1, source_target_pairs={{0,26},{1,27},{2,24},{3,25},{4,30},{5,31},{6,28},{7,29},{8,2},{9,3... | collective-permute-start | bytes 294920 | tf_op jit(solution)/shard_map/ppermute | solution.py:26
  8.8 0.8 %collective-permute-start.5 = (bf16[16,3072]{1,0:T(8,128)(2,1)S(1)}, bf16[16,3072]{1,0:T(8,128)(2,1)S(1)}, u32[]{:S(2)}, u32[]{:S(2)}) collective-permute-start(bf16[16,3072]{1,0:T(8,128)(2,1)S(1)} %shard_map.94), channel_id=1, source_target_pairs={{0,24},{1,25},{2,26},{3,27},{4,28},{5,29},{6,30},{7,31},{8,0},{9,1... | collective-permute-start | bytes 294920 | tf_op jit(solution)/shard_map/ppermute | solution.py:26
  9.7 1.7 %shard_map.95 = (bf16[160,4096]{1,0:T(8,128)(2,1)S(1)}, bf16[160,128]{1,0:T(8,128)(2,1)S(1)}, f32[160,64]{1,0:T(8,128)S(1)}, f32[160,64]{1,0:T(8,128)S(1)}, f32[...) custom-call(bf16[160,96]{1,0:T(8,128)(2,1)} %bitcast.21, ...), custom_call_target="tpu_custom_call" | custom-call | bytes 16777216 | tf_op jit(solution)/shard_map/pallas_call | solution.py:120
  11.4 0.0 collective-permute-done.6.refs_1_
  11.4 0.3 %collective-permute-start.7 = (bf16[16,3072]{1,0:T(8,128)(2,1)S(1)}, bf16[16,3072]{1,0:T(8,128)(2,1)S(1)}, u32[]{:S(2)}, u32[]{:S(2)}) collective-permute-start(bf16[16,3072]{1,0:T(8,128)(2,1)S(1)} %collective-permute-done.6.refs_1_), channel_id=1, source_target_pairs={{0,6},{1,7},{2,4},{3,5},{4,2},{5,3},{6,0},{7,1},{8,14},{9,15},{10,... | collective-permute-start | bytes 294920 | tf_op jit(solution)/shard_map/ppermute | solution.py:20
  11.7 0.0 collective-permute-done.2.refs_3_
  11.7 1.6 %collective-permute-start.4 = (bf16[16,3072]{1,0:T(8,128)(2,1)S(1)}, bf16[16,3072]{1,0:T(8,128)(2,1)S(1)}, u32[]{:S(2)}, u32[]{:S(2)}) collective-permute-start(bf16[16,3072]{1,0:T(8,128)(2,1)S(1)} %collective-permute-done.2.refs_3_), channel_id=1, source_target_pairs={{0,1},{1,0},{2,3},{3,2},{4,5},{5,4},{6,7},{7,6},{8,9},{9,8},{10,11... | collective-permute-start | bytes 294920 | tf_op jit(solution)/shard_map/ppermute | solution.py:20
  13.3 1.0 %collective-permute-start.3 = (bf16[16,3072]{1,0:T(8,128)(2,1)S(1)}, bf16[16,3072]{1,0:T(8,128)(2,1)S(1)}, u32[]{:S(2)}, u32[]{:S(2)}) collective-permute-start(bf16[16,3072]{1,0:T(8,128)(2,1)S(1)} %collective-permute-done.2.refs_3_), channel_id=1, source_target_pairs={{0,2},{1,3},{2,0},{3,1},{4,6},{5,7},{6,4},{7,5},{8,10},{9,11},{10,... | collective-permute-start | bytes 294920 | tf_op jit(solution)/shard_map/ppermute | solution.py:20
  14.3 0.0 collective-permute-done.refs_2_
  14.3 1.5 %collective-permute-start.1 = (bf16[16,3072]{1,0:T(8,128)(2,1)S(1)}, bf16[16,3072]{1,0:T(8,128)(2,1)S(1)}, u32[]{:S(2)}, u32[]{:S(2)}) collective-permute-start(bf16[16,3072]{1,0:T(8,128)(2,1)S(1)} %collective-permute-done.refs_2_), channel_id=1, source_target_pairs={{0,1},{1,0},{2,3},{3,2},{4,5},{5,4},{6,7},{7,6},{8,9},{9,8},{10,11... | collective-permute-start | bytes 294920 | tf_op jit(solution)/shard_map/ppermute | solution.py:20
  15.9 0.0 collective-permute-done.5.refs_0_
  15.9 0.6 %shard_map.96 = (bf16[64,4096]{1,0:T(8,128)(2,1)S(1)}, bf16[160,96]{1,0:T(8,128)(2,1)S(1)}, bf16[160,96]{1,0:T(8,128)(2,1)S(1)}) custom-call(bf16[16,3072]{1,0:T(8,128)(2,1)S(1)} %collective-permute-done.5.refs_0_, bf16[16,3072]{1,0:T(8,128)(2,1)S(1)} %collective-permute-done.6.refs_1_, bf16[16,3072]{1,0:T(8,128)(2,1)S(1)} %collective-permute-done.refs_2_, ...), custom_call_target="tpu_custom_call" | custom-call | bytes 16777216 | tf_op jit(solution)/shard_map/pallas_call | solution.py:175
  16.5 1.6 %collective-permute-done.7.refs_0_ = bf16[16,3072]{1,0:T(8,128)(2,1)S(1)} collective-permute-done((bf16[16,3072]{1,0:T(8,128)(2,1)S(1)}, bf16[16,3072]{1,0:T(8,128)(2,1)S(1)}, u32[]{:S(2)}, u32[]{:S(2)}) %collective-permute-start.7) | collective-permute-done | bytes 98336 | tf_op jit(solution)/shard_map/ppermute | solution.py:20
  18.1 0.7 %shard_map.97 = (bf16[16,4096]{1,0:T(8,128)(2,1)S(1)}, bf16[160,96]{1,0:T(8,128)(2,1)S(1)}, bf16[160,96]{1,0:T(8,128)(2,1)S(1)}) custom-call(bf16[16,3072]{1,0:T(8,128)(2,1)S(1)} %collective-permute-done.7.refs_0_, bf16[160,4096]{1,0:T(8,128)(2,1)S(1)} %get-tuple-element.23.refs_4_.refs_1_.refs_5_, f32[160,16]{1,0:T(8,128)S(1)} %get-tuple-element.27.refs_2_, ...), custom_call_target="tpu_custom_call" | custom-call | bytes 16777216 | tf_op jit(solution)/shard_map/pallas_call | solution.py:175
  18.8 0.0 collective-permute-done.4.refs_2_
  18.8 1.2 %collective-permute-done.3.refs_1_ = bf16[16,3072]{1,0:T(8,128)(2,1)S(1)} collective-permute-done((bf16[16,3072]{1,0:T(8,128)(2,1)S(1)}, bf16[16,3072]{1,0:T(8,128)(2,1)S(1)}, u32[]{:S(2)}, u32[]{:S(2)}) %collective-permute-start.3) | collective-permute-done | bytes 98336 | tf_op jit(solution)/shard_map/ppermute | solution.py:20
  20.0 0.0 collective-permute-done.1.refs_0_
  20.0 1.7 %shard_map.98 = (bf16[160,4096]{1,0:T(8,128)(2,1)}, bf16[160,96]{1,0:T(8,128)(2,1)}, bf16[160,96]{1,0:T(8,128)(2,1)}) custom-call(bf16[16,3072]{1,0:T(8,128)(2,1)S(1)} %collective-permute-done.1.refs_0_, bf16[16,3072]{1,0:T(8,128)(2,1)S(1)} %collective-permute-done.3.refs_1_, bf16[16,3072]{1,0:T(8,128)(2,1)S(1)} %collective-permute-done.4.refs_2_, ...), custom_call_target="tpu_custom_call" | custom-call | bytes 16777216 | tf_op jit(solution)/shard_map/pallas_call | solution.py:218
Async XLA Ops:
  1.6 9.8 %collective-permute-start.6 = (bf16[16,3072]{1,0:T(8,128)(2,1)S(1)}, bf16[16,3072]{1,0:T(8,128)(2,1)S(1)}, u32[]{:S(2)}, u32[]{:S(2)}) collective-permute-start(bf16[16,3072]{1,0:T(8,128)(2,1)S(1)} %shard_map.94), channel_id=1, source_target_pairs={{0,25},{1,24},{2,27},{3,26},{4,29},{5,28},{6,31},{7,30},{8,1},{9,0... | collective-permute-start | bytes 294920 | tf_op jit(solution)/shard_map/ppermute | solution.py:26
  5.0 6.7 %collective-permute-start.2 = (bf16[16,3072]{1,0:T(8,128)(2,1)S(1)}, bf16[16,3072]{1,0:T(8,128)(2,1)S(1)}, u32[]{:S(2)}, u32[]{:S(2)}) collective-permute-start(bf16[16,3072]{1,0:T(8,128)(2,1)S(1)} %shard_map.94), channel_id=1, source_target_pairs={{0,28},{1,29},{2,30},{3,31},{4,24},{5,25},{6,26},{7,27},{8,4},{9,5... | collective-permute-start | bytes 294920 | tf_op jit(solution)/shard_map/ppermute | solution.py:26
  7.8 6.5 %collective-permute-start = (bf16[16,3072]{1,0:T(8,128)(2,1)S(1)}, bf16[16,3072]{1,0:T(8,128)(2,1)S(1)}, u32[]{:S(2)}, u32[]{:S(2)}) collective-permute-start(bf16[16,3072]{1,0:T(8,128)(2,1)S(1)} %shard_map.94), channel_id=1, source_target_pairs={{0,26},{1,27},{2,24},{3,25},{4,30},{5,31},{6,28},{7,29},{8,2},{9,3... | collective-permute-start | bytes 294920 | tf_op jit(solution)/shard_map/ppermute | solution.py:26
  8.8 7.1 %collective-permute-start.5 = (bf16[16,3072]{1,0:T(8,128)(2,1)S(1)}, bf16[16,3072]{1,0:T(8,128)(2,1)S(1)}, u32[]{:S(2)}, u32[]{:S(2)}) collective-permute-start(bf16[16,3072]{1,0:T(8,128)(2,1)S(1)} %shard_map.94), channel_id=1, source_target_pairs={{0,24},{1,25},{2,26},{3,27},{4,28},{5,29},{6,30},{7,31},{8,0},{9,1... | collective-permute-start | bytes 294920 | tf_op jit(solution)/shard_map/ppermute | solution.py:26
  11.4 6.7 %collective-permute-start.7 = (bf16[16,3072]{1,0:T(8,128)(2,1)S(1)}, bf16[16,3072]{1,0:T(8,128)(2,1)S(1)}, u32[]{:S(2)}, u32[]{:S(2)}) collective-permute-start(bf16[16,3072]{1,0:T(8,128)(2,1)S(1)} %collective-permute-done.6.refs_1_), channel_id=1, source_target_pairs={{0,6},{1,7},{2,4},{3,5},{4,2},{5,3},{6,0},{7,1},{8,14},{9,15},{10,... | collective-permute-start | bytes 294920 | tf_op jit(solution)/shard_map/ppermute | solution.py:20
  11.7 7.1 %collective-permute-start.4 = (bf16[16,3072]{1,0:T(8,128)(2,1)S(1)}, bf16[16,3072]{1,0:T(8,128)(2,1)S(1)}, u32[]{:S(2)}, u32[]{:S(2)}) collective-permute-start(bf16[16,3072]{1,0:T(8,128)(2,1)S(1)} %collective-permute-done.2.refs_3_), channel_id=1, source_target_pairs={{0,1},{1,0},{2,3},{3,2},{4,5},{5,4},{6,7},{7,6},{8,9},{9,8},{10,11... | collective-permute-start | bytes 294920 | tf_op jit(solution)/shard_map/ppermute | solution.py:20
  13.3 6.7 %collective-permute-start.3 = (bf16[16,3072]{1,0:T(8,128)(2,1)S(1)}, bf16[16,3072]{1,0:T(8,128)(2,1)S(1)}, u32[]{:S(2)}, u32[]{:S(2)}) collective-permute-start(bf16[16,3072]{1,0:T(8,128)(2,1)S(1)} %collective-permute-done.2.refs_3_), channel_id=1, source_target_pairs={{0,2},{1,3},{2,0},{3,1},{4,6},{5,7},{6,4},{7,5},{8,10},{9,11},{10,... | collective-permute-start | bytes 294920 | tf_op jit(solution)/shard_map/ppermute | solution.py:20
  14.3 5.7 %collective-permute-start.1 = (bf16[16,3072]{1,0:T(8,128)(2,1)S(1)}, bf16[16,3072]{1,0:T(8,128)(2,1)S(1)}, u32[]{:S(2)}, u32[]{:S(2)}) collective-permute-start(bf16[16,3072]{1,0:T(8,128)(2,1)S(1)} %collective-permute-done.refs_2_), channel_id=1, source_target_pairs={{0,1},{1,0},{2,3},{3,2},{4,5},{5,4},{6,7},{7,6},{8,9},{9,8},{10,11... | collective-permute-start | bytes 294920 | tf_op jit(solution)/shard_map/ppermute | solution.py:20

commit v9 on v7

--- a/solution.py
+++ b/solution.py
@@ -199,12 +199,13 @@
         down = jnp.dot(hidden_ref[...], incoming, preferred_element_type=jnp.float32)
         held_refs[0][:, here] = down.astype(jnp.bfloat16)
         copies += started(held_refs[0].at[:, here], out_refs[0].at[:, here], sems.at[2 + i], i % 2)
-    slope = lax.dot_general(
-        weight_ref[...], newest_ref[...], (((1,), (1,)), ((), ())), preferred_element_type=jnp.float32
-    )
-    grads(group, count, slope, factor_refs, before_refs, held_refs[1:])
-    for i in range(2):
-        copies += started(held_refs[1 + i], out_refs[1 + i], sems.at[i])
+        if i == parts // 2 - 1:
+            slope = lax.dot_general(
+                weight_ref[...], newest_ref[...], (((1,), (1,)), ((), ())), preferred_element_type=jnp.float32
+            )
+            grads(group, count, slope, factor_refs, before_refs, held_refs[1:])
+            for j in range(2):
+                copies += started(held_refs[1 + j], out_refs[1 + j], sems.at[j])
     for copy in copies:
         copy.wait()
 
@@ -212,7 +213,7 @@
 def last(group, count, slots, earlier, weight, hidden, factors, before):
     units, width = weight.shape
     tokens = before[0].shape[1]
-    parts = 4
+    parts = 8
     operands = (*slots, *earlier, weight, hidden, *factors, *before)
     shapes = [(units, width), (units, tokens), (units, tokens)]
     return pl.pallas_call(
@@ -293,7 +294,7 @@
     count, width = operands[-1].shape[1:]
     free = TILE - count
     small = n & (n - 1) == 0 and 4 <= n <= TILE
-    fits = 0 < free < TILE and count % free == 0 and width * free % (TILE * 128) == 0 and width % (4 * 128) == 0
+    fits = 0 < free < TILE and count % free == 0 and width * free % (TILE * 128) == 0 and width % (8 * 128) == 0
     return fanned(*operands) if small and fits else ringed(*operands)
 
 

time: 21.2 us -> 21.6 us (1.019)
  Pallas kernels: 4.97 us -> 5.36 us
    pallas_call x1, Pallas kernels: 1.7 us -> 2.09 us  [last(): pl.pallas_call(functools.partial(last_kernel, len(slots) + len(earlier),...]
where the time goes in v9:
time: 21.6 us; the launch traced here: 21.5 us
  starting transfers between devices  13.5 us (62%)
  Pallas kernels  5.36 us (25%)
  waiting for transfers between devices  1.98 us (9%)
  between operations  0.68 us (3%)
    ppermute x4, starting transfers between devices, send(): return lax.ppermute(array, ('section', 'tp'), pairs)  8.09 us
    ppermute x4, starting transfers between devices, send(): return lax.ppermute(array, 'tp', [(t, t ^ flip) for t in range(count)])  5.36 us
    pallas_call x1, Pallas kernels, last(): pl.pallas_call(functools.partial(last_kernel, len(slots) + len(earlier),...  2.09 us
    pallas_call x1, Pallas kernels, prepare(): pl.pallas_call(functools.partial(prepare_kernel, groups, count), out_shap...  1.69 us
    ppermute x4, waiting for transfers between devices, send(): return lax.ppermute(array, 'tp', [(t, t ^ flip) for t in range(count)])  1.14 us
    pallas_call x1, Pallas kernels, pack(): pl.pallas_call(pack_kernel, out_shape=pltpu.VMEM((TILE, width * count //...  0.93 us
    ppermute x4, waiting for transfers between devices, send(): return lax.ppermute(array, ('section', 'tp'), pairs)  0.84 us
    pallas_call x1, Pallas kernels, stage(): pl.pallas_call(functools.partial(stage_kernel, group, count, len(before)...  0.65 us
  transfers between devices with their start and end apart: 8, of which 3 were waited for; matrix products, arithmetic and copies ran while one was open for 0% of the time, Pallas kernels for 11%

profile of v9, /device:TPU:0, one launch (start us, length us, event | category | flops | bytes accessed | tf_op | source)
XLA Modules:
  0.0 21.5 jit_solution(4091917826934404922)
XLA Ops:
  0.6 0.9 %shard_map.94 = bf16[16,3072]{1,0:T(8,128)(2,1)S(1)} custom-call(bf16[12,4096]{1,0:T(8,128)(2,1)} %bitcast.19), custom_call_target="tpu_custom_call" | custom-call | tf_op jit(solution)/shard_map/pallas_call | solution.py:52
  1.6 3.4 %collective-permute-start.5 = (bf16[16,3072]{1,0:T(8,128)(2,1)S(1)}, bf16[16,3072]{1,0:T(8,128)(2,1)S(1)}, u32[]{:S(2)}, u32[]{:S(2)}) collective-permute-start(bf16[16,3072]{1,0:T(8,128)(2,1)S(1)} %shard_map.94), channel_id=1, source_target_pairs={{0,25},{1,24},{2,27},{3,26},{4,29},{5,28},{6,31},{7,30},{8,1},{9,0... | collective-permute-start | bytes 294920 | tf_op jit(solution)/shard_map/ppermute | solution.py:26
  5.0 2.9 %collective-permute-start.2 = (bf16[16,3072]{1,0:T(8,128)(2,1)S(1)}, bf16[16,3072]{1,0:T(8,128)(2,1)S(1)}, u32[]{:S(2)}, u32[]{:S(2)}) collective-permute-start(bf16[16,3072]{1,0:T(8,128)(2,1)S(1)} %shard_map.94), channel_id=1, source_target_pairs={{0,28},{1,29},{2,30},{3,31},{4,24},{5,25},{6,26},{7,27},{8,4},{9,5... | collective-permute-start | bytes 294920 | tf_op jit(solution)/shard_map/ppermute | solution.py:26
  7.8 1.0 %collective-permute-start = (bf16[16,3072]{1,0:T(8,128)(2,1)S(1)}, bf16[16,3072]{1,0:T(8,128)(2,1)S(1)}, u32[]{:S(2)}, u32[]{:S(2)}) collective-permute-start(bf16[16,3072]{1,0:T(8,128)(2,1)S(1)} %shard_map.94), channel_id=1, source_target_pairs={{0,26},{1,27},{2,24},{3,25},{4,30},{5,31},{6,28},{7,29},{8,2},{9,3... | collective-permute-start | bytes 294920 | tf_op jit(solution)/shard_map/ppermute | solution.py:26
  8.8 0.8 %collective-permute-start.7 = (bf16[16,3072]{1,0:T(8,128)(2,1)S(1)}, bf16[16,3072]{1,0:T(8,128)(2,1)S(1)}, u32[]{:S(2)}, u32[]{:S(2)}) collective-permute-start(bf16[16,3072]{1,0:T(8,128)(2,1)S(1)} %shard_map.94), channel_id=1, source_target_pairs={{0,24},{1,25},{2,26},{3,27},{4,28},{5,29},{6,30},{7,31},{8,0},{9,1... | collective-permute-start | bytes 294920 | tf_op jit(solution)/shard_map/ppermute | solution.py:26
  9.7 0.0 collective-permute-done.5.refs_1_
  9.7 1.1 %collective-permute-start.6 = (bf16[16,3072]{1,0:T(8,128)(2,1)S(1)}, bf16[16,3072]{1,0:T(8,128)(2,1)S(1)}, u32[]{:S(2)}, u32[]{:S(2)}) collective-permute-start(bf16[16,3072]{1,0:T(8,128)(2,1)S(1)} %collective-permute-done.5.refs_1_), channel_id=1, source_target_pairs={{0,6},{1,7},{2,4},{3,5},{4,2},{5,3},{6,0},{7,1},{8,14},{9,15},{10,... | collective-permute-start | bytes 294920 | tf_op jit(solution)/shard_map/ppermute | solution.py:20
  10.8 0.8 %collective-permute-done.2.refs_3_ = bf16[16,3072]{1,0:T(8,128)(2,1)S(1)} collective-permute-done((bf16[16,3072]{1,0:T(8,128)(2,1)S(1)}, bf16[16,3072]{1,0:T(8,128)(2,1)S(1)}, u32[]{:S(2)}, u32[]{:S(2)}) %collective-permute-start.2) | collective-permute-done | bytes 98336 | tf_op jit(solution)/shard_map/ppermute | solution.py:26
  11.6 1.7 %collective-permute-start.4 = (bf16[16,3072]{1,0:T(8,128)(2,1)S(1)}, bf16[16,3072]{1,0:T(8,128)(2,1)S(1)}, u32[]{:S(2)}, u32[]{:S(2)}) collective-permute-start(bf16[16,3072]{1,0:T(8,128)(2,1)S(1)} %collective-permute-done.2.refs_3_), channel_id=1, source_target_pairs={{0,1},{1,0},{2,3},{3,2},{4,5},{5,4},{6,7},{7,6},{8,9},{9,8},{10,11... | collective-permute-start | bytes 294920 | tf_op jit(solution)/shard_map/ppermute | solution.py:20
  13.3 1.0 %collective-permute-start.3 = (bf16[16,3072]{1,0:T(8,128)(2,1)S(1)}, bf16[16,3072]{1,0:T(8,128)(2,1)S(1)}, u32[]{:S(2)}, u32[]{:S(2)}) collective-permute-start(bf16[16,3072]{1,0:T(8,128)(2,1)S(1)} %collective-permute-done.2.refs_3_), channel_id=1, source_target_pairs={{0,2},{1,3},{2,0},{3,1},{4,6},{5,7},{6,4},{7,5},{8,10},{9,11},{10,... | collective-permute-start | bytes 294920 | tf_op jit(solution)/shard_map/ppermute | solution.py:20
  14.3 0.0 collective-permute-done.refs_2_
  14.3 1.5 %collective-permute-start.1 = (bf16[16,3072]{1,0:T(8,128)(2,1)S(1)}, bf16[16,3072]{1,0:T(8,128)(2,1)S(1)}, u32[]{:S(2)}, u32[]{:S(2)}) collective-permute-start(bf16[16,3072]{1,0:T(8,128)(2,1)S(1)} %collective-permute-done.refs_2_), channel_id=1, source_target_pairs={{0,1},{1,0},{2,3},{3,2},{4,5},{5,4},{6,7},{7,6},{8,9},{9,8},{10,11... | collective-permute-start | bytes 294920 | tf_op jit(solution)/shard_map/ppermute | solution.py:20
  15.9 1.7 %shard_map.95 = (bf16[160,4096]{1,0:T(8,128)(2,1)S(1)}, bf16[160,128]{1,0:T(8,128)(2,1)S(1)}, f32[160,64]{1,0:T(8,128)S(1)}, f32[160,64]{1,0:T(8,128)S(1)}, f32[...) custom-call(bf16[160,96]{1,0:T(8,128)(2,1)} %bitcast.21, s32[5,1,96]{2,1,0:T(1,128)} %bitcast.23, bf16[160,96]{1,0:T(8,128)(2,1)} %bitcast.22, ...), custom_call_target="tpu_custom_call" | custom-call | bytes 16777216 | tf_op jit(solution)/shard_map/pallas_call | solution.py:120
  17.6 0.0 collective-permute-done.7.refs_0_
  17.6 0.6 %shard_map.96 = (bf16[64,4096]{1,0:T(8,128)(2,1)S(1)}, bf16[160,96]{1,0:T(8,128)(2,1)S(1)}, bf16[160,96]{1,0:T(8,128)(2,1)S(1)}) custom-call(bf16[16,3072]{1,0:T(8,128)(2,1)S(1)} %collective-permute-done.7.refs_0_, bf16[16,3072]{1,0:T(8,128)(2,1)S(1)} %collective-permute-done.5.refs_1_, bf16[16,3072]{1,0:T(8,128)(2,1)S(1)} %collective-permute-done.refs_2_, ...), custom_call_target="tpu_custom_call" | custom-call | bytes 16777216 | tf_op jit(solution)/shard_map/pallas_call | solution.py:175
  18.2 0.0 collective-permute-done.6.refs_3_
  18.2 0.0 collective-permute-done.4.refs_2_
  18.2 0.2 collective-permute-done.3.refs_1_
  18.4 1.0 %collective-permute-done.1.refs_0_ = bf16[16,3072]{1,0:T(8,128)(2,1)S(1)} collective-permute-done((bf16[16,3072]{1,0:T(8,128)(2,1)S(1)}, bf16[16,3072]{1,0:T(8,128)(2,1)S(1)}, u32[]{:S(2)}, u32[]{:S(2)}) %collective-permute-start.1) | collective-permute-done | bytes 98336 | tf_op jit(solution)/shard_map/ppermute | solution.py:20
  19.4 2.1 %shard_map.97 = (bf16[160,4096]{1,0:T(8,128)(2,1)}, bf16[160,96]{1,0:T(8,128)(2,1)}, bf16[160,96]{1,0:T(8,128)(2,1)}) custom-call(bf16[16,3072]{1,0:T(8,128)(2,1)S(1)} %collective-permute-done.1.refs_0_, bf16[16,3072]{1,0:T(8,128)(2,1)S(1)} %collective-permute-done.3.refs_1_, bf16[16,3072]{1,0:T(8,128)(2,1)S(1)} %collective-permute-done.4.refs_2_, ...), custom_call_target="tpu_custom_call" | custom-call | bytes 16777216 | tf_op jit(solution)/shard_map/pallas_call | solution.py:219
Async XLA Ops:
  1.6 8.1 %collective-permute-start.5 = (bf16[16,3072]{1,0:T(8,128)(2,1)S(1)}, bf16[16,3072]{1,0:T(8,128)(2,1)S(1)}, u32[]{:S(2)}, u32[]{:S(2)}) collective-permute-start(bf16[16,3072]{1,0:T(8,128)(2,1)S(1)} %shard_map.94), channel_id=1, source_target_pairs={{0,25},{1,24},{2,27},{3,26},{4,29},{5,28},{6,31},{7,30},{8,1},{9,0... | collective-permute-start | bytes 294920 | tf_op jit(solution)/shard_map/ppermute | solution.py:26
  5.0 6.7 %collective-permute-start.2 = (bf16[16,3072]{1,0:T(8,128)(2,1)S(1)}, bf16[16,3072]{1,0:T(8,128)(2,1)S(1)}, u32[]{:S(2)}, u32[]{:S(2)}) collective-permute-start(bf16[16,3072]{1,0:T(8,128)(2,1)S(1)} %shard_map.94), channel_id=1, source_target_pairs={{0,28},{1,29},{2,30},{3,31},{4,24},{5,25},{6,26},{7,27},{8,4},{9,5... | collective-permute-start | bytes 294920 | tf_op jit(solution)/shard_map/ppermute | solution.py:26
  7.8 6.5 %collective-permute-start = (bf16[16,3072]{1,0:T(8,128)(2,1)S(1)}, bf16[16,3072]{1,0:T(8,128)(2,1)S(1)}, u32[]{:S(2)}, u32[]{:S(2)}) collective-permute-start(bf16[16,3072]{1,0:T(8,128)(2,1)S(1)} %shard_map.94), channel_id=1, source_target_pairs={{0,26},{1,27},{2,24},{3,25},{4,30},{5,31},{6,28},{7,29},{8,2},{9,3... | collective-permute-start | bytes 294920 | tf_op jit(solution)/shard_map/ppermute | solution.py:26
  8.8 8.8 %collective-permute-start.7 = (bf16[16,3072]{1,0:T(8,128)(2,1)S(1)}, bf16[16,3072]{1,0:T(8,128)(2,1)S(1)}, u32[]{:S(2)}, u32[]{:S(2)}) collective-permute-start(bf16[16,3072]{1,0:T(8,128)(2,1)S(1)} %shard_map.94), channel_id=1, source_target_pairs={{0,24},{1,25},{2,26},{3,27},{4,28},{5,29},{6,30},{7,31},{8,0},{9,1... | collective-permute-start | bytes 294920 | tf_op jit(solution)/shard_map/ppermute | solution.py:26
  9.7 8.6 %collective-permute-start.6 = (bf16[16,3072]{1,0:T(8,128)(2,1)S(1)}, bf16[16,3072]{1,0:T(8,128)(2,1)S(1)}, u32[]{:S(2)}, u32[]{:S(2)}) collective-permute-start(bf16[16,3072]{1,0:T(8,128)(2,1)S(1)} %collective-permute-done.5.refs_1_), channel_id=1, source_target_pairs={{0,6},{1,7},{2,4},{3,5},{4,2},{5,3},{6,0},{7,1},{8,14},{9,15},{10,... | collective-permute-start | bytes 294920 | tf_op jit(solution)/shard_map/ppermute | solution.py:20
  11.6 6.6 %collective-permute-start.4 = (bf16[16,3072]{1,0:T(8,128)(2,1)S(1)}, bf16[16,3072]{1,0:T(8,128)(2,1)S(1)}, u32[]{:S(2)}, u32[]{:S(2)}) collective-permute-start(bf16[16,3072]{1,0:T(8,128)(2,1)S(1)} %collective-permute-done.2.refs_3_), channel_id=1, source_target_pairs={{0,1},{1,0},{2,3},{3,2},{4,5},{5,4},{6,7},{7,6},{8,9},{9,8},{10,11... | collective-permute-start | bytes 294920 | tf_op jit(solution)/shard_map/ppermute | solution.py:20
  13.3 5.1 %collective-permute-start.3 = (bf16[16,3072]{1,0:T(8,128)(2,1)S(1)}, bf16[16,3072]{1,0:T(8,128)(2,1)S(1)}, u32[]{:S(2)}, u32[]{:S(2)}) collective-permute-start(bf16[16,3072]{1,0:T(8,128)(2,1)S(1)} %collective-permute-done.2.refs_3_), channel_id=1, source_target_pairs={{0,2},{1,3},{2,0},{3,1},{4,6},{5,7},{6,4},{7,5},{8,10},{9,11},{10,... | collective-permute-start | bytes 294920 | tf_op jit(solution)/shard_map/ppermute | solution.py:20
  14.3 5.1 %collective-permute-start.1 = (bf16[16,3072]{1,0:T(8,128)(2,1)S(1)}, bf16[16,3072]{1,0:T(8,128)(2,1)S(1)}, u32[]{:S(2)}, u32[]{:S(2)}) collective-permute-start(bf16[16,3072]{1,0:T(8,128)(2,1)S(1)} %collective-permute-done.refs_2_), channel_id=1, source_target_pairs={{0,1},{1,0},{2,3},{3,2},{4,5},{5,4},{6,7},{7,6},{8,9},{9,8},{10,11... | collective-permute-start | bytes 294920 | tf_op jit(solution)/shard_map/ppermute | solution.py:20

commit v10 on v7

--- a/solution.py
+++ b/solution.py
@@ -212,7 +212,7 @@
 def last(group, count, slots, earlier, weight, hidden, factors, before):
     units, width = weight.shape
     tokens = before[0].shape[1]
-    parts = 4
+    parts = 2
     operands = (*slots, *earlier, weight, hidden, *factors, *before)
     shapes = [(units, width), (units, tokens), (units, tokens)]
     return pl.pallas_call(

time: 21.2 us -> 21.3 us (level)
  no operation moved by 1% of the time
where the time goes in v10:
time: 21.3 us; the launch traced here: 21.1 us
  starting transfers between devices  13.5 us (63%)
  Pallas kernels  5.03 us (24%)
  waiting for transfers between devices  1.98 us (9%)
  between operations  0.68 us (3%)
    ppermute x4, starting transfers between devices, send(): return lax.ppermute(array, ('section', 'tp'), pairs)  8.09 us
    ppermute x4, starting transfers between devices, send(): return lax.ppermute(array, 'tp', [(t, t ^ flip) for t in range(count)])  5.36 us
    pallas_call x1, Pallas kernels, last(): pl.pallas_call(functools.partial(last_kernel, len(slots) + len(earlier),...  1.76 us
    pallas_call x1, Pallas kernels, prepare(): pl.pallas_call(functools.partial(prepare_kernel, groups, count), out_shap...  1.69 us
    ppermute x4, waiting for transfers between devices, send(): return lax.ppermute(array, 'tp', [(t, t ^ flip) for t in range(count)])  1.14 us
    pallas_call x1, Pallas kernels, pack(): pl.pallas_call(pack_kernel, out_shape=pltpu.VMEM((TILE, width * count //...  0.93 us
    ppermute x4, waiting for transfers between devices, send(): return lax.ppermute(array, ('section', 'tp'), pairs)  0.84 us
    pallas_call x1, Pallas kernels, stage(): pl.pallas_call(functools.partial(stage_kernel, group, count, len(before)...  0.65 us
  transfers between devices with their start and end apart: 8, of which 3 were waited for; matrix products, arithmetic and copies ran while one was open for 0% of the time, Pallas kernels for 11%

profile of v10, /device:TPU:0, one launch (start us, length us, event | category | flops | bytes accessed | tf_op | source)
XLA Modules:
  0.0 21.1 jit_solution(10825507581594682532)
XLA Ops:
  0.6 0.9 %shard_map.94 = bf16[16,3072]{1,0:T(8,128)(2,1)S(1)} custom-call(bf16[12,4096]{1,0:T(8,128)(2,1)} %bitcast.19), custom_call_target="tpu_custom_call" | custom-call | tf_op jit(solution)/shard_map/pallas_call | solution.py:52
  1.6 3.4 %collective-permute-start.5 = (bf16[16,3072]{1,0:T(8,128)(2,1)S(1)}, bf16[16,3072]{1,0:T(8,128)(2,1)S(1)}, u32[]{:S(2)}, u32[]{:S(2)}) collective-permute-start(bf16[16,3072]{1,0:T(8,128)(2,1)S(1)} %shard_map.94), channel_id=1, source_target_pairs={{0,25},{1,24},{2,27},{3,26},{4,29},{5,28},{6,31},{7,30},{8,1},{9,0... | collective-permute-start | bytes 294920 | tf_op jit(solution)/shard_map/ppermute | solution.py:26
  5.0 2.9 %collective-permute-start.2 = (bf16[16,3072]{1,0:T(8,128)(2,1)S(1)}, bf16[16,3072]{1,0:T(8,128)(2,1)S(1)}, u32[]{:S(2)}, u32[]{:S(2)}) collective-permute-start(bf16[16,3072]{1,0:T(8,128)(2,1)S(1)} %shard_map.94), channel_id=1, source_target_pairs={{0,28},{1,29},{2,30},{3,31},{4,24},{5,25},{6,26},{7,27},{8,4},{9,5... | collective-permute-start | bytes 294920 | tf_op jit(solution)/shard_map/ppermute | solution.py:26
  7.8 1.0 %collective-permute-start = (bf16[16,3072]{1,0:T(8,128)(2,1)S(1)}, bf16[16,3072]{1,0:T(8,128)(2,1)S(1)}, u32[]{:S(2)}, u32[]{:S(2)}) collective-permute-start(bf16[16,3072]{1,0:T(8,128)(2,1)S(1)} %shard_map.94), channel_id=1, source_target_pairs={{0,26},{1,27},{2,24},{3,25},{4,30},{5,31},{6,28},{7,29},{8,2},{9,3... | collective-permute-start | bytes 294920 | tf_op jit(solution)/shard_map/ppermute | solution.py:26
  8.8 0.8 %collective-permute-start.7 = (bf16[16,3072]{1,0:T(8,128)(2,1)S(1)}, bf16[16,3072]{1,0:T(8,128)(2,1)S(1)}, u32[]{:S(2)}, u32[]{:S(2)}) collective-permute-start(bf16[16,3072]{1,0:T(8,128)(2,1)S(1)} %shard_map.94), channel_id=1, source_target_pairs={{0,24},{1,25},{2,26},{3,27},{4,28},{5,29},{6,30},{7,31},{8,0},{9,1... | collective-permute-start | bytes 294920 | tf_op jit(solution)/shard_map/ppermute | solution.py:26
  9.7 0.0 collective-permute-done.5.refs_1_
  9.7 1.1 %collective-permute-start.6 = (bf16[16,3072]{1,0:T(8,128)(2,1)S(1)}, bf16[16,3072]{1,0:T(8,128)(2,1)S(1)}, u32[]{:S(2)}, u32[]{:S(2)}) collective-permute-start(bf16[16,3072]{1,0:T(8,128)(2,1)S(1)} %collective-permute-done.5.refs_1_), channel_id=1, source_target_pairs={{0,6},{1,7},{2,4},{3,5},{4,2},{5,3},{6,0},{7,1},{8,14},{9,15},{10,... | collective-permute-start | bytes 294920 | tf_op jit(solution)/shard_map/ppermute | solution.py:20
  10.8 0.8 %collective-permute-done.2.refs_3_ = bf16[16,3072]{1,0:T(8,128)(2,1)S(1)} collective-permute-done((bf16[16,3072]{1,0:T(8,128)(2,1)S(1)}, bf16[16,3072]{1,0:T(8,128)(2,1)S(1)}, u32[]{:S(2)}, u32[]{:S(2)}) %collective-permute-start.2) | collective-permute-done | bytes 98336 | tf_op jit(solution)/shard_map/ppermute | solution.py:26
  11.6 1.7 %collective-permute-start.4 = (bf16[16,3072]{1,0:T(8,128)(2,1)S(1)}, bf16[16,3072]{1,0:T(8,128)(2,1)S(1)}, u32[]{:S(2)}, u32[]{:S(2)}) collective-permute-start(bf16[16,3072]{1,0:T(8,128)(2,1)S(1)} %collective-permute-done.2.refs_3_), channel_id=1, source_target_pairs={{0,1},{1,0},{2,3},{3,2},{4,5},{5,4},{6,7},{7,6},{8,9},{9,8},{10,11... | collective-permute-start | bytes 294920 | tf_op jit(solution)/shard_map/ppermute | solution.py:20
  13.3 1.0 %collective-permute-start.3 = (bf16[16,3072]{1,0:T(8,128)(2,1)S(1)}, bf16[16,3072]{1,0:T(8,128)(2,1)S(1)}, u32[]{:S(2)}, u32[]{:S(2)}) collective-permute-start(bf16[16,3072]{1,0:T(8,128)(2,1)S(1)} %collective-permute-done.2.refs_3_), channel_id=1, source_target_pairs={{0,2},{1,3},{2,0},{3,1},{4,6},{5,7},{6,4},{7,5},{8,10},{9,11},{10,... | collective-permute-start | bytes 294920 | tf_op jit(solution)/shard_map/ppermute | solution.py:20
  14.3 0.0 collective-permute-done.refs_2_
  14.3 1.5 %collective-permute-start.1 = (bf16[16,3072]{1,0:T(8,128)(2,1)S(1)}, bf16[16,3072]{1,0:T(8,128)(2,1)S(1)}, u32[]{:S(2)}, u32[]{:S(2)}) collective-permute-start(bf16[16,3072]{1,0:T(8,128)(2,1)S(1)} %collective-permute-done.refs_2_), channel_id=1, source_target_pairs={{0,1},{1,0},{2,3},{3,2},{4,5},{5,4},{6,7},{7,6},{8,9},{9,8},{10,11... | collective-permute-start | bytes 294920 | tf_op jit(solution)/shard_map/ppermute | solution.py:20
  15.9 1.7 %shard_map.95 = (bf16[160,4096]{1,0:T(8,128)(2,1)S(1)}, bf16[160,128]{1,0:T(8,128)(2,1)S(1)}, f32[160,64]{1,0:T(8,128)S(1)}, f32[160,64]{1,0:T(8,128)S(1)}, f32[...) custom-call(bf16[160,96]{1,0:T(8,128)(2,1)} %bitcast.21, s32[5,1,96]{2,1,0:T(1,128)} %bitcast.23, bf16[160,96]{1,0:T(8,128)(2,1)} %bitcast.22, ...), custom_call_target="tpu_custom_call" | custom-call | bytes 16777216 | tf_op jit(solution)/shard_map/pallas_call | solution.py:120
  17.6 0.0 collective-permute-done.7.refs_0_
  17.6 0.6 %shard_map.96 = (bf16[64,4096]{1,0:T(8,128)(2,1)S(1)}, bf16[160,96]{1,0:T(8,128)(2,1)S(1)}, bf16[160,96]{1,0:T(8,128)(2,1)S(1)}) custom-call(bf16[16,3072]{1,0:T(8,128)(2,1)S(1)} %collective-permute-done.7.refs_0_, bf16[16,3072]{1,0:T(8,128)(2,1)S(1)} %collective-permute-done.5.refs_1_, bf16[16,3072]{1,0:T(8,128)(2,1)S(1)} %collective-permute-done.refs_2_, ...), custom_call_target="tpu_custom_call" | custom-call | bytes 16777216 | tf_op jit(solution)/shard_map/pallas_call | solution.py:175
  18.2 0.0 collective-permute-done.6.refs_3_
  18.2 0.0 collective-permute-done.4.refs_2_
  18.2 0.2 collective-permute-done.3.refs_1_
  18.4 1.0 %collective-permute-done.1.refs_0_ = bf16[16,3072]{1,0:T(8,128)(2,1)S(1)} collective-permute-done((bf16[16,3072]{1,0:T(8,128)(2,1)S(1)}, bf16[16,3072]{1,0:T(8,128)(2,1)S(1)}, u32[]{:S(2)}, u32[]{:S(2)}) %collective-permute-start.1) | collective-permute-done | bytes 98336 | tf_op jit(solution)/shard_map/ppermute | solution.py:20
  19.4 1.8 %shard_map.97 = (bf16[160,4096]{1,0:T(8,128)(2,1)}, bf16[160,96]{1,0:T(8,128)(2,1)}, bf16[160,96]{1,0:T(8,128)(2,1)}) custom-call(bf16[16,3072]{1,0:T(8,128)(2,1)S(1)} %collective-permute-done.1.refs_0_, bf16[16,3072]{1,0:T(8,128)(2,1)S(1)} %collective-permute-done.3.refs_1_, bf16[16,3072]{1,0:T(8,128)(2,1)S(1)} %collective-permute-done.4.refs_2_, ...), custom_call_target="tpu_custom_call" | custom-call | bytes 16777216 | tf_op jit(solution)/shard_map/pallas_call | solution.py:218
Async XLA Ops:
  1.6 8.1 %collective-permute-start.5 = (bf16[16,3072]{1,0:T(8,128)(2,1)S(1)}, bf16[16,3072]{1,0:T(8,128)(2,1)S(1)}, u32[]{:S(2)}, u32[]{:S(2)}) collective-permute-start(bf16[16,3072]{1,0:T(8,128)(2,1)S(1)} %shard_map.94), channel_id=1, source_target_pairs={{0,25},{1,24},{2,27},{3,26},{4,29},{5,28},{6,31},{7,30},{8,1},{9,0... | collective-permute-start | bytes 294920 | tf_op jit(solution)/shard_map/ppermute | solution.py:26
  5.0 6.7 %collective-permute-start.2 = (bf16[16,3072]{1,0:T(8,128)(2,1)S(1)}, bf16[16,3072]{1,0:T(8,128)(2,1)S(1)}, u32[]{:S(2)}, u32[]{:S(2)}) collective-permute-start(bf16[16,3072]{1,0:T(8,128)(2,1)S(1)} %shard_map.94), channel_id=1, source_target_pairs={{0,28},{1,29},{2,30},{3,31},{4,24},{5,25},{6,26},{7,27},{8,4},{9,5... | collective-permute-start | bytes 294920 | tf_op jit(solution)/shard_map/ppermute | solution.py:26
  7.8 6.5 %collective-permute-start = (bf16[16,3072]{1,0:T(8,128)(2,1)S(1)}, bf16[16,3072]{1,0:T(8,128)(2,1)S(1)}, u32[]{:S(2)}, u32[]{:S(2)}) collective-permute-start(bf16[16,3072]{1,0:T(8,128)(2,1)S(1)} %shard_map.94), channel_id=1, source_target_pairs={{0,26},{1,27},{2,24},{3,25},{4,30},{5,31},{6,28},{7,29},{8,2},{9,3... | collective-permute-start | bytes 294920 | tf_op jit(solution)/shard_map/ppermute | solution.py:26
  8.8 8.8 %collective-permute-start.7 = (bf16[16,3072]{1,0:T(8,128)(2,1)S(1)}, bf16[16,3072]{1,0:T(8,128)(2,1)S(1)}, u32[]{:S(2)}, u32[]{:S(2)}) collective-permute-start(bf16[16,3072]{1,0:T(8,128)(2,1)S(1)} %shard_map.94), channel_id=1, source_target_pairs={{0,24},{1,25},{2,26},{3,27},{4,28},{5,29},{6,30},{7,31},{8,0},{9,1... | collective-permute-start | bytes 294920 | tf_op jit(solution)/shard_map/ppermute | solution.py:26
  9.7 8.6 %collective-permute-start.6 = (bf16[16,3072]{1,0:T(8,128)(2,1)S(1)}, bf16[16,3072]{1,0:T(8,128)(2,1)S(1)}, u32[]{:S(2)}, u32[]{:S(2)}) collective-permute-start(bf16[16,3072]{1,0:T(8,128)(2,1)S(1)} %collective-permute-done.5.refs_1_), channel_id=1, source_target_pairs={{0,6},{1,7},{2,4},{3,5},{4,2},{5,3},{6,0},{7,1},{8,14},{9,15},{10,... | collective-permute-start | bytes 294920 | tf_op jit(solution)/shard_map/ppermute | solution.py:20
  11.6 6.6 %collective-permute-start.4 = (bf16[16,3072]{1,0:T(8,128)(2,1)S(1)}, bf16[16,3072]{1,0:T(8,128)(2,1)S(1)}, u32[]{:S(2)}, u32[]{:S(2)}) collective-permute-start(bf16[16,3072]{1,0:T(8,128)(2,1)S(1)} %collective-permute-done.2.refs_3_), channel_id=1, source_target_pairs={{0,1},{1,0},{2,3},{3,2},{4,5},{5,4},{6,7},{7,6},{8,9},{9,8},{10,11... | collective-permute-start | bytes 294920 | tf_op jit(solution)/shard_map/ppermute | solution.py:20
  13.3 5.1 %collective-permute-start.3 = (bf16[16,3072]{1,0:T(8,128)(2,1)S(1)}, bf16[16,3072]{1,0:T(8,128)(2,1)S(1)}, u32[]{:S(2)}, u32[]{:S(2)}) collective-permute-start(bf16[16,3072]{1,0:T(8,128)(2,1)S(1)} %collective-permute-done.2.refs_3_), channel_id=1, source_target_pairs={{0,2},{1,3},{2,0},{3,1},{4,6},{5,7},{6,4},{7,5},{8,10},{9,11},{10,... | collective-permute-start | bytes 294920 | tf_op jit(solution)/shard_map/ppermute | solution.py:20
  14.3 5.1 %collective-permute-start.1 = (bf16[16,3072]{1,0:T(8,128)(2,1)S(1)}, bf16[16,3072]{1,0:T(8,128)(2,1)S(1)}, u32[]{:S(2)}, u32[]{:S(2)}) collective-permute-start(bf16[16,3072]{1,0:T(8,128)(2,1)S(1)} %collective-permute-done.refs_2_), channel_id=1, source_target_pairs={{0,1},{1,0},{2,3},{3,2},{4,5},{5,4},{6,7},{7,6},{8,9},{9,8},{10,11... | collective-permute-start | bytes 294920 | tf_op jit(solution)/shard_map/ppermute | solution.py:20
